TPU v7x, 32 devices: a whole 2x2x4 slice. The times are simulated.
32 devices in a mesh: ka: 4 (over x, core), ta: 8 (over z, y).
Axes of the slice: x: 2, y: 2, z: 4, core: 2. Of those that a mesh axis runs over, the one named last changes fastest.
Arguments:
- history: bfloat16 [512, 16, 32768], P('ta', None, 'ka'), may hold values from -6 to 6
- energy: float32 [512, 2, 32768], P('ta', None, 'ka'), may hold values from -0.5 to 0.5
- kernel: float32 [512, 16, 16], P('ta'), may hold values from -0.0625 to 0.0625
- newest: int32 [1], replicated, may hold values from 0 to 511
- current: float32 [16, 32768], P(None, 'ka'), may hold values from -6 to 6
- step_energy: float32 [2, 32768], P(None, 'ka'), may hold values from -3.140625 to 3.140625
Outputs:
- new_slice: float32 [16, 32768], P(None, 'ka')
- new_history: bfloat16 [512, 16, 32768], P('ta', None, 'ka')
Inputs may be any that keep to these rules, and one draw needn't show every extreme that they name: Stored steps form a circular buffer; the slot after the newest holds the oldest step.
All inputs are finite; a program needn't handle non-finite values.
Results may differ from a plain program's by a relative error of at most 0.001.
Values sent between devices are 32-bit elements; how exact they have to be, the bound alone decides.
No kernel may reach another device: no remote copies, remote signals or barrier semaphores. Data moves between devices by JAX's collectives and lax.ppermute only.
A program may use at most 128 MiB of HBM per device.

v0:
```python
import jax
import jax.numpy as jnp
from jax import lax
from jax.sharding import PartitionSpec as P


def entering(part, axis, combine, identity):
    count = lax.axis_size(axis)
    place = lax.axis_index(axis)
    ahead = count - 1 - place
    gathered = lax.all_gather(part, axis)
    state = jnp.zeros_like(part) + jnp.asarray(identity, part.dtype)

    def one(turn, state):
        source = count - 1 - turn
        return combine(state, lax.dynamic_index_in_dim(gathered, source, 0, False))

    return lax.fori_loop(0, ahead, one, state)


def rotate(values, angles):
    leading = angles.shape[:-2]
    columns = angles.shape[-1]
    spread_angles = jnp.broadcast_to(
        angles[..., None, :, None, :], leading + (2, 2, 2, columns)
    ).reshape(leading + (8, columns))
    cosine = jnp.cos(spread_angles)
    sine_part = jnp.sin(spread_angles)
    real_part = values[..., :8, :]
    imag_part = values[..., 8:, :]
    return jnp.concatenate(
        [cosine * real_part + sine_part * imag_part, cosine * imag_part - sine_part * real_part],
        axis=-2,
    )


def add_pair(earlier, later):
    return earlier + later


def on_device(history, energy, kernel, newest, current, step_energy):
    steps_dev = history.shape[0]
    cycle_size = lax.axis_size("ta")
    slot_ids = lax.axis_index("ta") * steps_dev + jnp.arange(steps_dev, dtype=jnp.int32)
    latest = newest[0]
    own_suffix = jnp.cumsum(energy[::-1], axis=0)[::-1]
    own_total = own_suffix[0]
    later_mask = (slot_ids > latest).astype(jnp.float32)
    own_after = jnp.sum(energy * later_mask[:, None, None], axis=0)
    above_sum = entering(own_total, "ta", add_pair, jnp.zeros_like(own_total))
    grand_total, after_latest = lax.psum((own_total, own_after), "ta")
    phases = (
        own_suffix
        + above_sum[None]
        - after_latest[None]
        + later_mask[:, None, None] * grand_total[None]
    )
    rotated = rotate(history.astype(jnp.float32), phases)
    start_slice = rotate(current, step_energy)
    own_pred = jnp.einsum("scd,sdk->ck", kernel, rotated, precision=lax.Precision.HIGHEST)
    memory_pred = lax.psum(own_pred, "ta")
    predicted = start_slice + memory_pred
    intersection = 0.25 * jnp.einsum(
        "ck,sck->sk", predicted, rotated, precision=lax.Precision.HIGHEST
    )
    vertex = 1.0 / (1.0 + intersection * intersection)
    memory_corr = lax.psum(
        jnp.einsum(
            "scd,sdk->ck", kernel, rotated * vertex[:, None, :], precision=lax.Precision.HIGHEST
        ),
        "ta",
    )
    corrected = start_slice + 0.5 * (memory_pred + memory_corr)
    target = (latest + 1) % (steps_dev * cycle_size)
    target_mask = slot_ids == target
    new_history = jnp.where(
        target_mask[:, None, None], corrected.astype(jnp.bfloat16)[None], history
    )
    return (corrected, new_history)


def solution(mesh):
    return jax.shard_map(
        on_device,
        mesh=mesh,
        in_specs=(
            P("ta", None, "ka"),
            P("ta", None, "ka"),
            P("ta", None, None),
            P(),
            P(None, "ka"),
            P(None, "ka"),
        ),
        out_specs=(P(None, "ka"), P("ta", None, "ka")),
        check_vma=False,
    )
```

profile of v0, /device:TPU:0, one launch (start us, length us, event | category | flops | bytes accessed | tf_op | source)
XLA Modules:
  0.0 384.9 jit_solution(15293894276252701847)
XLA Ops:
  7.2 0.0 copy-start
  7.2 0.0 all-reduce.9.cloned.1.call-start
  7.9 4.7 %rev.6 = f32[64,2,8192]{2,1,0:T(2,128)} reverse(f32[64,2,8192]{2,1,0:T(2,128)} %param.9), dimensions={0} | reverse | bytes 8388608 | tf_op jit(solution)/shard_map/rev | solution.py:46
  12.6 5.2 %fusion.10 = f32[2,8192]{1,0:T(2,128)} fusion(f32[64,2,8192]{2,1,0:T(2,128)} %param.9, f32[64]{0:T(128)S(1)} %compare_convert_fusion), kind=kLoop, calls=%fused_computation.18 | loop fusion | flops 2080768 | bytes 4260096 | tf_op jit(solution)/shard_map/reduce_sum | solution.py:49
  17.8 3.1 fusion.21
  20.9 0.0 copy-start.1
  20.9 2.0 copy-done.1
  22.9 0.7 fusion.19
  23.6 0.0 all-reduce.9.cloned.1.call-update
  23.6 0.0 all-reduce.5.cloned.1.call-start
  23.7 33.1 %all_gather.3 = f32[8,2,8192]{2,1,0:T(2,128)S(1)} all-gather(f32[1,2,8192]{2,1,0:T(2,128)S(1)} %get-tuple-element.75), channel_id=1, replica_groups=mesh['ka'=4,'ta'=8] {'ta'}, dimensions={0}, use_global_device_ids=true | all-gather | bytes 589824 | tf_op jit(solution)/shard_map/all_gather | solution.py:11
  56.8 0.7 while.12
  57.5 0.0 copy-start.5
  57.5 0.0 copy-start.2
  57.6 22.1 %copy_convert_fusion = f32[64,16,8192]{2,0,1:T(8,128)} fusion(bf16[64,16,8192]{2,1,0:T(8,128)(2,1)} %param.8), kind=kLoop, calls=%fused_computation.12 | loop fusion | flops 8388608 | bytes 50331648 | tf_op jit(solution)/shard_map/convert_element_type | solution.py:58
  79.6 0.0 copy-done.5
  79.6 0.9 fusion.20
  80.6 0.0 copy-done.2
  80.6 4.4 %copy.18 = f32[64,2,8192]{2,0,1:T(8,128)} copy(f32[64,2,8192]{2,1,0:T(2,128)S(1)} %copy-done.2) | data formatting | bytes 8388608 | tf_op jit(solution)/shard_map/jit(cumsum)/reduce_window_sum | solution.py:46
  85.0 32.7 %rev.7 = f32[64,2,8192]{2,0,1:T(8,128)} reverse(f32[64,2,8192]{2,0,1:T(8,128)} %copy.18), dimensions={0} | reverse | bytes 8388608 | tf_op jit(solution)/shard_map/rev | solution.py:46
  117.8 0.1 broadcast_in_dim.20
  117.8 0.2 cos.15
  118.0 0.1 broadcast_in_dim.21
  118.1 0.2 sin.15
  118.3 0.0 all-reduce.9.cloned.1.call-done
  118.3 16.5 %fusion.12 = (f32[64,2,8192]{2,0,1:T(8,128)S(1)}, f32[64,2,8192]{2,0,1:T(8,128)S(1)}) fusion(f32[64,2,8192]{2,0,1:T(8,128)} %rev.7, f32[2,8192]{1,0:T(2,128)} %get-tuple-element.67, f32[2,8192]{1,0:T(2,128)} %get-tuple-element.68, f32[64]{0:T(128)S(1)} %compare_convert_fusion, f32[2,8192]{1,0:T(2,128)S(1)} %get-tuple-element.58), kind=kLoop, calls=%fused_computation.21 | loop fusion | flops 4194304 | bytes 12779776 | tf_op jit(solution)/shard_map/cos | solution.py:27
  134.8 21.5 %fusion.3 = (f32[64,8,8192]{2,0,1:T(8,128)}, f32[64,8,8192]{2,0,1:T(8,128)}) fusion(f32[64,16,8192]{2,0,1:T(8,128)} %copy_convert_fusion, f32[64,2,8192]{2,0,1:T(8,128)S(1)} %get-tuple-element.74, f32[64,2,8192]{2,0,1:T(8,128)S(1)} %get-tuple-element.73), kind=kLoop, calls=%fused_computation.10 | loop fusion | flops 25165824 | bytes 75497472 | tf_op jit(solution)/shard_map/add | solution.py:32
  156.3 0.0 copy-done
  156.3 0.0 copy-start.4
  156.3 22.0 %fusion.6 = f32[16,8192]{1,0:T(8,128)} fusion(f32[64,8,8192]{2,0,1:T(8,128)} %get-tuple-element.72, f32[64,8,8192]{2,0,1:T(8,128)} %get-tuple-element.71, f32[64,16,16]{0,2,1:T(8,128)S(1)} %copy-done), kind=kOutput, calls=%fused_computation.15 | convolution fusion | flops 1619001344 | bytes 34144256 | tf_op jit(solution)/shard_map/scd,sdk->ck/dot_general | solution.py:60
  178.4 0.0 all-reduce.5.cloned.1.call-update
  178.4 0.0 all-reduce.7.cloned.1.call-start
  178.4 0.0 copy-done.4
  178.4 0.1 multiply_add_fusion.2
  178.5 72.9 %all-reduce.5.cloned.1.call-done = f32[16,8192]{1,0:T(8,128)} async-done(((f32[16,8192]{1,0:T(8,128)}), f32[16,8192]{1,0:T(8,128)}) %all-reduce.5.cloned.1.call-update) | async-done | bytes 524304 | tf_op jit(solution)/shard_map/psum | solution.py:61
  251.5 0.0 slice-start
  251.5 1.2 add_bitcast_fusion
  252.7 0.0 slice-start.1
  252.7 0.0 slice-start.2
  252.7 0.0 slice-start.3
  252.7 15.5 %multiply_reduce_fusion = f32[8192,64]{0,1:T(8,128)S(1)} fusion(f32[64,8,8192]{2,0,1:T(8,128)} %get-tuple-element.72, f32[64,8,8192]{2,0,1:T(8,128)} %get-tuple-element.71, f32[8192,16]{0,1:T(8,128)S(1)} %add_bitcast_fusion), kind=kLoop, calls=%fused_computation.2 | loop fusion | flops 24641536 | bytes 36175872 | tf_op jit(solution)/shard_map/ck,sck->sk/dot_general | solution.py:63
  268.2 0.3 divide_bitcast_fusion
  268.5 0.0 slice-done
  268.5 0.0 slice-done.1
  268.5 0.0 slice-done.2
  268.6 0.0 slice-done.3
  268.6 0.0 copy-start.3
  268.6 21.9 %fusion.7 = f32[16,8192]{1,0:T(8,128)} fusion(f32[64,8,8192]{2,0,1:T(8,128)} %get-tuple-element.72, f32[64,8,8192]{2,0,1:T(8,128)S(1)} %bitcast.39, f32[64,8192]{1,0:T(8,128)S(1)} %divide_bitcast_fusion, f32[64,16,16]{0,2,1:T(8,128)S(1)} %copy-done), kind=kOutput, calls=%fused_computation.16 | convolution fusion | flops 1627389952 | bytes 36241408 | tf_op jit(solution)/shard_map/scd,sdk->ck/dot_general | solution.py:68
  290.4 0.0 all-reduce.7.cloned.1.call-update
  290.5 71.8 %all-reduce.7.cloned.1.call-done = f32[16,8192]{1,0:T(8,128)} async-done(((f32[16,8192]{1,0:T(8,128)}), f32[16,8192]{1,0:T(8,128)}) %all-reduce.7.cloned.1.call-update) | async-done | bytes 524304 | tf_op jit(solution)/shard_map/psum | solution.py:67
  362.2 0.0 copy-done.3
  362.2 1.9 fusion.18
  364.2 14.2 %broadcast_select_fusion = bf16[64,16,8192]{2,1,0:T(8,128)(2,1)} fusion(bf16[64,16,8192]{2,1,0:T(8,128)(2,1)} %param.8, pred[64]{0:T(512)(128)(4,1)S(1)} %fusion.15, bf16[16,8192]{1,0:T(8,128)(2,1)S(1)} %get-tuple-element.69), kind=kLoop, calls=%fused_computation.14 | loop fusion | flops 8388608 | bytes 33816640 | tf_op jit(solution)/shard_map/jit(_where)/select_n | solution.py:76
  (11 shorter events, 0.4 us)
Async XLA Ops:
  7.2 149.2 %copy-start = (f32[64,16,16]{0,2,1:T(8,128)S(1)}, f32[64,16,16]{0,2,1:T(8,128)}, u32[]{:S(2)}) copy-start(f32[64,16,16]{0,2,1:T(8,128)} %param.10) | copy-start | bytes 196612
  7.2 111.1 %all-reduce.9.cloned.1.call-start = ((), (), s32[]{:S(2)}) async-start(), calls=%async_computation.2 | async-start | bytes 262144 | tf_op jit(solution)/shard_map/psum | solution.py:51
  20.9 2.0 copy-start.1
  23.6 227.9 %all-reduce.5.cloned.1.call-start = ((), (), s32[]{:S(2)}) async-start(), calls=%async_computation | async-start | bytes 1048576 | tf_op jit(solution)/shard_map/psum | solution.py:61
  57.5 22.1 %copy-start.5 = (f32[2,8192]{1,0:T(2,128)S(1)}, f32[2,8192]{1,0:T(2,128)}, u32[]{:S(2)}) copy-start(f32[2,8192]{1,0:T(2,128)} %param.13) | copy-start | bytes 196612
  57.5 23.0 %copy-start.2 = (f32[64,2,8192]{2,1,0:T(2,128)S(1)}, f32[64,2,8192]{2,1,0:T(2,128)}, u32[]{:S(2)}) copy-start(f32[64,2,8192]{2,1,0:T(2,128)} %copy-done.1) | copy-start | bytes 12582916
  156.3 22.1 %copy-start.4 = (f32[16,8192]{1,0:T(8,128)S(1)}, f32[16,8192]{1,0:T(8,128)}, u32[]{:S(2)}) copy-start(f32[16,8192]{1,0:T(8,128)} %param.12) | copy-start | bytes 1572868
  178.4 183.9 %all-reduce.7.cloned.1.call-start = ((), (), s32[]{:S(2)}) async-start(), calls=%async_computation.1 | async-start | bytes 1048576 | tf_op jit(solution)/shard_map/psum | solution.py:67
  251.5 17.1 %slice-start = ((s8[16777216]{0:T(1024)(128)(4,1)}), s8[4194304]{0:T(1024)(128)(4,1)S(1)}, s32[]{:S(2)}) async-start(s8[16777216]{0:T(1024)(128)(4,1)} %bitcast.38), calls=%async_computation.3 | async-start | bytes 8388608
  252.7 15.8 %slice-start.1 = ((s8[16777216]{0:T(1024)(128)(4,1)}), s8[4194304]{0:T(1024)(128)(4,1)S(1)}, s32[]{:S(2)}) async-start(s8[16777216]{0:T(1024)(128)(4,1)} %bitcast.38), calls=%async_computation.4 | async-start | bytes 8388608
  252.7 15.8 %slice-start.2 = ((s8[16777216]{0:T(1024)(128)(4,1)}), s8[4194304]{0:T(1024)(128)(4,1)S(1)}, s32[]{:S(2)}) async-start(s8[16777216]{0:T(1024)(128)(4,1)} %bitcast.38), calls=%async_computation.5 | async-start | bytes 8388608
  252.7 15.8 %slice-start.3 = ((s8[16777216]{0:T(1024)(128)(4,1)}), s8[4194304]{0:T(1024)(128)(4,1)S(1)}, s32[]{:S(2)}) async-start(s8[16777216]{0:T(1024)(128)(4,1)} %bitcast.38), calls=%async_computation.6 | async-start | bytes 8388608
  268.6 93.7 %copy-start.3 = (f32[16,8192]{1,0:T(8,128)S(1)}, f32[16,8192]{1,0:T(8,128)}, u32[]{:S(2)}) copy-start(f32[16,8192]{1,0:T(8,128)} %all-reduce.5.cloned.1.call-done) | copy-start | bytes 1572868
Sparse Core Ops, SparseCore 0:
  23.7 72.6 all-reduce.8
  178.5 72.9 all-reduce.4
  290.6 71.6 all-reduce.6
where the time goes:
time: 388 us; the launch traced here: 385 us
  waiting for transfers between devices  145 us (37%)
  other arithmetic  102 us (26%)
  local copies, waits for them, and re-layouts  46.1 us (12%)
  matrix products  43.9 us (11%)
  blocking collectives  33.1 us (9%)
  between operations  14.7 us (4%)
    psum x1, waiting for transfers between devices, on_device(): memory_pred = lax.psum(own_pred, 'ta')  72.9 us
    psum x1, waiting for transfers between devices, on_device(): lax.psum(jnp.einsum('scd,sdk->ck', kernel, rotated * vertex[:, None, :],...  71.8 us
    rev x2, local copies, waits for them, and re-layouts, on_device(): own_suffix = jnp.cumsum(energy[::-1], axis=0)[::-1]  37.4 us
    all_gather x1, blocking collectives, entering(): gathered = lax.all_gather(part, axis)  33.1 us
    convert_element_type x1, other arithmetic, on_device(): rotated = rotate(history.astype(jnp.float32), phases)  22.1 us
    dot_general x1, matrix products, on_device(): jnp.einsum('scd,sdk->ck', kernel, rotated, precision=lax.Precision.HIGHEST)  22 us
    dot_general x1, matrix products, on_device(): jnp.einsum('scd,sdk->ck', kernel, rotated * vertex[:, None, :], precision...  21.9 us
    add x2, other arithmetic, rotate(): cosine * real_part + sine_part * imag_part  21.6 us
  transfers between devices with their start and end apart: 3, of which 2 were waited for; matrix products, arithmetic and copies ran while one was open for 16% of the time, Pallas kernels for 0%

commit v1 on v0

v1 whole, which is shorter than its diff:
```python
import functools

import jax
import jax.numpy as jnp
import numpy as np
from jax import lax
from jax.experimental import pallas as pl
from jax.experimental.pallas import tpu as pltpu
from jax.sharding import PartitionSpec as P

LANES = 128
WIDE = 4 * LANES
CHUNK = 1024
VM = pl.BlockSpec(memory_space=pltpu.VMEM)
SM = pl.BlockSpec(memory_space=pltpu.SMEM)
HB = pl.BlockSpec(memory_space=pl.ANY)
SIN = (1.41420874, -0.235676110, 0.0117467684, -2.59660918e-4)
COS = (1.41421350, -0.707105432, 0.0589211807, -1.95919014e-3, 3.27400865e-5)
BF = jnp.bfloat16
F32 = jnp.float32


def group_of(steps):
    return 16 if steps % 16 == 0 else 8


def half_angle_sincos(half):
    turns = jnp.round(half * (1.0 / np.pi))
    u = half - turns * np.pi
    q = u * u
    z = u * (SIN[0] + q * (SIN[1] + q * (SIN[2] + q * SIN[3])))
    c = COS[0] + q * (COS[1] + q * (COS[2] + q * (COS[3] + q * COS[4])))
    return z * c, 1.0 - z * z


def trig_kernel(tri_ref, energy_ref, cos_ref, sin_ref, held, sems):
    steps, columns = cos_ref.shape[1:]
    chunk = min(CHUNK, columns)
    count = columns // chunk

    def copy(j, a):
        lanes = pl.ds(j * chunk, chunk)
        return pltpu.make_async_copy(
            energy_ref.at[:, a, lanes], held.at[a, :, lanes], sems.at[j, a]
        )

    for j in range(count):
        for a in range(2):
            copy(j, a).start()
    for j in range(count):
        for a in range(2):
            copy(j, a).wait()
        for n in range(chunk // WIDE):
            lanes = slice(j * chunk + n * WIDE, j * chunk + (n + 1) * WIDE)
            for a in range(2):
                e = held[a, :, lanes]
                top = e.astype(BF)
                rest = e - top.astype(F32)
                mid = rest.astype(BF)
                low = (rest - mid.astype(F32)).astype(BF)
                half = jnp.dot(
                    tri_ref[...],
                    jnp.concatenate([top, mid, low], axis=0),
                    preferred_element_type=F32,
                )
                s, c = half_angle_sincos(half)
                cos_ref[a, :, lanes] = c
                sin_ref[a, :, lanes] = s


def trig(energy):
    steps, _, columns = energy.shape
    tri = 0.5 * np.triu(np.ones((steps, steps), np.float32))
    tri = jnp.asarray(np.concatenate([tri] * 3, axis=1), BF)
    size = (2, steps, columns)
    return pl.pallas_call(
        trig_kernel,
        in_specs=[VM, HB],
        out_specs=[VM, VM],
        out_shape=[jax.ShapeDtypeStruct(size, F32)] * 2,
        scratch_shapes=[
            pltpu.VMEM(size, F32),
            pltpu.SemaphoreType.DMA((columns // min(CHUNK, columns), 2)),
        ],
        compiler_params=pltpu.CompilerParams(vmem_limit_bytes=32 << 20),
        cost_estimate=pl.CostEstimate(
            flops=40 * size[0] * size[1] * size[2], bytes_accessed=4 * 3 * size[0] * size[1] * size[2], transcendentals=0
        ),
        name="trig",
    )(tri, energy)


def permutation(group):
    rows = 16 * group
    p = np.zeros((rows, rows), np.float32)
    for tile in range(2):
        for c in range(8):
            for g in range(group // 8):
                for s in range(8):
                    p[((tile * 8 + c) * (group // 8) + g) * 8 + s, ((8 * g + s) * 2 + tile) * 8 + c] = 1
    return jnp.asarray(p, BF)


def kernel_rows(kernel):
    steps = kernel.shape[0]
    group = group_of(steps)
    k = kernel.reshape(steps // group, group // 8, 8, 16, 16).transpose(0, 3, 1, 4, 2)
    k = k.reshape(steps // group, 16, 16 * group)
    top = lax.reduce_precision(k, 8, 7)
    return jnp.concatenate([top, k - top], axis=1).astype(BF)


def mix_kernel(correct, copies, steps, group, sc_ref, perm_ref, k_ref, h_ref, cos_ref, sin_ref, off_ref, *rest):
    rest = list(rest)
    if correct:
        start_ref, pred_ref, out_ref, held, in_sems, wide_ref = rest
    else:
        if copies:
            rest.pop(0)
        out_ref, new_ref, held, in_sems, out_sems = rest
    columns = out_ref.shape[-1]
    chunk = min(CHUNK, columns)
    count = columns // chunk
    tiles = chunk // LANES
    blocks = group // 8
    edge = sc_ref[1]
    base = sc_ref[0] * columns

    def rows_at(j):
        return pl.ds(pl.multiple_of((sc_ref[0] * (columns // LANES) + j * tiles) * 8, 16), tiles * 8)

    def copy_in(j):
        here = pl.ds(pl.multiple_of(j * tiles * 8, 16), tiles * 8)
        return pltpu.make_async_copy(h_ref.at[:, :, rows_at(j)], held.at[:, :, here], in_sems.at[j])

    def copy_out(j):
        here = pl.ds(pl.multiple_of(j * tiles * 8, 16), tiles * 8)
        return pltpu.make_async_copy(held.at[:, :, here], new_ref.at[:, :, rows_at(j)], out_sems.at[j])

    for j in range(count):
        copy_in(j).start()

    def body(j, n):
        first = j * chunk + n * WIDE
        row = pl.multiple_of(j * tiles * 8 + n * 32, 16)
        local = [pl.ds(pl.multiple_of(first + LANES * t, LANES), LANES) for t in range(4)]
        whole = [pl.ds(pl.multiple_of(base + first + LANES * t, LANES), LANES) for t in range(4)]

        def both(ref, *index):
            return lambda t: jnp.concatenate([ref[(*index, whole[t])], ref[(*index, whole[t + 2])]], axis=-1)

        if correct:
            full = 0.25 * (
                start_ref[:, pl.ds(pl.multiple_of(base + first, LANES), WIDE)]
                + pred_ref[:, pl.ds(pl.multiple_of(first, LANES), WIDE)]
            )
            for c in range(16):
                wide_ref[c] = jnp.broadcast_to(full[c : c + 1], (8, WIDE))
        turn = [
            [
                [both(off_ref, part, slice(2 * side + a, 2 * side + a + 1))(t) for a in range(2)]
                for side in range(2)
            ]
            for part in range(2)
            for t in range(2)
        ]
        sums = [jnp.zeros((32, 2 * LANES), F32) for _ in range(2)]
        lows = [jnp.zeros((16, 2 * LANES), F32) for _ in range(2)]
        for i in range(steps // group):
            moved = []
            for part in range(2):
                h = jnp.concatenate(
                    [
                        held[i * group : (i + 1) * group, part, pl.ds(pl.multiple_of(row + 16 * p, 16), 16)].reshape(
                            16 * group, LANES
                        )
                        for p in range(2)
                    ],
                    axis=1,
                )
                moved.append(jnp.dot(perm_ref[...], h, preferred_element_type=F32))
            for t in range(2):
                parts = []
                for g in range(blocks):
                    s0 = i * group + 8 * g
                    after = lax.broadcasted_iota(jnp.int32, (8, 2 * LANES), 0) + s0 > edge
                    angle = []
                    for a in range(2):
                        c = both(cos_ref, a, slice(s0, s0 + 8))(t)
                        s = both(sin_ref, a, slice(s0, s0 + 8))(t)
                        co = jnp.where(after, turn[t][1][a], turn[t][0][a])
                        so = jnp.where(after, turn[2 + t][1][a], turn[2 + t][0][a])
                        angle.append((c * co - s * so, s * co + c * so))
                    real, imag = [], []
                    for e in range(8):
                        c, s = angle[(e >> 1) & 1]
                        at = ((t * 8 + e) * blocks + g) * 8
                        x = moved[0][at : at + 8]
                        y = moved[1][at : at + 8]
                        real.append(c * x + s * y)
                        imag.append(c * y - s * x)
                    turned = real + imag
                    if correct:
                        terms = [
                            turned[c]
                            * jnp.concatenate(
                                [
                                    wide_ref[c, :, t * LANES : (t + 1) * LANES],
                                    wide_ref[c, :, (t + 2) * LANES : (t + 3) * LANES],
                                ],
                                axis=-1,
                            )
                            for c in range(16)
                        ]
                        while len(terms) > 1:
                            terms = [terms[m] + terms[m + 1] for m in range(0, len(terms), 2)]
                        vertex = 1.0 / (1.0 + terms[0] * terms[0])
                        turned = [vertex * x for x in turned]
                    parts += turned
                x = jnp.concatenate(parts, axis=0)
                top = x.astype(BF)
                low = (x - top.astype(F32)).astype(BF)
                sums[t] = sums[t] + jnp.dot(k_ref[i], top, preferred_element_type=F32)
                lows[t] = lows[t] + jnp.dot(k_ref[i, :16], low, preferred_element_type=F32)
        for t in range(2):
            total = (sums[t][:16] + sums[t][16:]) + lows[t]
            out_ref[:, local[t]] = total[:, :LANES]
            out_ref[:, local[t + 2]] = total[:, LANES:]

    @pl.loop(0, count)
    def _(j):
        copy_in(j).wait()
        if not correct:
            copy_out(j).start()
        for n in range(chunk // WIDE):
            body(j, n)

    if not correct:
        for j in range(count):
            copy_out(j).wait()


def mix(side, edge, weights, stored, cosine, sine, off, start=None, pred=None, new=None):
    steps = cosine.shape[1]
    columns = cosine.shape[2] // 2
    group = group_of(steps)
    correct = pred is not None
    copies = new is not None
    chunk = min(CHUNK, columns)
    count = columns // chunk
    args = [jnp.stack([side, edge]).astype(jnp.int32), permutation(group), weights, stored, cosine, sine, off]
    specs = [SM, VM, VM, HB, VM, VM, VM]
    out_shape = [jax.ShapeDtypeStruct((16, columns), F32)]
    out_specs = [VM]
    scratch = [
        pltpu.VMEM((steps, 2, columns // 16, LANES), BF),
        pltpu.SemaphoreType.DMA((count,)),
    ]
    aliases = {}
    if correct:
        args += [start, pred]
        specs += [VM, VM]
        scratch.append(pltpu.VMEM((16, 8, WIDE), F32))
    else:
        if copies:
            aliases = {len(args): 1}
            args.append(new)
            specs.append(HB)
        out_shape.append(jax.ShapeDtypeStruct(stored.shape, stored.dtype))
        out_specs.append(HB)
        scratch.append(pltpu.SemaphoreType.DMA((count,)))
    size = steps * 16 * columns
    return pl.pallas_call(
        functools.partial(mix_kernel, correct, copies, steps, group),
        in_specs=specs,
        out_specs=out_specs,
        out_shape=out_shape,
        scratch_shapes=scratch,
        input_output_aliases=aliases,
        compiler_params=pltpu.CompilerParams(vmem_limit_bytes=36 << 20),
        cost_estimate=pl.CostEstimate(flops=200 * size, bytes_accessed=(2 if correct else 4) * size, transcendentals=0),
        name="correct" if correct else "predict",
    )(*args)


def place_kernel(sc_ref, old_ref, slice_ref, new_ref, held, sem):
    held[...] = slice_ref[...].astype(BF)

    @pl.when(sc_ref[0] == 1)
    def _():
        copy = pltpu.make_async_copy(held, new_ref.at[sc_ref[1]], sem)
        copy.start()
        copy.wait()


def place(own, slot, new, corrected):
    return pl.pallas_call(
        place_kernel,
        in_specs=[SM, HB, VM],
        out_specs=HB,
        out_shape=jax.ShapeDtypeStruct(new.shape, new.dtype),
        scratch_shapes=[pltpu.VMEM(new.shape[1:], BF), pltpu.SemaphoreType.DMA],
        input_output_aliases={1: 0},
        name="place",
    )(jnp.stack([own, slot]).astype(jnp.int32), new, corrected)


def tiled(x):
    lead, columns = x.shape[:-2], x.shape[-1]
    x = x.reshape(*lead, 2, 8, columns // LANES, LANES)
    return jnp.swapaxes(x, -3, -2).reshape(*lead, 2, columns // 16, LANES)


def untiled(x):
    lead, rows = x.shape[:-3], x.shape[-2]
    x = jnp.swapaxes(x.reshape(*lead, 2, rows // 8, 8, LANES), -3, -2)
    return x.reshape(*lead, 16, rows * 16)


def rotate(values, angles):
    columns = angles.shape[-1]
    spread = jnp.broadcast_to(angles[None, :, None, :], (2, 2, 2, columns)).reshape(8, columns)
    c, s = jnp.cos(spread), jnp.sin(spread)
    real, imag = values[:8], values[8:]
    return jnp.concatenate([c * real + s * imag, c * imag - s * real], axis=0)


def on_device(history, energy, kernel, newest, current, step_energy):
    steps, _, columns = history.shape
    count = lax.axis_size("ta")
    place_here = lax.axis_index("ta")
    bits = count.bit_length() - 1
    half = columns // 2
    latest = newest[0]
    owner = lax.div(latest, steps)
    edge = latest - place_here * steps
    side = place_here & 1
    other = 1 - side

    def swap(x, mask):
        return lax.ppermute(x, "ta", [(i, i ^ mask) for i in range(count)])

    masks = [2] + [6 if t == 2 else 1 << t for t in range(2, bits)]
    split = (place_here >> 1 ^ place_here >> 2) & 1

    slots = jnp.arange(steps, dtype=jnp.int32)
    early = jnp.sum(jnp.where((slots <= edge)[:, None, None], energy, 0.0), axis=0)
    late = jnp.sum(jnp.where((slots > edge)[:, None, None], energy, 0.0), axis=0)
    mine = place_here == owner
    value = jnp.where(mine, early, early + late)

    cosine, sine = trig(energy)

    total, ahead = value, jnp.zeros_like(value)
    for t in range(bits):
        mask = 6 if t == 2 else 1 << t
        got = swap(total, mask)
        here, there = place_here >> t, owner >> t
        upper = (here & 1) == 1
        partner = here ^ 1
        counted_low = ~((there == here) & (place_here < owner))
        counted_high = (there == partner) | ((there == here) & (place_here >= owner))
        ahead = ahead + jnp.where(jnp.where(upper, counted_high, counted_low), got, 0.0)
        low_group = jnp.where(upper, partner, here)
        total = jnp.where(there == low_group, jnp.where(upper, got, total), total + got)
    off = jnp.concatenate(
        [jnp.where(mine, -late, ahead), jnp.where(mine, ahead + value, ahead)], axis=0
    )
    off = jnp.stack([jnp.cos(off), jnp.sin(off)])

    weights = kernel_rows(kernel)
    stored = tiled(history)
    start = rotate(current, step_energy)

    def inner_sum(x):
        first = split == 0
        keep = jnp.where(first, x[:8], x[8:])
        send = jnp.where(first, x[8:], x[:8])
        keep = keep + swap(send, masks[0])
        for mask in masks[1:]:
            keep = keep + swap(keep, mask)
        rest = swap(keep, masks[0])
        return jnp.concatenate([jnp.where(first, keep, rest), jnp.where(first, rest, keep)], axis=0)

    part_other, new = mix(other, edge, weights, stored, cosine, sine, off)
    from_partner = swap(part_other, 1)
    part_own, new = mix(side, edge, weights, stored, cosine, sine, off, new=new)
    pred_own = inner_sum(part_own + from_partner)
    pred_other = swap(pred_own, 1)
    (corr_own,) = mix(side, edge, weights, stored, cosine, sine, off, start, pred_own)
    from_partner = swap(corr_own, 1)
    (corr_other,) = mix(other, edge, weights, stored, cosine, sine, off, start, pred_other)
    corr = inner_sum(corr_other + from_partner)
    start_other = jnp.where(side == 0, start[:, half:], start[:, :half])
    new_other = start_other + 0.5 * (pred_other + corr)
    new_own = swap(new_other, 1)
    corrected = jnp.concatenate(
        [jnp.where(side == 0, new_own, new_other), jnp.where(side == 0, new_other, new_own)], axis=1
    )
    target = lax.rem(latest + 1, steps * count)
    own = lax.div(target, steps) == place_here
    new = place(own, lax.rem(target, steps), new, tiled(corrected))
    return corrected, untiled(new)


def solution(mesh):
    return jax.shard_map(
        on_device,
        mesh=mesh,
        in_specs=(
            P("ta", None, "ka"),
            P("ta", None, "ka"),
            P("ta", None, None),
            P(),
            P(None, "ka"),
            P(None, "ka"),
        ),
        out_specs=(P(None, "ka"), P("ta", None, "ka")),
        check_vma=False,
    )
```

time: 388 us -> 138 us (0.36)
  waiting for transfers between devices: 145 us -> 34 us
  other arithmetic: 102 us -> 9.94 us
  Pallas kernels: 0 us -> 58.5 us
  matrix products: 43.9 us -> 0 us
  local copies, waits for them, and re-layouts: 46.1 us -> 10.9 us
  blocking collectives: 33.1 us -> 0 us
  starting transfers between devices: 0.12 us -> 21.9 us
  between operations: 14.7 us -> 1.94 us
    psum x3 -> x0, waiting for transfers between devices: 145 us -> none  [the longest x1 72.9 us: on_device(): memory_pred = lax.psum(own_pred, 'ta')]
    pallas_call x0 -> x6, Pallas kernels: none -> 58.5 us  [the longest x4 49.8 us: mix(): pl.pallas_call(functools.partial(mix_kernel, correct, copies, steps, grou...]
    dot_general x2 -> x0, matrix products: 43.9 us -> none  [the longest x1 22 us: on_device(): jnp.einsum('scd,sdk->ck', kernel, rotated, precision=lax.Precision.HIGHEST)]
    rev x2 -> x0, local copies, waits for them, and re-layouts: 37.4 us -> none  [on_device(): own_suffix = jnp.cumsum(energy[::-1], axis=0)[::-1]]
    ppermute x0 -> x13, waiting for transfers between devices: none -> 34 us  [swap(): return lax.ppermute(x, 'ta', [(i, i ^ mask) for i in range(count)])]
    all_gather x1 -> x0, blocking collectives: 33.1 us -> none  [entering(): gathered = lax.all_gather(part, axis)]
    convert_element_type x3 -> x0, other arithmetic: 24 us -> none  [the longest x1 22.1 us: on_device(): rotated = rotate(history.astype(jnp.float32), phases)]
    ppermute x0 -> x13, starting transfers between devices: none -> 21.9 us  [swap(): return lax.ppermute(x, 'ta', [(i, i ^ mask) for i in range(count)])]
  transfers between devices with their start and end apart: 3 -> 13, of which waited for: 2 -> 9; matrix products, arithmetic and copies ran while one was open for 16% -> 2% of each run, Pallas kernels for 0% -> 33%
where the time goes in v1:
time: 138 us; the launch traced here: 137 us
  Pallas kernels  58.5 us (42%)
  waiting for transfers between devices  34 us (25%)
  starting transfers between devices  21.9 us (16%)
  local copies, waits for them, and re-layouts  10.9 us (8%)
  other arithmetic  9.94 us (7%)
  between operations  1.94 us (1%)
    pallas_call x4, Pallas kernels, mix(): pl.pallas_call(functools.partial(mix_kernel, correct, copies, steps, grou...  49.8 us
    ppermute x13, waiting for transfers between devices, swap(): return lax.ppermute(x, 'ta', [(i, i ^ mask) for i in range(count)])  34 us
    ppermute x13, starting transfers between devices, swap(): return lax.ppermute(x, 'ta', [(i, i ^ mask) for i in range(count)])  21.9 us
    unnamed x25, local copies, waits for them, and re-layouts  9.06 us
    pallas_call x1, Pallas kernels, trig(): pl.pallas_call(trig_kernel, in_specs=[VM, HB], out_specs=[VM, VM], out_sh...  7.64 us
    reduce_sum x1, other arithmetic, on_device(): jnp.sum(jnp.where((slots > edge)[:, None, None], energy, 0.0), axis=0)  5.79 us
  transfers between devices with their start and end apart: 13, of which 9 were waited for; matrix products, arithmetic and copies ran while one was open for 2% of the time, Pallas kernels for 33%

profile of v1, /device:TPU:0, one launch (start us, length us, event | category | flops | bytes accessed | tf_op | source)
XLA Modules:
  0.0 137.2 jit_solution(5920077000160401309)
XLA Ops:
  0.6 0.0 copy-start.8
  0.6 0.0 copy-start.10
  1.4 5.8 %select_reduce_fusion.1 = (f32[2,8192]{1,0:T(2,128)S(1)}, f32[2,8192]{1,0:T(2,128)S(1)}) fusion(f32[64,2,8192]{2,1,0:T(2,128)} %energy_ref.1, pred[64]{0:T(512)(128)(4,1)S(1)} %get-tuple-element.33, pred[64]{0:T(512)(128)(4,1)S(1)} %get-tuple-element.32), kind=kLoop, calls=%fused_computation.1 | loop fusion | flops 4161536 | bytes 4325504 | tf_op jit(solution)/shard_map/reduce_sum | solution.py:348
  7.2 3.0 %collective-permute-start = (f32[2,8192]{1,0:T(2,128)S(1)}, f32[2,8192]{1,0:T(2,128)S(1)}, u32[]{:S(2)}, u32[]{:S(2)}) collective-permute-start(f32[2,8192]{1,0:T(2,128)S(1)} %add_select_fusion.1), channel_id=1, source_target_pairs={{0,1},{1,0},{2,3},{3,2},{4,5},{5,4},{6,7},{7,6},{8,9},{9,8},{10,11... | collective-permute-start | bytes 196616 | tf_op jit(solution)/shard_map/ppermute | solution.py:341
  10.2 0.0 copy-done.10
  10.2 0.3 copy.16
  10.5 0.0 copy-start.7
  10.5 0.2 copy.17
  10.8 0.2 copy.18
  11.0 0.0 copy-done.8
  11.0 0.0 copy-start.6
  11.1 2.2 %copy-done.6 = f32[64,2,8192]{2,1,0:T(2,128)S(1)} copy-done((f32[64,2,8192]{2,1,0:T(2,128)S(1)}, f32[64,2,8192]{2,1,0:T(2,128)}, u32[]{:S(2)}) %copy-start.6) | copy-done | bytes 4194328
  13.2 7.6 %trig.1 = (f32[2,64,8192]{2,1,0:T(8,128)S(1)}, f32[2,64,8192]{2,1,0:T(8,128)S(1)}) custom-call(bf16[64,192]{1,0:T(8,128)(2,1)S(1)} %copy-done.8, f32[64,2,8192]{2,1,0:T(2,128)S(1)} %copy-done.6), custom_call_target="tpu_custom_call" | custom-call | flops 41943040 | bytes 12582912 | tf_op jit(solution)/shard_map/trig/pallas_call | solution.py:76
  20.9 0.0 copy-start
  20.9 0.0 copy-start.3
  20.9 0.0 collective-permute-done
  21.0 1.6 %collective-permute-start.1 = (f32[2,8192]{1,0:T(2,128)S(1)}, f32[2,8192]{1,0:T(2,128)S(1)}, u32[]{:S(2)}, u32[]{:S(2)}) collective-permute-start(f32[2,8192]{1,0:T(2,128)S(1)} %add_select_fusion.3), channel_id=1, source_target_pairs={{0,2},{1,3},{2,0},{3,1},{4,6},{5,7},{6,4},{7,5},{8,10},{9,11},{10,... | collective-permute-start | bytes 196616 | tf_op jit(solution)/shard_map/ppermute | solution.py:341
  22.6 2.7 %collective-permute-done.1 = f32[2,8192]{1,0:T(2,128)S(1)} collective-permute-done((f32[2,8192]{1,0:T(2,128)S(1)}, f32[2,8192]{1,0:T(2,128)S(1)}, u32[]{:S(2)}, u32[]{:S(2)}) %collective-permute-start.1) | collective-permute-done | bytes 65568 | tf_op jit(solution)/shard_map/ppermute | solution.py:341
  25.3 3.7 %collective-permute-start.2 = (f32[2,8192]{1,0:T(2,128)S(1)}, f32[2,8192]{1,0:T(2,128)S(1)}, u32[]{:S(2)}, u32[]{:S(2)}) collective-permute-start(f32[2,8192]{1,0:T(2,128)S(1)} %add_select_fusion.2), channel_id=1, source_target_pairs={{0,6},{1,7},{2,4},{3,5},{4,2},{5,3},{6,0},{7,1},{8,14},{9,15},{10,... | collective-permute-start | bytes 196616 | tf_op jit(solution)/shard_map/ppermute | solution.py:341
  29.0 0.1 pad_add_fusion
  29.1 2.4 %collective-permute-done.2 = f32[2,8192]{1,0:T(2,128)S(1)} collective-permute-done((f32[2,8192]{1,0:T(2,128)S(1)}, f32[2,8192]{1,0:T(2,128)S(1)}, u32[]{:S(2)}, u32[]{:S(2)}) %collective-permute-start.2) | collective-permute-done | bytes 65568 | tf_op jit(solution)/shard_map/ppermute | solution.py:341
  31.5 0.1 select_bitcast_fusion
  31.6 1.0 fusion.6
  32.6 0.1 pad_maximum_fusion.2.off_ref
  32.7 0.0 copy-done.7
  32.7 12.4 %predict.2 = (f32[16,4096]{1,0:T(8,128)S(1)}, bf16[64,2,512,128]{3,2,1,0:T(8,128)(2,1)}) custom-call(s32[2]{0:T(128)S(1)} %get-tuple-element.35.sc_ref, bf16[256,256]{1,0:T(8,128)(2,1)S(1)} %copy-done.7, bf16[4,32,256]{2,1,0:T(8,128)(2,1)S(1)} %pad_maximum_fusion.5.k_ref, bf16[64,2,512,128]{3,2,1,0:T(8,128)(2,1)} %bitcast.35, ...), custom_call_target="tpu_custom_call" | custom-call | flops 838860800 | bytes 16777216 | tf_op jit(solution)/shard_map/predict/pallas_call | solution.py:273
  45.1 0.0 copy-done
  45.1 0.5 collective-permute-start.3
  45.6 2.2 %copy-done.1 = f32[2,64,8192]{2,1,0:T(8,128)S(1)} copy-done((f32[2,64,8192]{2,1,0:T(8,128)S(1)}, f32[2,64,8192]{2,1,0:T(8,128)}, u32[]{:S(2)}) %copy-start.1) | copy-done | bytes 4194328
  47.8 2.2 %copy-done.4 = f32[2,64,8192]{2,1,0:T(8,128)S(1)} copy-done((f32[2,64,8192]{2,1,0:T(8,128)S(1)}, f32[2,64,8192]{2,1,0:T(8,128)}, u32[]{:S(2)}) %copy-start.4) | copy-done | bytes 4194328
  49.9 12.3 %predict.3 = (f32[16,4096]{1,0:T(8,128)S(1)}, bf16[64,2,512,128]{3,2,1,0:T(8,128)(2,1)}) custom-call(s32[2]{0:T(128)S(1)} %get-tuple-element.34.sc_ref, bf16[256,256]{1,0:T(8,128)(2,1)S(1)} %copy-done.7, bf16[4,32,256]{2,1,0:T(8,128)(2,1)S(1)} %pad_maximum_fusion.5.k_ref, bf16[64,2,512,128]{3,2,1,0:T(8,128)(2,1)} %bitcast.36, ...), custom_call_target="tpu_custom_call", output_to_operand_aliasing={{1}: (7, {})} | custom-call | flops 838860800 | bytes 16777216 | tf_op jit(solution)/shard_map/predict/pallas_call | solution.py:273
  62.3 0.0 collective-permute-done.3
  62.4 0.7 collective-permute-start.4
  63.0 0.9 fusion.9
  64.0 0.1 broadcast_in_dim.34
  64.1 0.2 cos.18
  64.3 0.1 broadcast_in_dim.35
  64.3 0.2 sin.18
  64.5 2.9 %collective-permute-done.4 = f32[8,4096]{1,0:T(8,128)S(1)} collective-permute-done((f32[8,4096]{1,0:T(8,128)S(1)}, f32[8,4096]{1,0:T(8,128)S(1)}, u32[]{:S(2)}, u32[]{:S(2)}) %collective-permute-start.4) | collective-permute-done | bytes 131104 | tf_op jit(solution)/shard_map/ppermute | solution.py:341
  67.4 3.8 %collective-permute-start.5 = (f32[8,4096]{1,0:T(8,128)S(1)}, f32[8,4096]{1,0:T(8,128)S(1)}, u32[]{:S(2)}, u32[]{:S(2)}) collective-permute-start(f32[8,4096]{1,0:T(8,128)S(1)} %select_add_fusion.1), channel_id=1, source_target_pairs={{0,6},{1,7},{2,4},{3,5},{4,2},{5,3},{6,0},{7,1},{8,14},{9,15},{10,... | collective-permute-start | bytes 393224 | tf_op jit(solution)/shard_map/ppermute | solution.py:341
  71.2 0.1 multiply_subtract_fusion
  71.3 3.7 %collective-permute-done.5 = f32[8,4096]{1,0:T(8,128)S(1)} collective-permute-done((f32[8,4096]{1,0:T(8,128)S(1)}, f32[8,4096]{1,0:T(8,128)S(1)}, u32[]{:S(2)}, u32[]{:S(2)}) %collective-permute-start.5) | collective-permute-done | bytes 131104 | tf_op jit(solution)/shard_map/ppermute | solution.py:341
  75.0 1.0 collective-permute-start.6
  76.0 4.0 %collective-permute-done.6 = f32[8,4096]{1,0:T(8,128)S(1)} collective-permute-done((f32[8,4096]{1,0:T(8,128)S(1)}, f32[8,4096]{1,0:T(8,128)S(1)}, u32[]{:S(2)}, u32[]{:S(2)}) %collective-permute-start.6) | collective-permute-done | bytes 131104 | tf_op jit(solution)/shard_map/ppermute | solution.py:341
  80.1 1.8 %collective-permute-start.7 = (f32[16,4096]{1,0:T(8,128)S(1)}, f32[16,4096]{1,0:T(8,128)S(1)}, u32[]{:S(2)}, u32[]{:S(2)}) collective-permute-start(f32[16,4096]{1,0:T(8,128)S(1)} %pad_maximum_fusion.3.rest_1_), channel_id=1, source_target_pairs={{0,1},{1,0},{2,3},{3,2},{4,5},{5,4},{6,7},{7,6},{8,9},{9,8},{10,11... | collective-permute-start | bytes 786440 | tf_op jit(solution)/shard_map/ppermute | solution.py:341
  81.9 2.2 %copy-done.5 = f32[2,64,8192]{2,1,0:T(8,128)S(1)} copy-done((f32[2,64,8192]{2,1,0:T(8,128)S(1)}, f32[2,64,8192]{2,1,0:T(8,128)}, u32[]{:S(2)}) %copy-start.5) | copy-done | bytes 4194328
  84.1 12.6 %correct.3 = f32[16,4096]{1,0:T(8,128)S(1)} custom-call(s32[2]{0:T(128)S(1)} %get-tuple-element.34.sc_ref, bf16[256,256]{1,0:T(8,128)(2,1)S(1)} %copy-done.7, bf16[4,32,256]{2,1,0:T(8,128)(2,1)S(1)} %pad_maximum_fusion.5.k_ref, bf16[64,2,512,128]{3,2,1,0:T(8,128)(2,1)} %bitcast.37, f32[2,64,8192]{2,1,0:T(8,128)S(1)} %copy-done.2, ...), custom_call_target="tpu_custom_call" | custom-call | flops 838860800 | bytes 8388608 | tf_op jit(solution)/shard_map/correct/pallas_call | solution.py:273
  96.7 0.3 collective-permute-start.8
  97.0 0.0 collective-permute-done.7.rest_1_
  97.0 12.5 %correct.2 = f32[16,4096]{1,0:T(8,128)S(1)} custom-call(s32[2]{0:T(128)S(1)} %get-tuple-element.35.sc_ref, bf16[256,256]{1,0:T(8,128)(2,1)S(1)} %copy-done.7, bf16[4,32,256]{2,1,0:T(8,128)(2,1)S(1)} %pad_maximum_fusion.5.k_ref, bf16[64,2,512,128]{3,2,1,0:T(8,128)(2,1)} %bitcast.38, f32[2,64,8192]{2,1,0:T(8,128)S(1)} %copy-done.2, ...), custom_call_target="tpu_custom_call" | custom-call | flops 838860800 | bytes 8388608 | tf_op jit(solution)/shard_map/correct/pallas_call | solution.py:273
  109.5 0.0 collective-permute-done.8
  109.6 1.0 collective-permute-start.9
  110.6 5.2 %collective-permute-done.9 = f32[8,4096]{1,0:T(8,128)S(1)} collective-permute-done((f32[8,4096]{1,0:T(8,128)S(1)}, f32[8,4096]{1,0:T(8,128)S(1)}, u32[]{:S(2)}, u32[]{:S(2)}) %collective-permute-start.9) | collective-permute-done | bytes 131104 | tf_op jit(solution)/shard_map/ppermute | solution.py:341
  115.8 2.9 %collective-permute-start.10 = (f32[8,4096]{1,0:T(8,128)S(1)}, f32[8,4096]{1,0:T(8,128)S(1)}, u32[]{:S(2)}, u32[]{:S(2)}) collective-permute-start(f32[8,4096]{1,0:T(8,128)S(1)} %select_add_fusion), channel_id=1, source_target_pairs={{0,6},{1,7},{2,4},{3,5},{4,2},{5,3},{6,0},{7,1},{8,14},{9,15},{10,... | collective-permute-start | bytes 393224 | tf_op jit(solution)/shard_map/ppermute | solution.py:341
  118.7 4.0 %collective-permute-done.10 = f32[8,4096]{1,0:T(8,128)S(1)} collective-permute-done((f32[8,4096]{1,0:T(8,128)S(1)}, f32[8,4096]{1,0:T(8,128)S(1)}, u32[]{:S(2)}, u32[]{:S(2)}) %collective-permute-start.10) | collective-permute-done | bytes 131104 | tf_op jit(solution)/shard_map/ppermute | solution.py:341
  122.7 0.1 collective-permute-start.11
  122.8 4.9 %collective-permute-done.11 = f32[8,4096]{1,0:T(8,128)S(1)} collective-permute-done((f32[8,4096]{1,0:T(8,128)S(1)}, f32[8,4096]{1,0:T(8,128)S(1)}, u32[]{:S(2)}, u32[]{:S(2)}) %collective-permute-start.11) | collective-permute-done | bytes 131104 | tf_op jit(solution)/shard_map/ppermute | solution.py:341
  127.7 0.1 fusion.2
  127.8 1.6 %collective-permute-start.12 = (f32[16,4096]{1,0:T(8,128)S(1)}, f32[16,4096]{1,0:T(8,128)S(1)}, u32[]{:S(2)}, u32[]{:S(2)}) collective-permute-start(f32[16,4096]{1,0:T(8,128)S(1)} %fusion.2), channel_id=1, source_target_pairs={{0,1},{1,0},{2,3},{3,2},{4,5},{5,4},{6,7},{7,6},{8,9},{9,8},{10,11... | collective-permute-start | bytes 786440 | tf_op jit(solution)/shard_map/ppermute | solution.py:341
  129.4 0.6 pad_add_fusion.2.sc_ref
  130.0 4.2 %collective-permute-done.12 = f32[16,4096]{1,0:T(8,128)S(1)} collective-permute-done((f32[16,4096]{1,0:T(8,128)S(1)}, f32[16,4096]{1,0:T(8,128)S(1)}, u32[]{:S(2)}, u32[]{:S(2)}) %collective-permute-start.12) | collective-permute-done | bytes 262176 | tf_op jit(solution)/shard_map/ppermute | solution.py:341
  134.3 0.8 fusion.10.slice_ref
  135.1 0.8 pad_maximum_fusion.1
  135.9 1.1 place.1
  (30 shorter events, 0.5 us)
Async XLA Ops:
  0.6 10.4 %copy-start.8 = (bf16[64,192]{1,0:T(8,128)(2,1)S(1)}, bf16[64,192]{1,0:T(8,128)(2,1)}, u32[]{:S(2)}) copy-start(bf16[64,192]{1,0:T(8,128)(2,1)} %constant.32.clone.tri_ref) | copy-start | bytes 73732
  0.6 9.6 %copy-start.10 = (f32[64,16,16]{0,2,1:T(8,128)S(1)}, f32[64,16,16]{0,2,1:T(8,128)}, u32[]{:S(2)}) copy-start(f32[64,16,16]{0,2,1:T(8,128)} %param.13) | copy-start | bytes 196612
  7.2 13.7 %collective-permute-start = (f32[2,8192]{1,0:T(2,128)S(1)}, f32[2,8192]{1,0:T(2,128)S(1)}, u32[]{:S(2)}, u32[]{:S(2)}) collective-permute-start(f32[2,8192]{1,0:T(2,128)S(1)} %add_select_fusion.1), channel_id=1, source_target_pairs={{0,1},{1,0},{2,3},{3,2},{4,5},{5,4},{6,7},{7,6},{8,9},{9,8},{10,11... | collective-permute-start | bytes 196616 | tf_op jit(solution)/shard_map/ppermute | solution.py:341
  10.5 22.2 %copy-start.7 = (bf16[256,256]{1,0:T(8,128)(2,1)S(1)}, bf16[256,256]{1,0:T(8,128)(2,1)}, u32[]{:S(2)}) copy-start(bf16[256,256]{1,0:T(8,128)(2,1)} %constant.33.clone.perm_ref) | copy-start | bytes 393220
  11.0 2.2 %copy-start.6 = (f32[64,2,8192]{2,1,0:T(2,128)S(1)}, f32[64,2,8192]{2,1,0:T(2,128)}, u32[]{:S(2)}) copy-start(f32[64,2,8192]{2,1,0:T(2,128)} %energy_ref.1) | copy-start | bytes 12582916
  20.9 24.2 %copy-start = (f32[2,64,8192]{2,1,0:T(8,128)}, f32[2,64,8192]{2,1,0:T(8,128)S(1)}, u32[]{:S(2)}) copy-start(f32[2,64,8192]{2,1,0:T(8,128)S(1)} %get-tuple-element.8.cos_ref) | copy-start | bytes 12582916
  20.9 24.2 %copy-start.3 = (f32[2,64,8192]{2,1,0:T(8,128)}, f32[2,64,8192]{2,1,0:T(8,128)S(1)}, u32[]{:S(2)}) copy-start(f32[2,64,8192]{2,1,0:T(8,128)S(1)} %get-tuple-element.9.sin_ref) | copy-start | bytes 12582916
  21.0 4.3 %collective-permute-start.1 = (f32[2,8192]{1,0:T(2,128)S(1)}, f32[2,8192]{1,0:T(2,128)S(1)}, u32[]{:S(2)}, u32[]{:S(2)}) collective-permute-start(f32[2,8192]{1,0:T(2,128)S(1)} %add_select_fusion.3), channel_id=1, source_target_pairs={{0,2},{1,3},{2,0},{3,1},{4,6},{5,7},{6,4},{7,5},{8,10},{9,11},{10,... | collective-permute-start | bytes 196616 | tf_op jit(solution)/shard_map/ppermute | solution.py:341
  25.3 6.1 %collective-permute-start.2 = (f32[2,8192]{1,0:T(2,128)S(1)}, f32[2,8192]{1,0:T(2,128)S(1)}, u32[]{:S(2)}, u32[]{:S(2)}) collective-permute-start(f32[2,8192]{1,0:T(2,128)S(1)} %add_select_fusion.2), channel_id=1, source_target_pairs={{0,6},{1,7},{2,4},{3,5},{4,2},{5,3},{6,0},{7,1},{8,14},{9,15},{10,... | collective-permute-start | bytes 196616 | tf_op jit(solution)/shard_map/ppermute | solution.py:341
  45.1 17.2 %collective-permute-start.3 = (f32[16,4096]{1,0:T(8,128)S(1)}, f32[16,4096]{1,0:T(8,128)S(1)}, u32[]{:S(2)}, u32[]{:S(2)}) collective-permute-start(f32[16,4096]{1,0:T(8,128)S(1)} %get-tuple-element.12), channel_id=1, source_target_pairs={{0,1},{1,0},{2,3},{3,2},{4,5},{5,4},{6,7},{7,6},{8,9},{9,8},{10,11... | collective-permute-start | bytes 786440 | tf_op jit(solution)/shard_map/ppermute | solution.py:341
  45.6 2.2 %copy-start.1 = (f32[2,64,8192]{2,1,0:T(8,128)S(1)}, f32[2,64,8192]{2,1,0:T(8,128)}, u32[]{:S(2)}) copy-start(f32[2,64,8192]{2,1,0:T(8,128)} %copy-done) | copy-start | bytes 12582916
  47.7 2.2 %copy-start.4 = (f32[2,64,8192]{2,1,0:T(8,128)S(1)}, f32[2,64,8192]{2,1,0:T(8,128)}, u32[]{:S(2)}) copy-start(f32[2,64,8192]{2,1,0:T(8,128)} %copy-done.3) | copy-start | bytes 12582916
  49.9 13.1 %copy-start.11 = (f32[2,8192]{1,0:T(2,128)S(1)}, f32[2,8192]{1,0:T(2,128)}, u32[]{:S(2)}) copy-start(f32[2,8192]{1,0:T(2,128)} %param.16) | copy-start | bytes 196612
  49.9 21.3 %copy-start.9 = (f32[16,8192]{1,0:T(8,128)S(1)}, f32[16,8192]{1,0:T(8,128)}, u32[]{:S(2)}) copy-start(f32[16,8192]{1,0:T(8,128)} %param.15) | copy-start | bytes 1572868
  62.4 5.0 %collective-permute-start.4 = (f32[8,4096]{1,0:T(8,128)S(1)}, f32[8,4096]{1,0:T(8,128)S(1)}, u32[]{:S(2)}, u32[]{:S(2)}) collective-permute-start(f32[8,4096]{1,0:T(8,128)S(1)} %slice_select_fusion.1), channel_id=1, source_target_pairs={{0,2},{1,3},{2,0},{3,1},{4,6},{5,7},{6,4},{7,5},{8,10},{9,11},{10,... | collective-permute-start | bytes 393224 | tf_op jit(solution)/shard_map/ppermute | solution.py:341
  64.5 17.4 %copy-start.2 = (f32[2,64,8192]{2,1,0:T(8,128)S(1)}, f32[2,64,8192]{2,1,0:T(8,128)}, u32[]{:S(2)}) copy-start(f32[2,64,8192]{2,1,0:T(8,128)} %copy-done) | copy-start | bytes 12582916
  67.4 7.5 %collective-permute-start.5 = (f32[8,4096]{1,0:T(8,128)S(1)}, f32[8,4096]{1,0:T(8,128)S(1)}, u32[]{:S(2)}, u32[]{:S(2)}) collective-permute-start(f32[8,4096]{1,0:T(8,128)S(1)} %select_add_fusion.1), channel_id=1, source_target_pairs={{0,6},{1,7},{2,4},{3,5},{4,2},{5,3},{6,0},{7,1},{8,14},{9,15},{10,... | collective-permute-start | bytes 393224 | tf_op jit(solution)/shard_map/ppermute | solution.py:341
  75.0 5.0 %collective-permute-start.6 = (f32[8,4096]{1,0:T(8,128)S(1)}, f32[8,4096]{1,0:T(8,128)S(1)}, u32[]{:S(2)}, u32[]{:S(2)}) collective-permute-start(f32[8,4096]{1,0:T(8,128)S(1)} %add.57), channel_id=1, source_target_pairs={{0,2},{1,3},{2,0},{3,1},{4,6},{5,7},{6,4},{7,5},{8,10},{9,11},{10,... | collective-permute-start | bytes 393224 | tf_op jit(solution)/shard_map/ppermute | solution.py:341
  80.1 16.9 %collective-permute-start.7 = (f32[16,4096]{1,0:T(8,128)S(1)}, f32[16,4096]{1,0:T(8,128)S(1)}, u32[]{:S(2)}, u32[]{:S(2)}) collective-permute-start(f32[16,4096]{1,0:T(8,128)S(1)} %pad_maximum_fusion.3.rest_1_), channel_id=1, source_target_pairs={{0,1},{1,0},{2,3},{3,2},{4,5},{5,4},{6,7},{7,6},{8,9},{9,8},{10,11... | collective-permute-start | bytes 786440 | tf_op jit(solution)/shard_map/ppermute | solution.py:341
  81.9 2.2 %copy-start.5 = (f32[2,64,8192]{2,1,0:T(8,128)S(1)}, f32[2,64,8192]{2,1,0:T(8,128)}, u32[]{:S(2)}) copy-start(f32[2,64,8192]{2,1,0:T(8,128)} %copy-done.3) | copy-start | bytes 12582916
  96.7 12.9 %collective-permute-start.8 = (f32[16,4096]{1,0:T(8,128)S(1)}, f32[16,4096]{1,0:T(8,128)S(1)}, u32[]{:S(2)}, u32[]{:S(2)}) collective-permute-start(f32[16,4096]{1,0:T(8,128)S(1)} %correct.3), channel_id=1, source_target_pairs={{0,1},{1,0},{2,3},{3,2},{4,5},{5,4},{6,7},{7,6},{8,9},{9,8},{10,11... | collective-permute-start | bytes 786440 | tf_op jit(solution)/shard_map/ppermute | solution.py:341
  109.6 6.2 %collective-permute-start.9 = (f32[8,4096]{1,0:T(8,128)S(1)}, f32[8,4096]{1,0:T(8,128)S(1)}, u32[]{:S(2)}, u32[]{:S(2)}) collective-permute-start(f32[8,4096]{1,0:T(8,128)S(1)} %slice_select_fusion), channel_id=1, source_target_pairs={{0,2},{1,3},{2,0},{3,1},{4,6},{5,7},{6,4},{7,5},{8,10},{9,11},{10,... | collective-permute-start | bytes 393224 | tf_op jit(solution)/shard_map/ppermute | solution.py:341
  115.8 6.8 %collective-permute-start.10 = (f32[8,4096]{1,0:T(8,128)S(1)}, f32[8,4096]{1,0:T(8,128)S(1)}, u32[]{:S(2)}, u32[]{:S(2)}) collective-permute-start(f32[8,4096]{1,0:T(8,128)S(1)} %select_add_fusion), channel_id=1, source_target_pairs={{0,6},{1,7},{2,4},{3,5},{4,2},{5,3},{6,0},{7,1},{8,14},{9,15},{10,... | collective-permute-start | bytes 393224 | tf_op jit(solution)/shard_map/ppermute | solution.py:341
  122.7 5.0 %collective-permute-start.11 = (f32[8,4096]{1,0:T(8,128)S(1)}, f32[8,4096]{1,0:T(8,128)S(1)}, u32[]{:S(2)}, u32[]{:S(2)}) collective-permute-start(f32[8,4096]{1,0:T(8,128)S(1)} %add.60), channel_id=1, source_target_pairs={{0,2},{1,3},{2,0},{3,1},{4,6},{5,7},{6,4},{7,5},{8,10},{9,11},{10,... | collective-permute-start | bytes 393224 | tf_op jit(solution)/shard_map/ppermute | solution.py:341
  127.8 6.4 %collective-permute-start.12 = (f32[16,4096]{1,0:T(8,128)S(1)}, f32[16,4096]{1,0:T(8,128)S(1)}, u32[]{:S(2)}, u32[]{:S(2)}) collective-permute-start(f32[16,4096]{1,0:T(8,128)S(1)} %fusion.2), channel_id=1, source_target_pairs={{0,1},{1,0},{2,3},{3,2},{4,5},{5,4},{6,7},{7,6},{8,9},{9,8},{10,11... | collective-permute-start | bytes 786440 | tf_op jit(solution)/shard_map/ppermute | solution.py:341

commit v2 on v0

v2 whole, which is shorter than its diff:
```python
import functools

import jax
import jax.numpy as jnp
import numpy as np
from jax import lax
from jax.experimental import pallas as pl
from jax.experimental.pallas import tpu as pltpu
from jax.sharding import PartitionSpec as P

LANES = 128
WIDE = 4 * LANES
CHUNK = 1024
VM = pl.BlockSpec(memory_space=pltpu.VMEM)
SM = pl.BlockSpec(memory_space=pltpu.SMEM)
HB = pl.BlockSpec(memory_space=pltpu.HBM)
SIN = (1.41420874, -0.235676110, 0.0117467684, -2.59660918e-4)
COS = (1.41421350, -0.707105432, 0.0589211807, -1.95919014e-3, 3.27400865e-5)
BF = jnp.bfloat16
F32 = jnp.float32
SELF = [slice(t * LANES, (t + 1) * LANES) for t in range(4)]


GROUP = 8


def double_sincos(u):
    q = u * u
    z = u * (SIN[0] + q * (SIN[1] + q * (SIN[2] + q * SIN[3])))
    c = COS[0] + q * (COS[1] + q * (COS[2] + q * (COS[3] + q * COS[4])))
    return z * c, 1.0 - z * z


def half_angle_sincos(half):
    return double_sincos(half - jnp.round(half * (1.0 / np.pi)) * np.pi)


def sincos(angle):
    half = 0.5 * angle
    turns = jnp.round(half * (1.0 / np.pi))
    return double_sincos((half - turns * 3.140625) - turns * 9.67653589793e-4)


def pieces_of(steps):
    return 4 if steps % 4 == 0 else 1


def totals_kernel(edge_ref, energy_ref, value_ref, late_ref, held, sems):
    steps = energy_ref.shape[0]
    pieces = pieces_of(steps)
    each = steps // pieces
    edge = edge_ref[0]

    def copy(p):
        part = pl.ds(p * each, each)
        return pltpu.make_async_copy(energy_ref.at[part], held.at[part], sems.at[p])

    for p in range(pieces):
        copy(p).start()
    total = jnp.zeros(value_ref.shape, F32)
    late = jnp.zeros(value_ref.shape, F32)
    for p in range(pieces):
        copy(p).wait()
        for s in range(p * each, (p + 1) * each):
            e = held[s]
            total = total + e
            late = late + e * (s > edge).astype(F32)
    mine = (edge >= 0) & (edge < steps)
    value_ref[...] = jnp.where(mine, total - late, total)
    late_ref[...] = late


def totals(edge, energy):
    steps, _, columns = energy.shape
    rows = columns // (LANES // 2)
    view = energy.reshape(steps, 2, columns // LANES, LANES).transpose(0, 2, 1, 3).reshape(steps, rows, LANES)
    return pl.pallas_call(
        totals_kernel,
        in_specs=[SM, HB],
        out_specs=[VM, VM],
        out_shape=[jax.ShapeDtypeStruct((rows, LANES), F32)] * 2,
        scratch_shapes=[pltpu.VMEM(view.shape, F32), pltpu.SemaphoreType.DMA((pieces_of(steps),))],
        compiler_params=pltpu.CompilerParams(vmem_limit_bytes=54 << 20),
        cost_estimate=pl.CostEstimate(flops=4 * energy.size, bytes_accessed=4 * energy.size, transcendentals=0),
        name="totals",
    )(jnp.reshape(edge, (1,)).astype(jnp.int32), view)


def trig_kernel(tri_ref, energy_ref, waves_ref, held, made, in_sems, out_sems):
    columns = held.shape[-1]
    chunk = min(CHUNK, columns)
    count = columns // chunk

    def copy_in(j, a):
        lanes = pl.ds(j * chunk, chunk)
        return pltpu.make_async_copy(energy_ref.at[:, a, lanes], held.at[a, :, lanes], in_sems.at[j, a])

    def copy_out(j):
        lanes = pl.ds(j * chunk, chunk)
        return pltpu.make_async_copy(made.at[:, :, :, lanes], waves_ref.at[:, :, :, lanes], out_sems.at[j])

    for j in range(count):
        for a in range(2):
            copy_in(j, a).start()
    for j in range(count):
        for a in range(2):
            copy_in(j, a).wait()
        for n in range(chunk // WIDE):
            lanes = slice(j * chunk + n * WIDE, j * chunk + (n + 1) * WIDE)
            for a in range(2):
                e = held[a, :, lanes]
                top = e.astype(BF)
                rest = e - top.astype(F32)
                mid = rest.astype(BF)
                low = (rest - mid.astype(F32)).astype(BF)
                half = jnp.dot(
                    tri_ref[...],
                    jnp.concatenate([top, mid, low], axis=0),
                    preferred_element_type=F32,
                )
                s, c = half_angle_sincos(half)
                made[0, a, :, lanes] = c
                made[1, a, :, lanes] = s
        copy_out(j).start()
    for j in range(count):
        copy_out(j).wait()


def trig(energy):
    steps, _, columns = energy.shape
    tri = 0.5 * np.triu(np.ones((steps, steps), np.float32))
    tri = jnp.asarray(np.concatenate([tri] * 3, axis=1), BF)
    count = columns // min(CHUNK, columns)
    size = (2, 2, steps, columns)
    return pl.pallas_call(
        trig_kernel,
        in_specs=[VM, HB],
        out_specs=HB,
        out_shape=jax.ShapeDtypeStruct(size, F32),
        scratch_shapes=[
            pltpu.VMEM(size[1:], F32),
            pltpu.VMEM(size, F32),
            pltpu.SemaphoreType.DMA((count, 2)),
            pltpu.SemaphoreType.DMA((count,)),
        ],
        compiler_params=pltpu.CompilerParams(vmem_limit_bytes=54 << 20),
        cost_estimate=pl.CostEstimate(flops=40 * energy.size, bytes_accessed=12 * energy.size, transcendentals=0),
        name="trig",
    )(tri, energy)


def permutation(group):
    rows = 16 * group
    p = np.zeros((rows, rows), np.float32)
    for tile in range(2):
        for c in range(8):
            for g in range(group // 8):
                for s in range(8):
                    p[((tile * 8 + c) * (group // 8) + g) * 8 + s, ((8 * g + s) * 2 + tile) * 8 + c] = 1
    return jnp.asarray(p, BF)


def kernel_rows(kernel):
    steps = kernel.shape[0]
    group = GROUP
    k = kernel.reshape(steps // group, group // 8, 8, 16, 16).transpose(0, 3, 1, 4, 2)
    k = k.reshape(steps // group, 16, 16 * group)
    top = lax.reduce_precision(k, 8, 7)
    return jnp.concatenate([top, k - top], axis=1).astype(BF)


def predict_kernel(steps, group, sc_ref, perm_ref, k_ref, h_ref, waves_ref, off_ref, out_ref, turned_ref, held, in_sems, waves, wave_sems, kept, out_sems):
    columns = out_ref.shape[-1]
    chunk = kept.shape[-1]
    count = columns // chunk
    tiles = chunk // LANES
    blocks = group // 8
    edge = sc_ref[1]
    base = sc_ref[0] * columns

    def copy_in(j):
        there = pl.ds(pl.multiple_of((sc_ref[0] * (columns // LANES) + j * tiles) * 8, 16), tiles * 8)
        here = pl.ds(pl.multiple_of(j * tiles * 8, 16), tiles * 8)
        return pltpu.make_async_copy(h_ref.at[:, :, there], held.at[:, :, here], in_sems.at[j])

    def copy_out(j):
        there = pl.ds(pl.multiple_of(j * chunk, chunk), chunk)
        return pltpu.make_async_copy(kept.at[j % 2], turned_ref.at[:, there], out_sems.at[j % 2])

    def copy_waves(j):
        there = pl.ds(pl.multiple_of(base + j * chunk, chunk), chunk)
        here = pl.ds(pl.multiple_of(j * chunk, chunk), chunk)
        return pltpu.make_async_copy(waves_ref.at[:, :, :, there], waves.at[:, :, :, here], wave_sems.at[j])

    for j in range(count):
        copy_in(j).start()
        copy_waves(j).start()

    def spans(j, n):
        first = j * chunk + n * WIDE
        local = [pl.ds(pl.multiple_of(first + LANES * t, LANES), LANES) for t in range(4)]
        return local

    def pair(part, a, s0, local, t):
        rows = slice(s0, s0 + 8)
        return jnp.concatenate([waves[part, a, rows, local[t]], waves[part, a, rows, local[t + 2]]], axis=-1)

    def off_row(part, later_side, j, n, t, a):
        row = 2 * ((sc_ref[0] * (columns // LANES)) + j * tiles + 4 * n + t) + a
        return jnp.concatenate(
            [off_ref[part, later_side, pl.ds(row, 1)], off_ref[part, later_side, pl.ds(row + 4, 1)]], axis=-1
        )

    def move(j, n, i):
        row = pl.multiple_of(j * tiles * 8 + n * 32, 16)
        moved = []
        for part in range(2):
            h = [
                held[i * group : (i + 1) * group, part, pl.ds(pl.multiple_of(row + 16 * p, 16), 16)].reshape(
                    16 * group, LANES
                )
                for p in range(2)
            ]
            moved.append(jnp.dot(perm_ref[...], jnp.concatenate(h, axis=1), preferred_element_type=F32))
        return moved

    def turned_rows(local, i, t, g, moved, turn):
        s0 = i * group + 8 * g
        after = lax.broadcasted_iota(jnp.int32, (8, 2 * LANES), 0) + s0 > edge
        angle = []
        for a in range(2):
            c = pair(0, a, s0, local, t)
            s = pair(1, a, s0, local, t)
            co = jnp.where(after, turn[t][1][a], turn[t][0][a])
            so = jnp.where(after, turn[2 + t][1][a], turn[2 + t][0][a])
            angle.append((c * co - s * so, s * co + c * so))
        real, imag = [], []
        for e in range(8):
            c, s = angle[(e >> 1) & 1]
            at = ((t * 8 + e) * blocks + g) * 8
            x = moved[0][at : at + 8]
            y = moved[1][at : at + 8]
            real.append(c * x + s * y)
            imag.append(c * y - s * x)
        return real + imag

    def work(j):
        items = [(n, i) for n in range(chunk // WIDE) for i in range(steps // group)]
        sums = {}
        buf = j % 2

        def contract(n, i, ready):
            for t in range(2):
                top, low = ready[t]
                first = jnp.dot(k_ref[i], top, preferred_element_type=F32)
                second = jnp.dot(k_ref[i, :16], low, preferred_element_type=F32)
                if i > 0:
                    first, second = sums[n, t][0] + first, sums[n, t][1] + second
                sums[n, t] = first, second
                if i == steps // group - 1:
                    total = (first[:16] + first[16:]) + second
                    local = spans(j, n)
                    out_ref[:, local[t]] = total[:, :LANES]
                    out_ref[:, local[t + 2]] = total[:, LANES:]

        moved = move(j, *items[0])
        waiting = None
        for at, (n, i) in enumerate(items):
            if waiting is not None:
                contract(*waiting)
            later = move(j, *items[at + 1]) if at + 1 < len(items) else None
            local = spans(j, n)
            if i == 0:
                turn = [
                    [[off_row(part, later_side, j, n, t, a) for a in range(2)] for later_side in range(2)]
                    for part in range(2)
                    for t in range(2)
                ]
            ready = []
            rows = slice(i * 16 * group, (i + 1) * 16 * group)
            for t in range(2):
                x = jnp.concatenate(
                    [row for g in range(blocks) for row in turned_rows(local, i, t, g, moved, turn)], axis=0
                )
                kept[buf, rows, n * WIDE + t * LANES : n * WIDE + (t + 1) * LANES] = x[:, :LANES]
                kept[buf, rows, n * WIDE + (t + 2) * LANES : n * WIDE + (t + 3) * LANES] = x[:, LANES:]
                top = x.astype(BF)
                ready.append((top, (x - top.astype(F32)).astype(BF)))
            waiting = (n, i, ready)
            moved = later
        contract(*waiting)

    @pl.loop(0, count)
    def _(j):
        copy_in(j).wait()
        copy_waves(j).wait()

        @pl.when(j >= 2)
        def _():
            copy_out(j).wait()

        work(j)
        copy_out(j).start()

    for j in range(max(count - 2, 0), count):
        copy_out(j).wait()


def predict(side, edge, weights, stored, waves, off):
    steps = waves.shape[2]
    columns = waves.shape[3] // 2
    group = GROUP
    chunk = min(CHUNK, columns)
    count = columns // chunk
    size = steps * 16 * columns
    return pl.pallas_call(
        functools.partial(predict_kernel, steps, group),
        in_specs=[SM, VM, VM, HB, HB, VM],
        out_specs=[VM, HB],
        out_shape=[
            jax.ShapeDtypeStruct((16, columns), F32),
            jax.ShapeDtypeStruct((steps * 16, columns), F32),
        ],
        scratch_shapes=[
            pltpu.VMEM((steps, 2, columns // 16, LANES), BF),
            pltpu.SemaphoreType.DMA((count,)),
            pltpu.VMEM((2, 2, steps, columns), F32),
            pltpu.SemaphoreType.DMA((count,)),
            pltpu.VMEM((2, steps * 16, chunk), F32),
            pltpu.SemaphoreType.DMA((2,)),
        ],
        compiler_params=pltpu.CompilerParams(vmem_limit_bytes=50 << 20),
        cost_estimate=pl.CostEstimate(flops=200 * size, bytes_accessed=6 * size, transcendentals=0),
        name="predict",
    )(jnp.stack([side, edge]).astype(jnp.int32), permutation(group), weights, stored, waves, off)


def correct_kernel(steps, group, sc_ref, k_ref, turned_ref, start_ref, pred_ref, out_ref, held, sems, wide_ref):
    columns = out_ref.shape[-1]
    chunk = min(CHUNK, columns)
    count = columns // chunk
    width = 2 * LANES
    rows = 16 * group
    base = sc_ref[0] * columns

    def copy_in(j):
        lanes = pl.ds(pl.multiple_of(j * chunk, chunk), chunk)
        return pltpu.make_async_copy(turned_ref.at[:, lanes], held.at[:, lanes], sems.at[j])

    for j in range(count):
        copy_in(j).start()

    def work(j):
        items = [(n, i) for n in range(chunk // width) for i in range(steps // group)]
        sums = {}

        def span(n):
            return pl.ds(pl.multiple_of(j * chunk + n * width, width), width)

        def contract(n, i, top, low):
            first = jnp.dot(k_ref[i], top, preferred_element_type=F32)
            second = jnp.dot(k_ref[i, :16], low, preferred_element_type=F32)
            if i > 0:
                first, second = sums[n][0] + first, sums[n][1] + second
            sums[n] = first, second
            if i == steps // group - 1:
                out_ref[:, span(n)] = (first[:16] + first[16:]) + second

        waiting = None
        for n, i in items:
            if waiting is not None:
                contract(*waiting)
            if i == 0:
                full = start_ref[:, pl.ds(pl.multiple_of(base + j * chunk + n * width, width), width)] + pred_ref[:, span(n)]
                full = 0.25 * full
                for c in range(16):
                    wide_ref[n, c] = jnp.broadcast_to(full[c : c + 1], (8, width))
            parts = []
            for g in range(group // 8):
                at = i * rows + 128 * g
                turned = [held[at + 8 * c : at + 8 * c + 8, span(n)] for c in range(16)]
                terms = [turned[c] * wide_ref[n, c] for c in range(16)]
                while len(terms) > 1:
                    terms = [terms[m] + terms[m + 1] for m in range(0, len(terms), 2)]
                vertex = 1.0 / (1.0 + terms[0] * terms[0])
                parts += [vertex * x for x in turned]
            x = jnp.concatenate(parts, axis=0)
            top = x.astype(BF)
            waiting = (n, i, top, (x - top.astype(F32)).astype(BF))
        contract(*waiting)

    @pl.loop(0, count)
    def _(j):
        copy_in(j).wait()
        work(j)


def correct(side, weights, turned, start, pred):
    columns = pred.shape[1]
    steps = turned.shape[0] // 16
    group = GROUP
    chunk = min(CHUNK, columns)
    size = steps * 16 * columns
    return pl.pallas_call(
        functools.partial(correct_kernel, steps, group),
        in_specs=[SM, VM, HB, VM, VM],
        out_specs=VM,
        out_shape=jax.ShapeDtypeStruct((16, columns), F32),
        scratch_shapes=[
            pltpu.VMEM(turned.shape, F32),
            pltpu.SemaphoreType.DMA((columns // chunk,)),
            pltpu.VMEM((chunk // (2 * LANES), 16, 8, 2 * LANES), F32),
        ],
        compiler_params=pltpu.CompilerParams(vmem_limit_bytes=46 << 20),
        cost_estimate=pl.CostEstimate(flops=120 * size, bytes_accessed=4 * size, transcendentals=0),
        name="correct",
    )(jnp.reshape(side, (1,)).astype(jnp.int32), weights, turned, start, pred)


def carry_kernel(piece, stored_ref, *rest):
    new_ref, held, in_sems, out_sems = rest[-4:]
    steps = stored_ref.shape[0]
    each = held.shape[0]
    count = in_sems.shape[0]
    part = each // count

    def ends(p):
        here = held.at[pl.ds(p * part, part)]
        there = pl.ds(piece * each + p * part, part)
        read = pltpu.make_async_copy(stored_ref.at[there], here, in_sems.at[p])
        write = pltpu.make_async_copy(here, new_ref.at[there], out_sems.at[p])
        return read, write

    both = [ends(p) for p in range(count)]
    for read, _ in both:
        read.start()
    for read, write in both:
        read.wait()
        write.start()
    for _, write in both:
        write.wait()


def carry(piece, stored, new=None):
    steps = stored.shape[0]
    each = steps // pieces_of(steps)
    count = 4 if each % 4 == 0 else 1
    args = [stored] if new is None else [stored, new]
    size = 4 * stored.size // pieces_of(steps)
    return pl.pallas_call(
        functools.partial(carry_kernel, piece),
        in_specs=[HB] * len(args),
        out_specs=HB,
        out_shape=jax.ShapeDtypeStruct(stored.shape, stored.dtype),
        scratch_shapes=[
            pltpu.VMEM((each, *stored.shape[1:]), BF),
            pltpu.SemaphoreType.DMA((count,)),
            pltpu.SemaphoreType.DMA((count,)),
        ],
        input_output_aliases={} if new is None else {1: 0},
        compiler_params=pltpu.CompilerParams(vmem_limit_bytes=46 << 20),
        cost_estimate=pl.CostEstimate(flops=0, bytes_accessed=size, transcendentals=0),
        name="carry",
    )(*args)


def finish_kernel(sc_ref, old_ref, own_ref, other_ref, whole_ref, new_ref, held, sem):
    half = own_ref.shape[1]
    side = sc_ref[0]
    for at, ref in ((side, own_ref), (1 - side, other_ref)):
        whole_ref[:, pl.ds(pl.multiple_of(at * half, LANES), half)] = ref[...]

    @pl.when(sc_ref[1] == 1)
    def _():
        for at, ref in ((side, own_ref), (1 - side, other_ref)):
            for part in range(2):
                for n in range(half // (2 * LANES)):
                    tiles = [
                        ref[8 * part : 8 * part + 8, (2 * n + t) * LANES : (2 * n + t + 1) * LANES] for t in range(2)
                    ]
                    rows = pl.ds(pl.multiple_of(at * (half // 16) + 16 * n, 16), 16)
                    held[part, rows] = jnp.concatenate(tiles, axis=0).astype(BF)
        copy = pltpu.make_async_copy(held, new_ref.at[sc_ref[2]], sem)
        copy.start()
        copy.wait()


def finish(side, own, slot, new, new_own, new_other):
    rows, half = new_own.shape
    return pl.pallas_call(
        finish_kernel,
        in_specs=[SM, HB, VM, VM],
        out_specs=[VM, HB],
        out_shape=[jax.ShapeDtypeStruct((rows, 2 * half), F32), jax.ShapeDtypeStruct(new.shape, new.dtype)],
        scratch_shapes=[pltpu.VMEM(new.shape[1:], BF), pltpu.SemaphoreType.DMA],
        input_output_aliases={1: 1},
        compiler_params=pltpu.CompilerParams(vmem_limit_bytes=40 << 20),
        name="finish",
    )(jnp.stack([side, own, slot]).astype(jnp.int32), new, new_own, new_other)


def tiled(x):
    lead, columns = x.shape[:-2], x.shape[-1]
    x = x.reshape(*lead, 2, 8, columns // LANES, LANES)
    return jnp.swapaxes(x, -3, -2).reshape(*lead, 2, columns // 16, LANES)


def untiled(x):
    lead, rows = x.shape[:-3], x.shape[-2]
    x = jnp.swapaxes(x.reshape(*lead, 2, rows // 8, 8, LANES), -3, -2)
    return x.reshape(*lead, 16, rows * 16)


def rotate(values, angles):
    columns = angles.shape[-1]
    spread = jnp.broadcast_to(angles[None, :, None, :], (2, 2, 2, columns)).reshape(8, columns)
    c, s = jnp.cos(spread), jnp.sin(spread)
    real, imag = values[:8], values[8:]
    return jnp.concatenate([c * real + s * imag, c * imag - s * real], axis=0)


def on_device(history, energy, kernel, newest, current, step_energy):
    steps, _, columns = history.shape
    count = lax.axis_size("ta")
    place_here = lax.axis_index("ta")
    bits = count.bit_length() - 1
    half = columns // 2
    latest = newest[0]
    owner = lax.div(latest, steps)
    edge = latest - place_here * steps
    side = place_here & 1
    other = 1 - side

    def swap(x, mask):
        return lax.ppermute(x, "ta", [(i, i ^ mask) for i in range(count)])

    masks = [2] + [6 if t == 2 else 1 << t for t in range(2, bits)]
    split = (place_here >> 1 ^ place_here >> 2) & 1

    mine = place_here == owner
    value, late = totals(edge, energy)
    waves = trig(energy)

    total, ahead = value, jnp.zeros_like(value)
    for t in range(bits):
        mask = 6 if t == 2 else 1 << t
        got = swap(total, mask)
        here, there = place_here >> t, owner >> t
        upper = (here & 1) == 1
        partner = here ^ 1
        counted_low = ~((there == here) & (place_here < owner))
        counted_high = (there == partner) | ((there == here) & (place_here >= owner))
        ahead = ahead + jnp.where(jnp.where(upper, counted_high, counted_low), got, 0.0)
        low_group = jnp.where(upper, partner, here)
        total = jnp.where(there == low_group, jnp.where(upper, got, total), total + got)
    off = jnp.stack([jnp.where(mine, -late, ahead), jnp.where(mine, ahead + value, ahead)])
    off_sin, off_cos = sincos(off)
    off = jnp.stack([off_cos, off_sin])

    weights = kernel_rows(kernel)
    stored = tiled(history)
    start = rotate(current, step_energy)

    new = None
    piece = 0

    def swap_beside(x, mask):
        nonlocal new, piece
        if piece == pieces_of(steps):
            return swap(x, mask)
        x, here = lax.optimization_barrier((x, stored))
        got = swap(x, mask)
        got, new = lax.optimization_barrier((got, carry(piece, here, new)))
        piece += 1
        return got

    first = split == 0

    def inner_part(x):
        keep = jnp.where(first, x[:8], x[8:])
        send = jnp.where(first, x[8:], x[:8])
        keep = keep + swap_beside(send, masks[0])
        for mask in masks[1:]:
            keep = keep + swap_beside(keep, mask)
        return keep

    def joined(keep, rest):
        return jnp.concatenate([jnp.where(first, keep, rest), jnp.where(first, rest, keep)], axis=0)

    part_other, turned_other = predict(other, edge, weights, stored, waves, off)
    from_partner = swap(part_other, 1)
    part_own, turned_own = predict(side, edge, weights, stored, waves, off)
    pred_own = inner_part(part_own + from_partner)
    pred_own = joined(pred_own, swap_beside(pred_own, masks[0]))
    pred_other = swap(pred_own, 1)
    corr_own = correct(side, weights, turned_own, start, pred_own)
    from_partner = swap(corr_own, 1)
    corr_other = correct(other, weights, turned_other, start, pred_other)
    def mine_of(x):
        x = jnp.where(side == 0, x[:, half:], x[:, :half]) if x.shape[1] > half else x
        return jnp.where(first, x[:8], x[8:])

    corr = inner_part(corr_other + from_partner)
    fresh = mine_of(start) + 0.5 * (mine_of(pred_other) + corr)
    gathered = [swap(fresh, mask) for mask in (masks[0], masks[0] ^ 1, 1)]
    new_other = joined(fresh, gathered[0])
    new_own = joined(gathered[2], gathered[1])
    while piece < pieces_of(steps):
        new = carry(piece, stored, new)
        piece += 1
    target = lax.rem(latest + 1, steps * count)
    own = lax.div(target, steps) == place_here
    corrected, new = finish(side, own, lax.rem(target, steps), new, new_own, new_other)
    return corrected, untiled(new)


def solution(mesh):
    return jax.shard_map(
        on_device,
        mesh=mesh,
        in_specs=(
            P("ta", None, "ka"),
            P("ta", None, "ka"),
            P("ta", None, None),
            P(),
            P(None, "ka"),
            P(None, "ka"),
        ),
        out_specs=(P(None, "ka"), P("ta", None, "ka")),
        check_vma=False,
    )
```

time: 388 us -> 113 us (0.29)
  waiting for transfers between devices: 145 us -> 13.9 us
  other arithmetic: 102 us -> 3.35 us
  Pallas kernels: 0 us -> 65 us
  matrix products: 43.9 us -> 0 us
  local copies, waits for them, and re-layouts: 46.1 us -> 3.03 us
  blocking collectives: 33.1 us -> 0 us
  starting transfers between devices: 0.12 us -> 25.7 us
  between operations: 14.7 us -> 1.88 us
    psum x3 -> x0, waiting for transfers between devices: 145 us -> none  [the longest x1 72.9 us: on_device(): memory_pred = lax.psum(own_pred, 'ta')]
    pallas_call x0 -> x11, Pallas kernels: none -> 65 us  [the longest x2 24 us: predict(): pl.pallas_call(functools.partial(predict_kernel, steps, group), in_specs=...]
    dot_general x2 -> x0, matrix products: 43.9 us -> none  [the longest x1 22 us: on_device(): jnp.einsum('scd,sdk->ck', kernel, rotated, precision=lax.Precision.HIGHEST)]
    rev x2 -> x0, local copies, waits for them, and re-layouts: 37.4 us -> none  [on_device(): own_suffix = jnp.cumsum(energy[::-1], axis=0)[::-1]]
    all_gather x1 -> x0, blocking collectives: 33.1 us -> none  [entering(): gathered = lax.all_gather(part, axis)]
    ppermute x0 -> x14, starting transfers between devices: none -> 25.7 us  [swap(): return lax.ppermute(x, 'ta', [(i, i ^ mask) for i in range(count)])]
    convert_element_type x3 -> x0, other arithmetic: 24 us -> none  [the longest x1 22.1 us: on_device(): rotated = rotate(history.astype(jnp.float32), phases)]
    add x9 -> x7, other arithmetic: 21.9 us -> 0.24 us  [the longest x1 0.06 us: on_device(): fresh = mine_of(start) + 0.5 * (mine_of(pred_other) + corr)]
  transfers between devices with their start and end apart: 3 -> 14, of which waited for: 2 -> 8; matrix products, arithmetic and copies ran while one was open for 16% -> 3% of each run, Pallas kernels for 0% -> 43%
where the time goes in v2:
time: 113 us
  Pallas kernels  65 us (58%)
  starting transfers between devices  25.7 us (23%)
  waiting for transfers between devices  13.9 us (12%)
  other arithmetic  3.35 us (3%)
  local copies, waits for them, and re-layouts  3.03 us (3%)
  between operations  1.88 us (2%)
    ppermute x14, starting transfers between devices, swap(): return lax.ppermute(x, 'ta', [(i, i ^ mask) for i in range(count)])  25.7 us
    pallas_call x2, Pallas kernels, predict(): pl.pallas_call(functools.partial(predict_kernel, steps, group), in_specs=...  24 us
    pallas_call x2, Pallas kernels, correct(): pl.pallas_call(functools.partial(correct_kernel, steps, group), in_specs=...  15.7 us
    ppermute x14, waiting for transfers between devices, swap(): return lax.ppermute(x, 'ta', [(i, i ^ mask) for i in range(count)])  13.9 us
    pallas_call x4, Pallas kernels, carry(): pl.pallas_call(functools.partial(carry_kernel, piece), in_specs=[HB] * le...  13.3 us
    pallas_call x1, Pallas kernels, trig(): pl.pallas_call(trig_kernel, in_specs=[VM, HB], out_specs=HB, out_shape=ja...  7.63 us
    pallas_call x1, Pallas kernels, totals(): pl.pallas_call(totals_kernel, in_specs=[SM, HB], out_specs=[VM, VM], out_...  2.98 us
  transfers between devices with their start and end apart: 14, of which 8 were waited for; matrix products, arithmetic and copies ran while one was open for 3% of the time, Pallas kernels for 43%

profile of v2, /device:TPU:0, one launch (start us, length us, event | category | flops | bytes accessed | tf_op | source)
XLA Modules:
  0.0 112.8 jit_solution(4850991522848113510)
XLA Ops:
  0.6 0.0 copy-start
  1.3 3.0 %totals.1 = (f32[128,128]{1,0:T(8,128)}, f32[128,128]{1,0:T(8,128)}) custom-call(s32[1]{0:T(128)} %bitcast.8.edge_ref, f32[64,128,128]{2,1,0:T(8,128)} %bitcast.41), custom_call_target="tpu_custom_call" | custom-call | flops 4194304 | bytes 4194304 | tf_op jit(solution)/shard_map/totals/pallas_call | solution.py:77
  4.3 3.0 %collective-permute-start = (f32[128,128]{1,0:T(8,128)}, f32[128,128]{1,0:T(8,128)S(1)}, u32[]{:S(2)}, u32[]{:S(2)}) collective-permute-start(f32[128,128]{1,0:T(8,128)} %get-tuple-element.27), channel_id=1, source_target_pairs={{0,1},{1,0},{2,3},{3,2},{4,5},{5,4},{6,7},{7,6},{8,9},{9,8},{10,11... | collective-permute-start | bytes 196616 | tf_op jit(solution)/shard_map/ppermute | solution.py:535
  7.3 1.2 %copy.17 = f32[64,16,16]{2,1,0:T(8,128)S(1)} copy(f32[64,16,16]{0,2,1:T(8,128)} %param.11) | data formatting | bytes 131072 | tf_op args[2]
  8.5 0.2 copy.18
  8.7 0.2 copy.19
  9.0 7.6 %trig.1.waves_ref = f32[2,2,64,8192]{3,2,1,0:T(8,128)} custom-call(bf16[64,192]{1,0:T(8,128)(2,1)} %constant.60.clone.tri_ref, f32[64,2,8192]{2,1,0:T(2,128)} %energy_ref.1), custom_call_target="tpu_custom_call" | custom-call | flops 41943040 | bytes 12582912 | tf_op jit(solution)/shard_map/trig/pallas_call | solution.py:135
  16.7 0.0 collective-permute-done
  16.7 0.9 add_select_fusion.2
  17.5 1.6 %collective-permute-start.1 = (f32[128,128]{1,0:T(8,128)S(1)}, f32[128,128]{1,0:T(8,128)S(1)}, u32[]{:S(2)}, u32[]{:S(2)}) collective-permute-start(f32[128,128]{1,0:T(8,128)S(1)} %add_select_fusion.2), channel_id=1, source_target_pairs={{0,2},{1,3},{2,0},{3,1},{4,6},{5,7},{6,4},{7,5},{8,10},{9,11},{10,... | collective-permute-start | bytes 196616 | tf_op jit(solution)/shard_map/ppermute | solution.py:535
  19.2 2.7 %collective-permute-done.1 = f32[128,128]{1,0:T(8,128)S(1)} collective-permute-done((f32[128,128]{1,0:T(8,128)S(1)}, f32[128,128]{1,0:T(8,128)S(1)}, u32[]{:S(2)}, u32[]{:S(2)}) %collective-permute-start.1) | collective-permute-done | bytes 65568 | tf_op jit(solution)/shard_map/ppermute | solution.py:535
  21.9 3.7 %collective-permute-start.2 = (f32[128,128]{1,0:T(8,128)S(1)}, f32[128,128]{1,0:T(8,128)S(1)}, u32[]{:S(2)}, u32[]{:S(2)}) collective-permute-start(f32[128,128]{1,0:T(8,128)S(1)} %add_select_fusion.1), channel_id=1, source_target_pairs={{0,6},{1,7},{2,4},{3,5},{4,2},{5,3},{6,0},{7,1},{8,14},{9,15},{10,... | collective-permute-start | bytes 196616 | tf_op jit(solution)/shard_map/ppermute | solution.py:535
  25.5 0.1 pad_add_fusion.1
  25.6 2.4 %collective-permute-done.2 = f32[128,128]{1,0:T(8,128)S(1)} collective-permute-done((f32[128,128]{1,0:T(8,128)S(1)}, f32[128,128]{1,0:T(8,128)S(1)}, u32[]{:S(2)}, u32[]{:S(2)}) %collective-permute-start.2) | collective-permute-done | bytes 65568 | tf_op jit(solution)/shard_map/ppermute | solution.py:535
  28.0 0.9 select_bitcast_fusion
  28.9 0.9 fusion.8
  29.7 0.1 multiply_subtract_fusion.1
  29.9 0.0 copy-done
  29.9 12.0 %predict.2 = (f32[16,4096]{1,0:T(8,128)S(1)}, f32[1024,4096]{1,0:T(8,128)}) custom-call(s32[2]{0:T(128)S(1)} %get-tuple-element.66.sc_ref, bf16[128,128]{1,0:T(8,128)(2,1)S(1)} %copy-done, bf16[8,32,128]{2,1,0:T(8,128)(2,1)S(1)} %pad_maximum_fusion.6.k_ref, bf16[64,2,512,128]{3,2,1,0:T(8,128)(2,1)} %bitcast.34, f32[2,2,64,8192]{3,2,1,0:T(8,128)} %trig.1.waves_ref, ...), custom_call_target="tpu_custom_call" | custom-call | flops 838860800 | bytes 25165824 | tf_op jit(solution)/shard_map/predict/pallas_call | solution.py:316
  41.9 0.0 copy-start.2
  41.9 0.5 collective-permute-start.3
  42.4 12.0 %predict.3 = (f32[16,4096]{1,0:T(8,128)S(1)}, f32[1024,4096]{1,0:T(8,128)}) custom-call(s32[2]{0:T(128)S(1)} %get-tuple-element.67.sc_ref, bf16[128,128]{1,0:T(8,128)(2,1)S(1)} %copy-done, bf16[8,32,128]{2,1,0:T(8,128)(2,1)S(1)} %pad_maximum_fusion.6.k_ref, bf16[64,2,512,128]{3,2,1,0:T(8,128)(2,1)} %bitcast.35, f32[2,2,64,8192]{3,2,1,0:T(8,128)} %trig.1.waves_ref, ...), custom_call_target="tpu_custom_call" | custom-call | flops 838860800 | bytes 25165824 | tf_op jit(solution)/shard_map/predict/pallas_call | solution.py:316
  54.4 0.0 collective-permute-done.3
  54.5 0.7 collective-permute-start.4
  55.1 0.0 copy-done.2
  55.1 0.9 fusion.9
  56.1 0.1 broadcast_in_dim.15
  56.2 0.2 cos.8
  56.4 0.1 broadcast_in_dim.16
  56.4 0.2 sin.8
  56.6 0.0 copy-start.1
  56.6 3.4 %carry.4.rest_0_ = bf16[64,2,512,128]{3,2,1,0:T(8,128)(2,1)} custom-call(bf16[64,2,512,128]{3,2,1,0:T(8,128)(2,1)} %bitcast.36), custom_call_target="tpu_custom_call" | custom-call | bytes 8388608 | tf_op jit(solution)/shard_map/carry/pallas_call | solution.py:450
  60.0 0.0 collective-permute-done.4
  60.0 3.3 %collective-permute-start.5 = (f32[8,4096]{1,0:T(8,128)S(1)}, f32[8,4096]{1,0:T(8,128)S(1)}, u32[]{:S(2)}, u32[]{:S(2)}) collective-permute-start(f32[8,4096]{1,0:T(8,128)S(1)} %select_add_fusion.1), channel_id=1, source_target_pairs={{0,6},{1,7},{2,4},{3,5},{4,2},{5,3},{6,0},{7,1},{8,14},{9,15},{10,... | collective-permute-start | bytes 393224 | tf_op jit(solution)/shard_map/ppermute | solution.py:535
  63.3 0.0 copy-done.1
  63.3 0.1 multiply_add_fusion
  63.4 3.3 %carry.5.rest_0_ = bf16[64,2,512,128]{3,2,1,0:T(8,128)(2,1)} custom-call(bf16[64,2,512,128]{3,2,1,0:T(8,128)(2,1)} %bitcast.37, bf16[64,2,512,128]{3,2,1,0:T(8,128)(2,1)} %carry.4.rest_0_), custom_call_target="tpu_custom_call", output_to_operand_aliasing={{}: (1, {})} | custom-call | bytes 8388608 | tf_op jit(solution)/shard_map/carry/pallas_call | solution.py:450
  66.7 0.4 collective-permute-done.5
  67.1 1.7 %collective-permute-start.6 = (f32[8,4096]{1,0:T(8,128)S(1)}, f32[8,4096]{1,0:T(8,128)S(1)}, u32[]{:S(2)}, u32[]{:S(2)}) collective-permute-start(f32[8,4096]{1,0:T(8,128)S(1)} %add.171), channel_id=1, source_target_pairs={{0,2},{1,3},{2,0},{3,1},{4,6},{5,7},{6,4},{7,5},{8,10},{9,11},{10,... | collective-permute-start | bytes 393224 | tf_op jit(solution)/shard_map/ppermute | solution.py:535
  68.8 3.3 %carry.6.rest_0_ = bf16[64,2,512,128]{3,2,1,0:T(8,128)(2,1)} custom-call(bf16[64,2,512,128]{3,2,1,0:T(8,128)(2,1)} %bitcast.38, bf16[64,2,512,128]{3,2,1,0:T(8,128)(2,1)} %carry.5.rest_0_), custom_call_target="tpu_custom_call", output_to_operand_aliasing={{}: (1, {})} | custom-call | bytes 8388608 | tf_op jit(solution)/shard_map/carry/pallas_call | solution.py:450
  72.1 0.0 collective-permute-done.6
  72.2 1.5 %collective-permute-start.7 = (f32[16,4096]{1,0:T(8,128)S(1)}, f32[16,4096]{1,0:T(8,128)S(1)}, u32[]{:S(2)}, u32[]{:S(2)}) collective-permute-start(f32[16,4096]{1,0:T(8,128)S(1)} %pad_maximum_fusion.2.pred_ref), channel_id=1, source_target_pairs={{0,1},{1,0},{2,3},{3,2},{4,5},{5,4},{6,7},{7,6},{8,9},{9,8},{10,11... | collective-permute-start | bytes 786440 | tf_op jit(solution)/shard_map/ppermute | solution.py:535
  73.7 7.9 %correct.3 = f32[16,4096]{1,0:T(8,128)S(1)} custom-call(s32[1]{0:T(128)} %bitcast.sc_ref, bf16[8,32,128]{2,1,0:T(8,128)(2,1)S(1)} %pad_maximum_fusion.6.k_ref, f32[1024,4096]{1,0:T(8,128)} %get-tuple-element.42.turned_ref, f32[16,8192]{1,0:T(8,128)S(1)} %pad_maximum_fusion.start_ref, f32[16,4096]{1,0:T(8,128)S(1)} %pad_maximum_fusion.2.pred_ref), custom_call_target="tpu_custom_call" | custom-call | flops 503316480 | bytes 16777216 | tf_op jit(solution)/shard_map/correct/pallas_call | solution.py:404
  81.6 0.7 collective-permute-start.8
  82.2 0.0 collective-permute-done.7.pred_ref
  82.2 7.9 %correct.2 = f32[16,4096]{1,0:T(8,128)S(1)} custom-call(s32[1]{0:T(128)} %bitcast.4.sc_ref, bf16[8,32,128]{2,1,0:T(8,128)(2,1)S(1)} %pad_maximum_fusion.6.k_ref, f32[1024,4096]{1,0:T(8,128)} %get-tuple-element.28.turned_ref, f32[16,8192]{1,0:T(8,128)S(1)} %pad_maximum_fusion.start_ref, f32[16,4096]{1,0:T(8,128)S(1)} %collective-permute-done.7.pred_ref), custom_call_target="tpu_custom_call" | custom-call | flops 503316480 | bytes 16777216 | tf_op jit(solution)/shard_map/correct/pallas_call | solution.py:404
  90.1 0.0 collective-permute-done.8
  90.2 1.7 %collective-permute-start.9 = (f32[8,4096]{1,0:T(8,128)S(1)}, f32[8,4096]{1,0:T(8,128)S(1)}, u32[]{:S(2)}, u32[]{:S(2)}) collective-permute-start(f32[8,4096]{1,0:T(8,128)S(1)} %slice_select_fusion.2), channel_id=1, source_target_pairs={{0,2},{1,3},{2,0},{3,1},{4,6},{5,7},{6,4},{7,5},{8,10},{9,11},{10,... | collective-permute-start | bytes 393224 | tf_op jit(solution)/shard_map/ppermute | solution.py:535
  91.9 3.3 %carry.7.old_ref = bf16[64,2,512,128]{3,2,1,0:T(8,128)(2,1)} custom-call(bf16[64,2,512,128]{3,2,1,0:T(8,128)(2,1)} %bitcast.39, bf16[64,2,512,128]{3,2,1,0:T(8,128)(2,1)} %carry.6.rest_0_), custom_call_target="tpu_custom_call", output_to_operand_aliasing={{}: (1, {})} | custom-call | bytes 8388608 | tf_op jit(solution)/shard_map/carry/pallas_call | solution.py:450
  95.2 1.5 %collective-permute-done.9 = f32[8,4096]{1,0:T(8,128)S(1)} collective-permute-done((f32[8,4096]{1,0:T(8,128)S(1)}, f32[8,4096]{1,0:T(8,128)S(1)}, u32[]{:S(2)}, u32[]{:S(2)}) %collective-permute-start.9) | collective-permute-done | bytes 131104 | tf_op jit(solution)/shard_map/ppermute | solution.py:535
  96.6 3.9 %collective-permute-start.10 = (f32[8,4096]{1,0:T(8,128)S(1)}, f32[8,4096]{1,0:T(8,128)S(1)}, u32[]{:S(2)}, u32[]{:S(2)}) collective-permute-start(f32[8,4096]{1,0:T(8,128)S(1)} %select_add_fusion), channel_id=1, source_target_pairs={{0,6},{1,7},{2,4},{3,5},{4,2},{5,3},{6,0},{7,1},{8,14},{9,15},{10,... | collective-permute-start | bytes 393224 | tf_op jit(solution)/shard_map/ppermute | solution.py:535
  100.5 3.3 %collective-permute-done.10 = f32[8,4096]{1,0:T(8,128)S(1)} collective-permute-done((f32[8,4096]{1,0:T(8,128)S(1)}, f32[8,4096]{1,0:T(8,128)S(1)}, u32[]{:S(2)}, u32[]{:S(2)}) %collective-permute-start.10) | collective-permute-done | bytes 131104 | tf_op jit(solution)/shard_map/ppermute | solution.py:535
  103.8 0.1 fusion.5
  103.9 0.9 collective-permute-start.13
  104.8 0.1 pad_add_fusion.sc_ref
  104.9 0.5 collective-permute-start.11
  105.4 2.2 %collective-permute-start.12 = (f32[8,4096]{1,0:T(8,128)S(1)}, f32[8,4096]{1,0:T(8,128)S(1)}, u32[]{:S(2)}, u32[]{:S(2)}) collective-permute-start(f32[8,4096]{1,0:T(8,128)S(1)} %fusion.5), channel_id=1, source_target_pairs={{0,3},{1,2},{2,1},{3,0},{4,7},{5,6},{6,5},{7,4},{8,11},{9,10},{10,... | collective-permute-start | bytes 393224 | tf_op jit(solution)/shard_map/ppermute | solution.py:535
  107.5 1.4 %collective-permute-done.13 = f32[8,4096]{1,0:T(8,128)S(1)} collective-permute-done((f32[8,4096]{1,0:T(8,128)S(1)}, f32[8,4096]{1,0:T(8,128)S(1)}, u32[]{:S(2)}, u32[]{:S(2)}) %collective-permute-start.13) | collective-permute-done | bytes 131104 | tf_op jit(solution)/shard_map/ppermute | solution.py:535
  109.0 0.8 collective-permute-done.11
  109.8 1.4 %collective-permute-done.12 = f32[8,4096]{1,0:T(8,128)S(1)} collective-permute-done((f32[8,4096]{1,0:T(8,128)S(1)}, f32[8,4096]{1,0:T(8,128)S(1)}, u32[]{:S(2)}, u32[]{:S(2)}) %collective-permute-start.12) | collective-permute-done | bytes 131104 | tf_op jit(solution)/shard_map/ppermute | solution.py:535
  111.3 1.4 %finish.1 = (f32[16,8192]{1,0:T(8,128)}, bf16[64,2,512,128]{3,2,1,0:T(8,128)(2,1)}) custom-call(s32[3]{0:T(128)S(1)} %pad_add_fusion.sc_ref, bf16[64,2,512,128]{3,2,1,0:T(8,128)(2,1)} %carry.7.old_ref, f32[16,4096]{1,0:T(8,128)S(1)} %pad_maximum_fusion.3.own_ref, f32[16,4096]{1,0:T(8,128)S(1)} %pad_maximum_fusion.4.other_ref), custom_call_target="tpu_custom_call", output_to_operand_aliasing={{1}: (1, {})} | custom-call | tf_op jit(solution)/shard_map/finish/pallas_call | solution.py:490
  (19 shorter events, 0.4 us)
Async XLA Ops:
  0.6 29.2 %copy-start = (bf16[128,128]{1,0:T(8,128)(2,1)S(1)}, bf16[128,128]{1,0:T(8,128)(2,1)}, u32[]{:S(2)}) copy-start(bf16[128,128]{1,0:T(8,128)(2,1)} %constant.61.clone.perm_ref) | copy-start | bytes 98308
  4.3 12.4 %collective-permute-start = (f32[128,128]{1,0:T(8,128)}, f32[128,128]{1,0:T(8,128)S(1)}, u32[]{:S(2)}, u32[]{:S(2)}) collective-permute-start(f32[128,128]{1,0:T(8,128)} %get-tuple-element.27), channel_id=1, source_target_pairs={{0,1},{1,0},{2,3},{3,2},{4,5},{5,4},{6,7},{7,6},{8,9},{9,8},{10,11... | collective-permute-start | bytes 196616 | tf_op jit(solution)/shard_map/ppermute | solution.py:535
  17.5 4.3 %collective-permute-start.1 = (f32[128,128]{1,0:T(8,128)S(1)}, f32[128,128]{1,0:T(8,128)S(1)}, u32[]{:S(2)}, u32[]{:S(2)}) collective-permute-start(f32[128,128]{1,0:T(8,128)S(1)} %add_select_fusion.2), channel_id=1, source_target_pairs={{0,2},{1,3},{2,0},{3,1},{4,6},{5,7},{6,4},{7,5},{8,10},{9,11},{10,... | collective-permute-start | bytes 196616 | tf_op jit(solution)/shard_map/ppermute | solution.py:535
  21.9 6.1 %collective-permute-start.2 = (f32[128,128]{1,0:T(8,128)S(1)}, f32[128,128]{1,0:T(8,128)S(1)}, u32[]{:S(2)}, u32[]{:S(2)}) collective-permute-start(f32[128,128]{1,0:T(8,128)S(1)} %add_select_fusion.1), channel_id=1, source_target_pairs={{0,6},{1,7},{2,4},{3,5},{4,2},{5,3},{6,0},{7,1},{8,14},{9,15},{10,... | collective-permute-start | bytes 196616 | tf_op jit(solution)/shard_map/ppermute | solution.py:535
  41.9 13.2 %copy-start.2 = (f32[2,8192]{1,0:T(2,128)S(1)}, f32[2,8192]{1,0:T(2,128)}, u32[]{:S(2)}) copy-start(f32[2,8192]{1,0:T(2,128)} %param.14) | copy-start | bytes 196612
  41.9 12.5 %collective-permute-start.3 = (f32[16,4096]{1,0:T(8,128)S(1)}, f32[16,4096]{1,0:T(8,128)S(1)}, u32[]{:S(2)}, u32[]{:S(2)}) collective-permute-start(f32[16,4096]{1,0:T(8,128)S(1)} %get-tuple-element.30), channel_id=1, source_target_pairs={{0,1},{1,0},{2,3},{3,2},{4,5},{5,4},{6,7},{7,6},{8,9},{9,8},{10,11... | collective-permute-start | bytes 786440 | tf_op jit(solution)/shard_map/ppermute | solution.py:535
  54.5 5.5 %collective-permute-start.4 = (f32[8,4096]{1,0:T(8,128)S(1)}, f32[8,4096]{1,0:T(8,128)S(1)}, u32[]{:S(2)}, u32[]{:S(2)}) collective-permute-start(f32[8,4096]{1,0:T(8,128)S(1)} %slice_select_fusion.3), channel_id=1, source_target_pairs={{0,2},{1,3},{2,0},{3,1},{4,6},{5,7},{6,4},{7,5},{8,10},{9,11},{10,... | collective-permute-start | bytes 393224 | tf_op jit(solution)/shard_map/ppermute | solution.py:535
  56.6 6.7 %copy-start.1 = (f32[16,8192]{1,0:T(8,128)S(1)}, f32[16,8192]{1,0:T(8,128)}, u32[]{:S(2)}) copy-start(f32[16,8192]{1,0:T(8,128)} %param.13) | copy-start | bytes 1572868
  60.0 7.0 %collective-permute-start.5 = (f32[8,4096]{1,0:T(8,128)S(1)}, f32[8,4096]{1,0:T(8,128)S(1)}, u32[]{:S(2)}, u32[]{:S(2)}) collective-permute-start(f32[8,4096]{1,0:T(8,128)S(1)} %select_add_fusion.1), channel_id=1, source_target_pairs={{0,6},{1,7},{2,4},{3,5},{4,2},{5,3},{6,0},{7,1},{8,14},{9,15},{10,... | collective-permute-start | bytes 393224 | tf_op jit(solution)/shard_map/ppermute | solution.py:535
  67.1 5.0 %collective-permute-start.6 = (f32[8,4096]{1,0:T(8,128)S(1)}, f32[8,4096]{1,0:T(8,128)S(1)}, u32[]{:S(2)}, u32[]{:S(2)}) collective-permute-start(f32[8,4096]{1,0:T(8,128)S(1)} %add.171), channel_id=1, source_target_pairs={{0,2},{1,3},{2,0},{3,1},{4,6},{5,7},{6,4},{7,5},{8,10},{9,11},{10,... | collective-permute-start | bytes 393224 | tf_op jit(solution)/shard_map/ppermute | solution.py:535
  72.2 10.0 %collective-permute-start.7 = (f32[16,4096]{1,0:T(8,128)S(1)}, f32[16,4096]{1,0:T(8,128)S(1)}, u32[]{:S(2)}, u32[]{:S(2)}) collective-permute-start(f32[16,4096]{1,0:T(8,128)S(1)} %pad_maximum_fusion.2.pred_ref), channel_id=1, source_target_pairs={{0,1},{1,0},{2,3},{3,2},{4,5},{5,4},{6,7},{7,6},{8,9},{9,8},{10,11... | collective-permute-start | bytes 786440 | tf_op jit(solution)/shard_map/ppermute | solution.py:535
  81.6 8.5 %collective-permute-start.8 = (f32[16,4096]{1,0:T(8,128)S(1)}, f32[16,4096]{1,0:T(8,128)S(1)}, u32[]{:S(2)}, u32[]{:S(2)}) collective-permute-start(f32[16,4096]{1,0:T(8,128)S(1)} %correct.3), channel_id=1, source_target_pairs={{0,1},{1,0},{2,3},{3,2},{4,5},{5,4},{6,7},{7,6},{8,9},{9,8},{10,11... | collective-permute-start | bytes 786440 | tf_op jit(solution)/shard_map/ppermute | solution.py:535
  90.2 6.4 %collective-permute-start.9 = (f32[8,4096]{1,0:T(8,128)S(1)}, f32[8,4096]{1,0:T(8,128)S(1)}, u32[]{:S(2)}, u32[]{:S(2)}) collective-permute-start(f32[8,4096]{1,0:T(8,128)S(1)} %slice_select_fusion.2), channel_id=1, source_target_pairs={{0,2},{1,3},{2,0},{3,1},{4,6},{5,7},{6,4},{7,5},{8,10},{9,11},{10,... | collective-permute-start | bytes 393224 | tf_op jit(solution)/shard_map/ppermute | solution.py:535
  96.6 7.2 %collective-permute-start.10 = (f32[8,4096]{1,0:T(8,128)S(1)}, f32[8,4096]{1,0:T(8,128)S(1)}, u32[]{:S(2)}, u32[]{:S(2)}) collective-permute-start(f32[8,4096]{1,0:T(8,128)S(1)} %select_add_fusion), channel_id=1, source_target_pairs={{0,6},{1,7},{2,4},{3,5},{4,2},{5,3},{6,0},{7,1},{8,14},{9,15},{10,... | collective-permute-start | bytes 393224 | tf_op jit(solution)/shard_map/ppermute | solution.py:535
  103.9 5.0 %collective-permute-start.13 = (f32[8,4096]{1,0:T(8,128)S(1)}, f32[8,4096]{1,0:T(8,128)S(1)}, u32[]{:S(2)}, u32[]{:S(2)}) collective-permute-start(f32[8,4096]{1,0:T(8,128)S(1)} %fusion.5), channel_id=1, source_target_pairs={{0,2},{1,3},{2,0},{3,1},{4,6},{5,7},{6,4},{7,5},{8,10},{9,11},{10,... | collective-permute-start | bytes 393224 | tf_op jit(solution)/shard_map/ppermute | solution.py:535
  104.9 5.0 %collective-permute-start.11 = (f32[8,4096]{1,0:T(8,128)S(1)}, f32[8,4096]{1,0:T(8,128)S(1)}, u32[]{:S(2)}, u32[]{:S(2)}) collective-permute-start(f32[8,4096]{1,0:T(8,128)S(1)} %fusion.5), channel_id=1, source_target_pairs={{0,1},{1,0},{2,3},{3,2},{4,5},{5,4},{6,7},{7,6},{8,9},{9,8},{10,11... | collective-permute-start | bytes 393224 | tf_op jit(solution)/shard_map/ppermute | solution.py:535
  105.4 5.9 %collective-permute-start.12 = (f32[8,4096]{1,0:T(8,128)S(1)}, f32[8,4096]{1,0:T(8,128)S(1)}, u32[]{:S(2)}, u32[]{:S(2)}) collective-permute-start(f32[8,4096]{1,0:T(8,128)S(1)} %fusion.5), channel_id=1, source_target_pairs={{0,3},{1,2},{2,1},{3,0},{4,7},{5,6},{6,5},{7,4},{8,11},{9,10},{10,... | collective-permute-start | bytes 393224 | tf_op jit(solution)/shard_map/ppermute | solution.py:535

commit v3 on v2

--- a/solution.py
+++ b/solution.py
@@ -80,20 +80,21 @@
         out_specs=[VM, VM],
         out_shape=[jax.ShapeDtypeStruct((rows, LANES), F32)] * 2,
         scratch_shapes=[pltpu.VMEM(view.shape, F32), pltpu.SemaphoreType.DMA((pieces_of(steps),))],
-        compiler_params=pltpu.CompilerParams(vmem_limit_bytes=54 << 20),
+        compiler_params=pltpu.CompilerParams(vmem_limit_bytes=51 << 20),
         cost_estimate=pl.CostEstimate(flops=4 * energy.size, bytes_accessed=4 * energy.size, transcendentals=0),
         name="totals",
     )(jnp.reshape(edge, (1,)).astype(jnp.int32), view)
 
 
-def trig_kernel(tri_ref, energy_ref, waves_ref, held, made, in_sems, out_sems):
+def trig_kernel(side_ref, tri_ref, energy_ref, waves_ref, held, made, in_sems, out_sems):
     columns = held.shape[-1]
     chunk = min(CHUNK, columns)
     count = columns // chunk
 
     def copy_in(j, a):
+        there = pl.ds(pl.multiple_of(side_ref[0] * columns + j * chunk, chunk), chunk)
         lanes = pl.ds(j * chunk, chunk)
-        return pltpu.make_async_copy(energy_ref.at[:, a, lanes], held.at[a, :, lanes], in_sems.at[j, a])
+        return pltpu.make_async_copy(energy_ref.at[:, a, there], held.at[a, :, lanes], in_sems.at[j, a])
 
     def copy_out(j):
         lanes = pl.ds(j * chunk, chunk)
@@ -126,15 +127,15 @@
         copy_out(j).wait()
 
 
-def trig(energy):
-    steps, _, columns = energy.shape
+def trig(side, energy):
+    steps, columns = energy.shape[0], energy.shape[2] // 2
     tri = 0.5 * np.triu(np.ones((steps, steps), np.float32))
     tri = jnp.asarray(np.concatenate([tri] * 3, axis=1), BF)
     count = columns // min(CHUNK, columns)
     size = (2, 2, steps, columns)
     return pl.pallas_call(
         trig_kernel,
-        in_specs=[VM, HB],
+        in_specs=[SM, VM, HB],
         out_specs=HB,
         out_shape=jax.ShapeDtypeStruct(size, F32),
         scratch_shapes=[
@@ -144,9 +145,9 @@
             pltpu.SemaphoreType.DMA((count,)),
         ],
         compiler_params=pltpu.CompilerParams(vmem_limit_bytes=54 << 20),
-        cost_estimate=pl.CostEstimate(flops=40 * energy.size, bytes_accessed=12 * energy.size, transcendentals=0),
+        cost_estimate=pl.CostEstimate(flops=20 * energy.size, bytes_accessed=6 * energy.size, transcendentals=0),
         name="trig",
-    )(tri, energy)
+    )(jnp.reshape(side, (1,)).astype(jnp.int32), tri, energy)
 
 
 def permutation(group):
@@ -169,28 +170,29 @@
     return jnp.concatenate([top, k - top], axis=1).astype(BF)
 
 
-def predict_kernel(steps, group, sc_ref, perm_ref, k_ref, h_ref, waves_ref, off_ref, out_ref, turned_ref, held, in_sems, waves, wave_sems, kept, out_sems):
+def predict_kernel(inside, steps, group, sc_ref, perm_ref, k_ref, h_ref, waves_ref, off_ref, out_ref, *rest):
+    near_ref, far_ref, held, in_sems, waves, wave_sems, kept, out_sems = rest
     columns = out_ref.shape[-1]
     chunk = kept.shape[-1]
     count = columns // chunk
     tiles = chunk // LANES
     blocks = group // 8
     edge = sc_ref[1]
-    base = sc_ref[0] * columns
 
     def copy_in(j):
         there = pl.ds(pl.multiple_of((sc_ref[0] * (columns // LANES) + j * tiles) * 8, 16), tiles * 8)
         here = pl.ds(pl.multiple_of(j * tiles * 8, 16), tiles * 8)
         return pltpu.make_async_copy(h_ref.at[:, :, there], held.at[:, :, here], in_sems.at[j])
 
-    def copy_out(j):
-        there = pl.ds(pl.multiple_of(j * chunk, chunk), chunk)
-        return pltpu.make_async_copy(kept.at[j % 2], turned_ref.at[:, there], out_sems.at[j % 2])
+    def copy_out(j, near):
+        there = pl.ds(pl.multiple_of((j if near else j - inside) * chunk, chunk), chunk)
+        return pltpu.make_async_copy(
+            kept.at[j % 2], (near_ref if near else far_ref).at[:, there], out_sems.at[j % 2]
+        )
 
     def copy_waves(j):
-        there = pl.ds(pl.multiple_of(base + j * chunk, chunk), chunk)
-        here = pl.ds(pl.multiple_of(j * chunk, chunk), chunk)
-        return pltpu.make_async_copy(waves_ref.at[:, :, :, there], waves.at[:, :, :, here], wave_sems.at[j])
+        lanes = pl.ds(pl.multiple_of(j * chunk, chunk), chunk)
+        return pltpu.make_async_copy(waves_ref.at[:, :, :, lanes], waves.at[:, :, :, lanes], wave_sems.at[j])
 
     for j in range(count):
         copy_in(j).start()
@@ -290,37 +292,39 @@
             moved = later
         contract(*waiting)
 
-    @pl.loop(0, count)
-    def _(j):
-        copy_in(j).wait()
-        copy_waves(j).wait()
-
-        @pl.when(j >= 2)
-        def _():
-            copy_out(j).wait()
-
-        work(j)
-        copy_out(j).start()
-
+    def span(first, last, near):
+        @pl.loop(first, last)
+        def _(j):
+            copy_in(j).wait()
+            copy_waves(j).wait()
+
+            @pl.when(j >= 2)
+            def _():
+                copy_out(j, near).wait()
+
+            work(j)
+            copy_out(j, near).start()
+
+    span(0, inside, True)
+    span(inside, count, False)
     for j in range(max(count - 2, 0), count):
-        copy_out(j).wait()
+        copy_out(j, j < inside).wait()
 
 
 def predict(side, edge, weights, stored, waves, off):
     steps = waves.shape[2]
-    columns = waves.shape[3] // 2
+    columns = waves.shape[3]
     group = GROUP
     chunk = min(CHUNK, columns)
     count = columns // chunk
+    inside = count // 2
     size = steps * 16 * columns
     return pl.pallas_call(
-        functools.partial(predict_kernel, steps, group),
+        functools.partial(predict_kernel, inside, steps, group),
         in_specs=[SM, VM, VM, HB, HB, VM],
-        out_specs=[VM, HB],
-        out_shape=[
-            jax.ShapeDtypeStruct((16, columns), F32),
-            jax.ShapeDtypeStruct((steps * 16, columns), F32),
-        ],
+        out_specs=[VM, HB, HB],
+        out_shape=[jax.ShapeDtypeStruct((16, columns), F32)]
+        + [jax.ShapeDtypeStruct((steps * 16, c), F32) for c in (inside * chunk, columns - inside * chunk)],
         scratch_shapes=[
             pltpu.VMEM((steps, 2, columns // 16, LANES), BF),
             pltpu.SemaphoreType.DMA((count,)),
@@ -329,13 +333,15 @@
             pltpu.VMEM((2, steps * 16, chunk), F32),
             pltpu.SemaphoreType.DMA((2,)),
         ],
-        compiler_params=pltpu.CompilerParams(vmem_limit_bytes=50 << 20),
+        compiler_params=pltpu.CompilerParams(vmem_limit_bytes=51 << 20),
         cost_estimate=pl.CostEstimate(flops=200 * size, bytes_accessed=6 * size, transcendentals=0),
         name="predict",
     )(jnp.stack([side, edge]).astype(jnp.int32), permutation(group), weights, stored, waves, off)
 
 
-def correct_kernel(steps, group, sc_ref, k_ref, turned_ref, start_ref, pred_ref, out_ref, held, sems, wide_ref):
+def correct_kernel(inside, steps, group, sc_ref, k_ref, start_ref, pred_ref, *rest):
+    near_ref = rest[0] if inside else None
+    far_ref, out_ref, held, sems, wide_ref = rest[-5:]
     columns = out_ref.shape[-1]
     chunk = min(CHUNK, columns)
     count = columns // chunk
@@ -345,12 +351,12 @@
 
     def copy_in(j):
         lanes = pl.ds(pl.multiple_of(j * chunk, chunk), chunk)
-        return pltpu.make_async_copy(turned_ref.at[:, lanes], held.at[:, lanes], sems.at[j])
-
-    for j in range(count):
+        return pltpu.make_async_copy(far_ref.at[:, lanes], held.at[:, lanes], sems.at[j])
+
+    for j in range(count - inside):
         copy_in(j).start()
 
-    def work(j):
+    def work(j, source, offset):
         items = [(n, i) for n in range(chunk // width) for i in range(steps // group)]
         sums = {}
 
@@ -376,9 +382,10 @@
                 for c in range(16):
                     wide_ref[n, c] = jnp.broadcast_to(full[c : c + 1], (8, width))
             parts = []
+            here = pl.ds(pl.multiple_of((j - offset) * chunk + n * width, width), width)
             for g in range(group // 8):
                 at = i * rows + 128 * g
-                turned = [held[at + 8 * c : at + 8 * c + 8, span(n)] for c in range(16)]
+                turned = [source[at + 8 * c : at + 8 * c + 8, here] for c in range(16)]
                 terms = [turned[c] * wide_ref[n, c] for c in range(16)]
                 while len(terms) > 1:
                     terms = [terms[m] + terms[m + 1] for m in range(0, len(terms), 2)]
@@ -389,32 +396,40 @@
             waiting = (n, i, top, (x - top.astype(F32)).astype(BF))
         contract(*waiting)
 
-    @pl.loop(0, count)
+    if inside:
+
+        @pl.loop(0, inside)
+        def _(j):
+            work(j, near_ref, 0)
+
+    @pl.loop(inside, count)
     def _(j):
-        copy_in(j).wait()
-        work(j)
-
-
-def correct(side, weights, turned, start, pred):
+        copy_in(j - inside).wait()
+        work(j, held, inside)
+
+
+def correct(side, weights, start, pred, *turned):
     columns = pred.shape[1]
-    steps = turned.shape[0] // 16
+    steps = turned[0].shape[0] // 16
     group = GROUP
     chunk = min(CHUNK, columns)
     size = steps * 16 * columns
+    far = turned[-1]
+    inside = (columns - far.shape[1]) // chunk
     return pl.pallas_call(
-        functools.partial(correct_kernel, steps, group),
-        in_specs=[SM, VM, HB, VM, VM],
+        functools.partial(correct_kernel, inside, steps, group),
+        in_specs=[SM, VM, VM, VM] + [VM] * (inside > 0) + [HB],
         out_specs=VM,
         out_shape=jax.ShapeDtypeStruct((16, columns), F32),
         scratch_shapes=[
-            pltpu.VMEM(turned.shape, F32),
-            pltpu.SemaphoreType.DMA((columns // chunk,)),
+            pltpu.VMEM(far.shape, F32),
+            pltpu.SemaphoreType.DMA((columns // chunk - inside,)),
             pltpu.VMEM((chunk // (2 * LANES), 16, 8, 2 * LANES), F32),
         ],
-        compiler_params=pltpu.CompilerParams(vmem_limit_bytes=46 << 20),
+        compiler_params=pltpu.CompilerParams(vmem_limit_bytes=44 << 20),
         cost_estimate=pl.CostEstimate(flops=120 * size, bytes_accessed=4 * size, transcendentals=0),
         name="correct",
-    )(jnp.reshape(side, (1,)).astype(jnp.int32), weights, turned, start, pred)
+    )(jnp.reshape(side, (1,)).astype(jnp.int32), weights, start, pred, *turned)
 
 
 def carry_kernel(piece, stored_ref, *rest):
@@ -458,21 +473,26 @@
             pltpu.SemaphoreType.DMA((count,)),
         ],
         input_output_aliases={} if new is None else {1: 0},
-        compiler_params=pltpu.CompilerParams(vmem_limit_bytes=46 << 20),
+        compiler_params=pltpu.CompilerParams(vmem_limit_bytes=42 << 20),
         cost_estimate=pl.CostEstimate(flops=0, bytes_accessed=size, transcendentals=0),
         name="carry",
     )(*args)
 
 
-def finish_kernel(sc_ref, old_ref, own_ref, other_ref, whole_ref, new_ref, held, sem):
+def finish_kernel(sc_ref, old_ref, own_ref, other_ref, whole_ref, new_ref, held, sem, sems):
     half = own_ref.shape[1]
     side = sc_ref[0]
-    for at, ref in ((side, own_ref), (1 - side, other_ref)):
-        whole_ref[:, pl.ds(pl.multiple_of(at * half, LANES), half)] = ref[...]
+    places = ((side, own_ref), (1 - side, other_ref))
+    writes = [
+        pltpu.make_async_copy(ref, whole_ref.at[:, pl.ds(pl.multiple_of(at * half, LANES), half)], sems.at[n])
+        for n, (at, ref) in enumerate(places)
+    ]
+    for write in writes:
+        write.start()
 
     @pl.when(sc_ref[1] == 1)
     def _():
-        for at, ref in ((side, own_ref), (1 - side, other_ref)):
+        for at, ref in places:
             for part in range(2):
                 for n in range(half // (2 * LANES)):
                     tiles = [
@@ -484,15 +504,22 @@
         copy.start()
         copy.wait()
 
+    for write in writes:
+        write.wait()
+
 
 def finish(side, own, slot, new, new_own, new_other):
     rows, half = new_own.shape
     return pl.pallas_call(
         finish_kernel,
         in_specs=[SM, HB, VM, VM],
-        out_specs=[VM, HB],
+        out_specs=[HB, HB],
         out_shape=[jax.ShapeDtypeStruct((rows, 2 * half), F32), jax.ShapeDtypeStruct(new.shape, new.dtype)],
-        scratch_shapes=[pltpu.VMEM(new.shape[1:], BF), pltpu.SemaphoreType.DMA],
+        scratch_shapes=[
+            pltpu.VMEM(new.shape[1:], BF),
+            pltpu.SemaphoreType.DMA,
+            pltpu.SemaphoreType.DMA((2,)),
+        ],
         input_output_aliases={1: 1},
         compiler_params=pltpu.CompilerParams(vmem_limit_bytes=40 << 20),
         name="finish",
@@ -539,12 +566,17 @@
 
     mine = place_here == owner
     value, late = totals(edge, energy)
-    waves = trig(energy)
 
     total, ahead = value, jnp.zeros_like(value)
+    waves = []
     for t in range(bits):
         mask = 6 if t == 2 else 1 << t
-        got = swap(total, mask)
+        if t < 2:
+            total, seen = lax.optimization_barrier((total, energy))
+            got, made = lax.optimization_barrier((swap(total, mask), trig((other, side)[t], seen)))
+            waves.append(made)
+        else:
+            got = swap(total, mask)
         here, there = place_here >> t, owner >> t
         upper = (here & 1) == 1
         partner = here ^ 1
@@ -557,6 +589,8 @@
     off_sin, off_cos = sincos(off)
     off = jnp.stack([off_cos, off_sin])
 
+    while len(waves) < 2:
+        waves.append(trig((other, side)[len(waves)], energy))
     weights = kernel_rows(kernel)
     stored = tiled(history)
     start = rotate(current, step_energy)
@@ -587,15 +621,15 @@
     def joined(keep, rest):
         return jnp.concatenate([jnp.where(first, keep, rest), jnp.where(first, rest, keep)], axis=0)
 
-    part_other, turned_other = predict(other, edge, weights, stored, waves, off)
+    part_other, *turned_other = predict(other, edge, weights, stored, waves[0], off)
     from_partner = swap(part_other, 1)
-    part_own, turned_own = predict(side, edge, weights, stored, waves, off)
+    part_own, *turned_own = predict(side, edge, weights, stored, waves[1], off)
     pred_own = inner_part(part_own + from_partner)
     pred_own = joined(pred_own, swap_beside(pred_own, masks[0]))
     pred_other = swap(pred_own, 1)
-    corr_own = correct(side, weights, turned_own, start, pred_own)
+    corr_own = correct(side, weights, start, pred_own, *turned_own)
     from_partner = swap(corr_own, 1)
-    corr_other = correct(other, weights, turned_other, start, pred_other)
+    corr_other = correct(other, weights, start, pred_other, *turned_other)
     def mine_of(x):
         x = jnp.where(side == 0, x[:, half:], x[:, :half]) if x.shape[1] > half else x
         return jnp.where(first, x[:8], x[8:])

time: 113 us -> 107 us (0.947)
  starting transfers between devices: 25.7 us -> 22.2 us
  other arithmetic: 3.35 us -> 0.83 us
    ppermute x14, starting transfers between devices: 25.7 us -> 22.2 us  [swap(): return lax.ppermute(x, 'ta', [(i, i ^ mask) for i in range(count)])]
    another operation x2, other arithmetic: 1.72 us -> 0.04 us  [on_device(): jnp.stack([jnp.where(mine, -late, ahead), jnp.where(mine, ahead + value,...]
    pallas_call x6 -> x7, Pallas kernels: 48.8 us -> 48 us  [the longest x2 24.3 us: predict(): pl.pallas_call(functools.partial(predict_kernel, inside, steps, group), i...]
  transfers between devices with their start and end apart: 14 -> 14, of which waited for: 8 -> 8; matrix products, arithmetic and copies ran while one was open for 3% -> 3% of each run, Pallas kernels for 43% -> 45%
where the time goes in v3:
time: 107 us; the launch traced here: 106 us
  Pallas kernels  64.2 us (60%)
  starting transfers between devices  22.2 us (21%)
  waiting for transfers between devices  14 us (13%)
  local copies, waits for them, and re-layouts  3.07 us (3%)
  between operations  2 us (2%)
    pallas_call x2, Pallas kernels, predict(): pl.pallas_call(functools.partial(predict_kernel, inside, steps, group), i...  24.3 us
    ppermute x14, starting transfers between devices, swap(): return lax.ppermute(x, 'ta', [(i, i ^ mask) for i in range(count)])  22.2 us
    ppermute x14, waiting for transfers between devices, swap(): return lax.ppermute(x, 'ta', [(i, i ^ mask) for i in range(count)])  14 us
    pallas_call x4, Pallas kernels, carry(): pl.pallas_call(functools.partial(carry_kernel, piece), in_specs=[HB] * le...  13.8 us
    pallas_call x2, Pallas kernels, correct(): pl.pallas_call(functools.partial(correct_kernel, inside, steps, group), i...  11.8 us
    pallas_call x2, Pallas kernels, trig(): pl.pallas_call(trig_kernel, in_specs=[SM, VM, HB], out_specs=HB, out_shap...  10.5 us
    pallas_call x1, Pallas kernels, totals(): pl.pallas_call(totals_kernel, in_specs=[SM, HB], out_specs=[VM, VM], out_...  2.33 us
  transfers between devices with their start and end apart: 14, of which 8 were waited for; matrix products, arithmetic and copies ran while one was open for 3% of the time, Pallas kernels for 45%

profile of v3, /device:TPU:0, one launch (start us, length us, event | category | flops | bytes accessed | tf_op | source)
XLA Modules:
  0.0 106.2 jit_solution(10811626102082523457)
XLA Ops:
  1.3 2.3 %totals.1 = (f32[128,128]{1,0:T(8,128)S(1)}, f32[128,128]{1,0:T(8,128)S(1)}) custom-call(s32[1]{0:T(128)} %bitcast.8.edge_ref, f32[64,128,128]{2,1,0:T(8,128)} %bitcast.45), custom_call_target="tpu_custom_call" | custom-call | flops 4194304 | bytes 4194304 | tf_op jit(solution)/shard_map/totals/pallas_call | solution.py:77
  3.6 3.0 %collective-permute-start = (f32[128,128]{1,0:T(8,128)S(1)}, f32[128,128]{1,0:T(8,128)S(1)}, u32[]{:S(2)}, u32[]{:S(2)}) collective-permute-start(f32[128,128]{1,0:T(8,128)S(1)} %get-tuple-element.37), channel_id=1, source_target_pairs={{0,1},{1,0},{2,3},{3,2},{4,5},{5,4},{6,7},{7,6},{8,9},{9,8},{10,11... | collective-permute-start | bytes 196616 | tf_op jit(solution)/shard_map/ppermute | solution.py:562
  6.7 1.2 %copy.18 = f32[64,16,16]{2,1,0:T(8,128)S(1)} copy(f32[64,16,16]{0,2,1:T(8,128)} %param.12) | data formatting | bytes 131072 | tf_op args[2]
  7.8 0.2 copy.19
  8.1 0.2 copy.20
  8.4 0.0 copy-start
  8.4 5.3 %trig.2.waves_ref = f32[2,2,64,4096]{3,2,1,0:T(8,128)} custom-call(s32[1]{0:T(128)} %bitcast.4.side_ref.sc_ref, bf16[64,192]{1,0:T(8,128)(2,1)} %constant.60.clone.tri_ref, f32[64,2,8192]{2,1,0:T(2,128)} %energy_ref.1), custom_call_target="tpu_custom_call" | custom-call | flops 20971520 | bytes 6291456 | tf_op jit(solution)/shard_map/trig/pallas_call | solution.py:136
  13.7 0.0 collective-permute-done
  13.7 1.6 %collective-permute-start.1 = (f32[128,128]{1,0:T(8,128)S(1)}, f32[128,128]{1,0:T(8,128)S(1)}, u32[]{:S(2)}, u32[]{:S(2)}) collective-permute-start(f32[128,128]{1,0:T(8,128)S(1)} %add_select_fusion.2), channel_id=1, source_target_pairs={{0,2},{1,3},{2,0},{3,1},{4,6},{5,7},{6,4},{7,5},{8,10},{9,11},{10,... | collective-permute-start | bytes 196616 | tf_op jit(solution)/shard_map/ppermute | solution.py:562
  15.4 5.2 %trig.3.waves_ref = f32[2,2,64,4096]{3,2,1,0:T(8,128)} custom-call(s32[1]{0:T(128)} %bitcast.side_ref.sc_ref, bf16[64,192]{1,0:T(8,128)(2,1)} %constant.60.clone.tri_ref, f32[64,2,8192]{2,1,0:T(2,128)} %energy_ref.1), custom_call_target="tpu_custom_call" | custom-call | flops 20971520 | bytes 6291456 | tf_op jit(solution)/shard_map/trig/pallas_call | solution.py:136
  20.6 0.0 collective-permute-done.1
  20.6 2.5 %collective-permute-start.2 = (f32[128,128]{1,0:T(8,128)S(1)}, f32[128,128]{1,0:T(8,128)S(1)}, u32[]{:S(2)}, u32[]{:S(2)}) collective-permute-start(f32[128,128]{1,0:T(8,128)S(1)} %add_select_fusion.1), channel_id=1, source_target_pairs={{0,6},{1,7},{2,4},{3,5},{4,2},{5,3},{6,0},{7,1},{8,14},{9,15},{10,... | collective-permute-start | bytes 196616 | tf_op jit(solution)/shard_map/ppermute | solution.py:562
  23.2 0.1 pad_add_fusion.1
  23.2 3.5 %collective-permute-done.2 = f32[128,128]{1,0:T(8,128)S(1)} collective-permute-done((f32[128,128]{1,0:T(8,128)S(1)}, f32[128,128]{1,0:T(8,128)S(1)}, u32[]{:S(2)}, u32[]{:S(2)}) %collective-permute-start.2) | collective-permute-done | bytes 65568 | tf_op jit(solution)/shard_map/ppermute | solution.py:562
  26.8 0.1 multiply_subtract_fusion.1
  26.9 0.0 copy-done
  27.0 12.2 %predict.3 = (f32[16,4096]{1,0:T(8,128)S(1)}, f32[1024,2048]{1,0:T(8,128)}, f32[1024,2048]{1,0:T(8,128)}) custom-call(s32[2]{0:T(128)S(1)} %get-tuple-element.87.sc_ref, bf16[128,128]{1,0:T(8,128)(2,1)S(1)} %copy-done, bf16[8,32,128]{2,1,0:T(8,128)(2,1)S(1)} %pad_maximum_fusion.6.k_ref, bf16[64,2,512,128]{3,2,1,0:T(8,128)(2,1)} %bitcast.38, ...), custom_call_target="tpu_custom_call" | custom-call | flops 838860800 | bytes 25165824 | tf_op jit(solution)/shard_map/predict/pallas_call | solution.py:322
  39.1 0.6 collective-permute-start.3
  39.7 12.1 %predict.2 = (f32[16,4096]{1,0:T(8,128)S(1)}, f32[1024,2048]{1,0:T(8,128)}, f32[1024,2048]{1,0:T(8,128)}) custom-call(s32[2]{0:T(128)S(1)} %get-tuple-element.86.sc_ref, bf16[128,128]{1,0:T(8,128)(2,1)S(1)} %copy-done, bf16[8,32,128]{2,1,0:T(8,128)(2,1)S(1)} %pad_maximum_fusion.6.k_ref, bf16[64,2,512,128]{3,2,1,0:T(8,128)(2,1)} %bitcast.39, ...), custom_call_target="tpu_custom_call" | custom-call | flops 838860800 | bytes 25165824 | tf_op jit(solution)/shard_map/predict/pallas_call | solution.py:322
  51.8 0.0 collective-permute-done.3
  51.9 0.1 collective-permute-start.4
  52.0 0.0 copy-done.2
  52.0 1.0 fusion.9
  53.0 0.1 broadcast_in_dim.14
  53.0 0.2 cos.8
  53.2 0.1 broadcast_in_dim.15
  53.3 0.2 sin.8
  53.5 0.0 copy-start.1
  53.5 3.4 %carry.4.rest_0_ = bf16[64,2,512,128]{3,2,1,0:T(8,128)(2,1)} custom-call(bf16[64,2,512,128]{3,2,1,0:T(8,128)(2,1)} %bitcast.40), custom_call_target="tpu_custom_call" | custom-call | bytes 8388608 | tf_op jit(solution)/shard_map/carry/pallas_call | solution.py:465
  56.9 0.1 collective-permute-done.4
  57.0 2.5 %collective-permute-start.5 = (f32[8,4096]{1,0:T(8,128)S(1)}, f32[8,4096]{1,0:T(8,128)S(1)}, u32[]{:S(2)}, u32[]{:S(2)}) collective-permute-start(f32[8,4096]{1,0:T(8,128)S(1)} %select_add_fusion.1), channel_id=1, source_target_pairs={{0,6},{1,7},{2,4},{3,5},{4,2},{5,3},{6,0},{7,1},{8,14},{9,15},{10,... | collective-permute-start | bytes 393224 | tf_op jit(solution)/shard_map/ppermute | solution.py:562
  59.5 0.0 copy-done.1
  59.5 0.1 multiply_add_fusion
  59.6 0.0 slice-start
  59.6 3.6 %carry.5.rest_0_ = bf16[64,2,512,128]{3,2,1,0:T(8,128)(2,1)} custom-call(bf16[64,2,512,128]{3,2,1,0:T(8,128)(2,1)} %bitcast.41, bf16[64,2,512,128]{3,2,1,0:T(8,128)(2,1)} %carry.4.rest_0_), custom_call_target="tpu_custom_call", output_to_operand_aliasing={{}: (1, {})} | custom-call | bytes 8388608 | tf_op jit(solution)/shard_map/carry/pallas_call | solution.py:465
  63.2 0.8 collective-permute-done.5
  64.0 1.5 %collective-permute-start.6 = (f32[8,4096]{1,0:T(8,128)S(1)}, f32[8,4096]{1,0:T(8,128)S(1)}, u32[]{:S(2)}, u32[]{:S(2)}) collective-permute-start(f32[8,4096]{1,0:T(8,128)S(1)} %add.171), channel_id=1, source_target_pairs={{0,2},{1,3},{2,0},{3,1},{4,6},{5,7},{6,4},{7,5},{8,10},{9,11},{10,... | collective-permute-start | bytes 393224 | tf_op jit(solution)/shard_map/ppermute | solution.py:562
  65.5 0.0 slice-start.3
  65.5 0.0 slice-start.1
  65.5 3.6 %carry.6.rest_0_ = bf16[64,2,512,128]{3,2,1,0:T(8,128)(2,1)} custom-call(bf16[64,2,512,128]{3,2,1,0:T(8,128)(2,1)} %bitcast.42, bf16[64,2,512,128]{3,2,1,0:T(8,128)(2,1)} %carry.5.rest_0_), custom_call_target="tpu_custom_call", output_to_operand_aliasing={{}: (1, {})} | custom-call | bytes 8388608 | tf_op jit(solution)/shard_map/carry/pallas_call | solution.py:465
  69.1 0.0 collective-permute-done.6
  69.1 1.6 %collective-permute-start.7 = (f32[16,4096]{1,0:T(8,128)S(1)}, f32[16,4096]{1,0:T(8,128)S(1)}, u32[]{:S(2)}, u32[]{:S(2)}) collective-permute-start(f32[16,4096]{1,0:T(8,128)S(1)} %pad_maximum_fusion.2.pred_ref), channel_id=1, source_target_pairs={{0,1},{1,0},{2,3},{3,2},{4,5},{5,4},{6,7},{7,6},{8,9},{9,8},{10,11... | collective-permute-start | bytes 786440 | tf_op jit(solution)/shard_map/ppermute | solution.py:562
  70.7 0.0 slice-done.2
  70.7 0.0 slice-done.3
  70.7 5.8 %correct.3 = f32[16,4096]{1,0:T(8,128)S(1)} custom-call(s32[1]{0:T(128)} %bitcast.side_ref.sc_ref, bf16[8,32,128]{2,1,0:T(8,128)(2,1)S(1)} %pad_maximum_fusion.6.k_ref, f32[16,8192]{1,0:T(8,128)S(1)} %pad_maximum_fusion.start_ref, f32[16,4096]{1,0:T(8,128)S(1)} %pad_maximum_fusion.2.pred_ref, f32[1024,2048]{1,0:T(8,128)S(1)} %bitcast.37, ...), custom_call_target="tpu_custom_call" | custom-call | flops 503316480 | bytes 16777216 | tf_op jit(solution)/shard_map/correct/pallas_call | solution.py:419
  76.5 1.5 %collective-permute-start.8 = (f32[16,4096]{1,0:T(8,128)S(1)}, f32[16,4096]{1,0:T(8,128)S(1)}, u32[]{:S(2)}, u32[]{:S(2)}) collective-permute-start(f32[16,4096]{1,0:T(8,128)S(1)} %correct.3), channel_id=1, source_target_pairs={{0,1},{1,0},{2,3},{3,2},{4,5},{5,4},{6,7},{7,6},{8,9},{9,8},{10,11... | collective-permute-start | bytes 786440 | tf_op jit(solution)/shard_map/ppermute | solution.py:562
  78.0 0.0 collective-permute-done.7.pred_ref
  78.0 0.0 slice-done
  78.0 0.0 slice-done.1
  78.0 6.0 %correct.2 = f32[16,4096]{1,0:T(8,128)S(1)} custom-call(s32[1]{0:T(128)} %bitcast.4.side_ref.sc_ref, bf16[8,32,128]{2,1,0:T(8,128)(2,1)S(1)} %pad_maximum_fusion.6.k_ref, f32[16,8192]{1,0:T(8,128)S(1)} %pad_maximum_fusion.start_ref, f32[16,4096]{1,0:T(8,128)S(1)} %collective-permute-done.7.pred_ref, f32[1024,2048]{1,0:T(8,128)S(1)} %bitcast.35, ...), custom_call_target="tpu_custom_call" | custom-call | flops 503316480 | bytes 16777216 | tf_op jit(solution)/shard_map/correct/pallas_call | solution.py:419
  84.0 0.0 collective-permute-done.8
  84.1 1.1 %collective-permute-start.9 = (f32[8,4096]{1,0:T(8,128)S(1)}, f32[8,4096]{1,0:T(8,128)S(1)}, u32[]{:S(2)}, u32[]{:S(2)}) collective-permute-start(f32[8,4096]{1,0:T(8,128)S(1)} %slice_select_fusion.2), channel_id=1, source_target_pairs={{0,2},{1,3},{2,0},{3,1},{4,6},{5,7},{6,4},{7,5},{8,10},{9,11},{10,... | collective-permute-start | bytes 393224 | tf_op jit(solution)/shard_map/ppermute | solution.py:562
  85.2 3.3 %carry.7.old_ref = bf16[64,2,512,128]{3,2,1,0:T(8,128)(2,1)} custom-call(bf16[64,2,512,128]{3,2,1,0:T(8,128)(2,1)} %bitcast.43, bf16[64,2,512,128]{3,2,1,0:T(8,128)(2,1)} %carry.6.rest_0_), custom_call_target="tpu_custom_call", output_to_operand_aliasing={{}: (1, {})} | custom-call | bytes 8388608 | tf_op jit(solution)/shard_map/carry/pallas_call | solution.py:465
  88.5 0.6 collective-permute-done.9
  89.1 2.7 %collective-permute-start.10 = (f32[8,4096]{1,0:T(8,128)S(1)}, f32[8,4096]{1,0:T(8,128)S(1)}, u32[]{:S(2)}, u32[]{:S(2)}) collective-permute-start(f32[8,4096]{1,0:T(8,128)S(1)} %select_add_fusion), channel_id=1, source_target_pairs={{0,6},{1,7},{2,4},{3,5},{4,2},{5,3},{6,0},{7,1},{8,14},{9,15},{10,... | collective-permute-start | bytes 393224 | tf_op jit(solution)/shard_map/ppermute | solution.py:562
  91.8 5.1 %collective-permute-done.10 = f32[8,4096]{1,0:T(8,128)S(1)} collective-permute-done((f32[8,4096]{1,0:T(8,128)S(1)}, f32[8,4096]{1,0:T(8,128)S(1)}, u32[]{:S(2)}, u32[]{:S(2)}) %collective-permute-start.10) | collective-permute-done | bytes 131104 | tf_op jit(solution)/shard_map/ppermute | solution.py:562
  97.0 0.1 collective-permute-start.13
  97.1 0.1 pad_add_fusion.sc_ref
  97.2 1.5 %collective-permute-start.11 = (f32[8,4096]{1,0:T(8,128)S(1)}, f32[8,4096]{1,0:T(8,128)S(1)}, u32[]{:S(2)}, u32[]{:S(2)}) collective-permute-start(f32[8,4096]{1,0:T(8,128)S(1)} %fusion.5), channel_id=1, source_target_pairs={{0,1},{1,0},{2,3},{3,2},{4,5},{5,4},{6,7},{7,6},{8,9},{9,8},{10,11... | collective-permute-start | bytes 393224 | tf_op jit(solution)/shard_map/ppermute | solution.py:562
  98.7 2.0 %collective-permute-start.12 = (f32[8,4096]{1,0:T(8,128)S(1)}, f32[8,4096]{1,0:T(8,128)S(1)}, u32[]{:S(2)}, u32[]{:S(2)}) collective-permute-start(f32[8,4096]{1,0:T(8,128)S(1)} %fusion.5), channel_id=1, source_target_pairs={{0,3},{1,2},{2,1},{3,0},{4,7},{5,6},{6,5},{7,4},{8,11},{9,10},{10,... | collective-permute-start | bytes 393224 | tf_op jit(solution)/shard_map/ppermute | solution.py:562
  100.6 1.4 %collective-permute-done.13 = f32[8,4096]{1,0:T(8,128)S(1)} collective-permute-done((f32[8,4096]{1,0:T(8,128)S(1)}, f32[8,4096]{1,0:T(8,128)S(1)}, u32[]{:S(2)}, u32[]{:S(2)}) %collective-permute-start.13) | collective-permute-done | bytes 131104 | tf_op jit(solution)/shard_map/ppermute | solution.py:562
  102.1 0.1 collective-permute-done.11
  102.2 2.4 %collective-permute-done.12 = f32[8,4096]{1,0:T(8,128)S(1)} collective-permute-done((f32[8,4096]{1,0:T(8,128)S(1)}, f32[8,4096]{1,0:T(8,128)S(1)}, u32[]{:S(2)}, u32[]{:S(2)}) %collective-permute-start.12) | collective-permute-done | bytes 131104 | tf_op jit(solution)/shard_map/ppermute | solution.py:562
  104.6 1.5 %finish.1 = (f32[16,8192]{1,0:T(8,128)}, bf16[64,2,512,128]{3,2,1,0:T(8,128)(2,1)}) custom-call(s32[3]{0:T(128)S(1)} %pad_add_fusion.sc_ref, bf16[64,2,512,128]{3,2,1,0:T(8,128)(2,1)} %carry.7.old_ref, f32[16,4096]{1,0:T(8,128)S(1)} %pad_maximum_fusion.3.own_ref, f32[16,4096]{1,0:T(8,128)S(1)} %pad_maximum_fusion.4.other_ref), custom_call_target="tpu_custom_call", output_to_operand_aliasing={{1}: (1, {})} | custom-call | tf_op jit(solution)/shard_map/finish/pallas_call | solution.py:513
  (27 shorter events, 0.5 us)
Async XLA Ops:
  3.6 10.1 %collective-permute-start = (f32[128,128]{1,0:T(8,128)S(1)}, f32[128,128]{1,0:T(8,128)S(1)}, u32[]{:S(2)}, u32[]{:S(2)}) collective-permute-start(f32[128,128]{1,0:T(8,128)S(1)} %get-tuple-element.37), channel_id=1, source_target_pairs={{0,1},{1,0},{2,3},{3,2},{4,5},{5,4},{6,7},{7,6},{8,9},{9,8},{10,11... | collective-permute-start | bytes 196616 | tf_op jit(solution)/shard_map/ppermute | solution.py:562
  8.4 18.6 %copy-start = (bf16[128,128]{1,0:T(8,128)(2,1)S(1)}, bf16[128,128]{1,0:T(8,128)(2,1)}, u32[]{:S(2)}) copy-start(bf16[128,128]{1,0:T(8,128)(2,1)} %constant.61.clone.perm_ref) | copy-start | bytes 98308
  13.7 6.9 %collective-permute-start.1 = (f32[128,128]{1,0:T(8,128)S(1)}, f32[128,128]{1,0:T(8,128)S(1)}, u32[]{:S(2)}, u32[]{:S(2)}) collective-permute-start(f32[128,128]{1,0:T(8,128)S(1)} %add_select_fusion.2), channel_id=1, source_target_pairs={{0,2},{1,3},{2,0},{3,1},{4,6},{5,7},{6,4},{7,5},{8,10},{9,11},{10,... | collective-permute-start | bytes 196616 | tf_op jit(solution)/shard_map/ppermute | solution.py:562
  20.6 6.1 %collective-permute-start.2 = (f32[128,128]{1,0:T(8,128)S(1)}, f32[128,128]{1,0:T(8,128)S(1)}, u32[]{:S(2)}, u32[]{:S(2)}) collective-permute-start(f32[128,128]{1,0:T(8,128)S(1)} %add_select_fusion.1), channel_id=1, source_target_pairs={{0,6},{1,7},{2,4},{3,5},{4,2},{5,3},{6,0},{7,1},{8,14},{9,15},{10,... | collective-permute-start | bytes 196616 | tf_op jit(solution)/shard_map/ppermute | solution.py:562
  39.1 12.7 %collective-permute-start.3 = (f32[16,4096]{1,0:T(8,128)S(1)}, f32[16,4096]{1,0:T(8,128)S(1)}, u32[]{:S(2)}, u32[]{:S(2)}) collective-permute-start(f32[16,4096]{1,0:T(8,128)S(1)} %get-tuple-element.47), channel_id=1, source_target_pairs={{0,1},{1,0},{2,3},{3,2},{4,5},{5,4},{6,7},{7,6},{8,9},{9,8},{10,11... | collective-permute-start | bytes 786440 | tf_op jit(solution)/shard_map/ppermute | solution.py:562
  39.7 12.3 %copy-start.2 = (f32[2,8192]{1,0:T(2,128)S(1)}, f32[2,8192]{1,0:T(2,128)}, u32[]{:S(2)}) copy-start(f32[2,8192]{1,0:T(2,128)} %param.15) | copy-start | bytes 196612
  51.9 5.0 %collective-permute-start.4 = (f32[8,4096]{1,0:T(8,128)S(1)}, f32[8,4096]{1,0:T(8,128)S(1)}, u32[]{:S(2)}, u32[]{:S(2)}) collective-permute-start(f32[8,4096]{1,0:T(8,128)S(1)} %slice_select_fusion.3), channel_id=1, source_target_pairs={{0,2},{1,3},{2,0},{3,1},{4,6},{5,7},{6,4},{7,5},{8,10},{9,11},{10,... | collective-permute-start | bytes 393224 | tf_op jit(solution)/shard_map/ppermute | solution.py:562
  53.5 6.0 %copy-start.1 = (f32[16,8192]{1,0:T(8,128)S(1)}, f32[16,8192]{1,0:T(8,128)}, u32[]{:S(2)}) copy-start(f32[16,8192]{1,0:T(8,128)} %param.14) | copy-start | bytes 1572868
  57.0 7.0 %collective-permute-start.5 = (f32[8,4096]{1,0:T(8,128)S(1)}, f32[8,4096]{1,0:T(8,128)S(1)}, u32[]{:S(2)}, u32[]{:S(2)}) collective-permute-start(f32[8,4096]{1,0:T(8,128)S(1)} %select_add_fusion.1), channel_id=1, source_target_pairs={{0,6},{1,7},{2,4},{3,5},{4,2},{5,3},{6,0},{7,1},{8,14},{9,15},{10,... | collective-permute-start | bytes 393224 | tf_op jit(solution)/shard_map/ppermute | solution.py:562
  59.6 18.4 %slice-start = ((s8[8388608]{0:T(1024)(128)(4,1)}), s8[4194304]{0:T(1024)(128)(4,1)S(1)}, s32[]{:S(2)}) async-start(s8[8388608]{0:T(1024)(128)(4,1)} %bitcast.34), calls=%async_computation | async-start | bytes 8388608
  63.9 6.8 %slice-start.2 = ((s8[8388608]{0:T(1024)(128)(4,1)}), s8[4194304]{0:T(1024)(128)(4,1)S(1)}, s32[]{:S(2)}) async-start(s8[8388608]{0:T(1024)(128)(4,1)} %bitcast.36), calls=%async_computation.2 | async-start | bytes 8388608
  64.0 5.1 %collective-permute-start.6 = (f32[8,4096]{1,0:T(8,128)S(1)}, f32[8,4096]{1,0:T(8,128)S(1)}, u32[]{:S(2)}, u32[]{:S(2)}) collective-permute-start(f32[8,4096]{1,0:T(8,128)S(1)} %add.171), channel_id=1, source_target_pairs={{0,2},{1,3},{2,0},{3,1},{4,6},{5,7},{6,4},{7,5},{8,10},{9,11},{10,... | collective-permute-start | bytes 393224 | tf_op jit(solution)/shard_map/ppermute | solution.py:562
  65.5 5.3 %slice-start.3 = ((s8[8388608]{0:T(1024)(128)(4,1)}), s8[4194304]{0:T(1024)(128)(4,1)S(1)}, s32[]{:S(2)}) async-start(s8[8388608]{0:T(1024)(128)(4,1)} %bitcast.36), calls=%async_computation.3 | async-start | bytes 8388608
  65.5 12.5 %slice-start.1 = ((s8[8388608]{0:T(1024)(128)(4,1)}), s8[4194304]{0:T(1024)(128)(4,1)S(1)}, s32[]{:S(2)}) async-start(s8[8388608]{0:T(1024)(128)(4,1)} %bitcast.34), calls=%async_computation.1 | async-start | bytes 8388608
  69.1 8.8 %collective-permute-start.7 = (f32[16,4096]{1,0:T(8,128)S(1)}, f32[16,4096]{1,0:T(8,128)S(1)}, u32[]{:S(2)}, u32[]{:S(2)}) collective-permute-start(f32[16,4096]{1,0:T(8,128)S(1)} %pad_maximum_fusion.2.pred_ref), channel_id=1, source_target_pairs={{0,1},{1,0},{2,3},{3,2},{4,5},{5,4},{6,7},{7,6},{8,9},{9,8},{10,11... | collective-permute-start | bytes 786440 | tf_op jit(solution)/shard_map/ppermute | solution.py:562
  76.5 7.5 %collective-permute-start.8 = (f32[16,4096]{1,0:T(8,128)S(1)}, f32[16,4096]{1,0:T(8,128)S(1)}, u32[]{:S(2)}, u32[]{:S(2)}) collective-permute-start(f32[16,4096]{1,0:T(8,128)S(1)} %correct.3), channel_id=1, source_target_pairs={{0,1},{1,0},{2,3},{3,2},{4,5},{5,4},{6,7},{7,6},{8,9},{9,8},{10,11... | collective-permute-start | bytes 786440 | tf_op jit(solution)/shard_map/ppermute | solution.py:562
  84.1 5.0 %collective-permute-start.9 = (f32[8,4096]{1,0:T(8,128)S(1)}, f32[8,4096]{1,0:T(8,128)S(1)}, u32[]{:S(2)}, u32[]{:S(2)}) collective-permute-start(f32[8,4096]{1,0:T(8,128)S(1)} %slice_select_fusion.2), channel_id=1, source_target_pairs={{0,2},{1,3},{2,0},{3,1},{4,6},{5,7},{6,4},{7,5},{8,10},{9,11},{10,... | collective-permute-start | bytes 393224 | tf_op jit(solution)/shard_map/ppermute | solution.py:562
  89.1 7.8 %collective-permute-start.10 = (f32[8,4096]{1,0:T(8,128)S(1)}, f32[8,4096]{1,0:T(8,128)S(1)}, u32[]{:S(2)}, u32[]{:S(2)}) collective-permute-start(f32[8,4096]{1,0:T(8,128)S(1)} %select_add_fusion), channel_id=1, source_target_pairs={{0,6},{1,7},{2,4},{3,5},{4,2},{5,3},{6,0},{7,1},{8,14},{9,15},{10,... | collective-permute-start | bytes 393224 | tf_op jit(solution)/shard_map/ppermute | solution.py:562
  97.0 5.0 %collective-permute-start.13 = (f32[8,4096]{1,0:T(8,128)S(1)}, f32[8,4096]{1,0:T(8,128)S(1)}, u32[]{:S(2)}, u32[]{:S(2)}) collective-permute-start(f32[8,4096]{1,0:T(8,128)S(1)} %fusion.5), channel_id=1, source_target_pairs={{0,2},{1,3},{2,0},{3,1},{4,6},{5,7},{6,4},{7,5},{8,10},{9,11},{10,... | collective-permute-start | bytes 393224 | tf_op jit(solution)/shard_map/ppermute | solution.py:562
  97.2 5.0 %collective-permute-start.11 = (f32[8,4096]{1,0:T(8,128)S(1)}, f32[8,4096]{1,0:T(8,128)S(1)}, u32[]{:S(2)}, u32[]{:S(2)}) collective-permute-start(f32[8,4096]{1,0:T(8,128)S(1)} %fusion.5), channel_id=1, source_target_pairs={{0,1},{1,0},{2,3},{3,2},{4,5},{5,4},{6,7},{7,6},{8,9},{9,8},{10,11... | collective-permute-start | bytes 393224 | tf_op jit(solution)/shard_map/ppermute | solution.py:562
  98.7 5.9 %collective-permute-start.12 = (f32[8,4096]{1,0:T(8,128)S(1)}, f32[8,4096]{1,0:T(8,128)S(1)}, u32[]{:S(2)}, u32[]{:S(2)}) collective-permute-start(f32[8,4096]{1,0:T(8,128)S(1)} %fusion.5), channel_id=1, source_target_pairs={{0,3},{1,2},{2,1},{3,0},{4,7},{5,6},{6,5},{7,4},{8,11},{9,10},{10,... | collective-permute-start | bytes 393224 | tf_op jit(solution)/shard_map/ppermute | solution.py:562

commit v4 on v3

--- a/solution.py
+++ b/solution.py
@@ -31,12 +31,7 @@
     return z * c, 1.0 - z * z
 
 
-def half_angle_sincos(half):
-    return double_sincos(half - jnp.round(half * (1.0 / np.pi)) * np.pi)
-
-
-def sincos(angle):
-    half = 0.5 * angle
+def half_sincos(half):
     turns = jnp.round(half * (1.0 / np.pi))
     return double_sincos((half - turns * 3.140625) - turns * 9.67653589793e-4)
 
@@ -86,79 +81,17 @@
     )(jnp.reshape(edge, (1,)).astype(jnp.int32), view)
 
 
-def trig_kernel(side_ref, tri_ref, energy_ref, waves_ref, held, made, in_sems, out_sems):
-    columns = held.shape[-1]
-    chunk = min(CHUNK, columns)
-    count = columns // chunk
-
-    def copy_in(j, a):
-        there = pl.ds(pl.multiple_of(side_ref[0] * columns + j * chunk, chunk), chunk)
-        lanes = pl.ds(j * chunk, chunk)
-        return pltpu.make_async_copy(energy_ref.at[:, a, there], held.at[a, :, lanes], in_sems.at[j, a])
-
-    def copy_out(j):
-        lanes = pl.ds(j * chunk, chunk)
-        return pltpu.make_async_copy(made.at[:, :, :, lanes], waves_ref.at[:, :, :, lanes], out_sems.at[j])
-
-    for j in range(count):
-        for a in range(2):
-            copy_in(j, a).start()
-    for j in range(count):
-        for a in range(2):
-            copy_in(j, a).wait()
-        for n in range(chunk // WIDE):
-            lanes = slice(j * chunk + n * WIDE, j * chunk + (n + 1) * WIDE)
-            for a in range(2):
-                e = held[a, :, lanes]
-                top = e.astype(BF)
-                rest = e - top.astype(F32)
-                mid = rest.astype(BF)
-                low = (rest - mid.astype(F32)).astype(BF)
-                half = jnp.dot(
-                    tri_ref[...],
-                    jnp.concatenate([top, mid, low], axis=0),
-                    preferred_element_type=F32,
-                )
-                s, c = half_angle_sincos(half)
-                made[0, a, :, lanes] = c
-                made[1, a, :, lanes] = s
-        copy_out(j).start()
-    for j in range(count):
-        copy_out(j).wait()
-
-
-def trig(side, energy):
-    steps, columns = energy.shape[0], energy.shape[2] // 2
-    tri = 0.5 * np.triu(np.ones((steps, steps), np.float32))
-    tri = jnp.asarray(np.concatenate([tri] * 3, axis=1), BF)
-    count = columns // min(CHUNK, columns)
-    size = (2, 2, steps, columns)
-    return pl.pallas_call(
-        trig_kernel,
-        in_specs=[SM, VM, HB],
-        out_specs=HB,
-        out_shape=jax.ShapeDtypeStruct(size, F32),
-        scratch_shapes=[
-            pltpu.VMEM(size[1:], F32),
-            pltpu.VMEM(size, F32),
-            pltpu.SemaphoreType.DMA((count, 2)),
-            pltpu.SemaphoreType.DMA((count,)),
-        ],
-        compiler_params=pltpu.CompilerParams(vmem_limit_bytes=54 << 20),
-        cost_estimate=pl.CostEstimate(flops=20 * energy.size, bytes_accessed=6 * energy.size, transcendentals=0),
-        name="trig",
-    )(jnp.reshape(side, (1,)).astype(jnp.int32), tri, energy)
-
-
-def permutation(group):
-    rows = 16 * group
-    p = np.zeros((rows, rows), np.float32)
-    for tile in range(2):
-        for c in range(8):
-            for g in range(group // 8):
-                for s in range(8):
-                    p[((tile * 8 + c) * (group // 8) + g) * 8 + s, ((8 * g + s) * 2 + tile) * 8 + c] = 1
-    return jnp.asarray(p, BF)
+def suffix_rows(steps):
+    row = lax.broadcasted_iota(jnp.int32, (steps, 3 * steps), 0)
+    column = lax.rem(lax.broadcasted_iota(jnp.int32, (steps, 3 * steps), 1), steps)
+    return jnp.where(column >= row, 0.5, 0.0).astype(BF)
+
+
+def permutation():
+    rows = 16 * GROUP
+    row = lax.broadcasted_iota(jnp.int32, (rows, rows), 0)
+    column = lax.broadcasted_iota(jnp.int32, (rows, rows), 1)
+    return jnp.where(column == (row & (GROUP - 1)) * 16 + lax.div(row, GROUP), 1.0, 0.0).astype(BF)
 
 
 def kernel_rows(kernel):
@@ -170,8 +103,8 @@
     return jnp.concatenate([top, k - top], axis=1).astype(BF)
 
 
-def predict_kernel(inside, steps, group, sc_ref, perm_ref, k_ref, h_ref, waves_ref, off_ref, out_ref, *rest):
-    near_ref, far_ref, held, in_sems, waves, wave_sems, kept, out_sems = rest
+def predict_kernel(inside, steps, group, sc_ref, k_ref, h_ref, energy_ref, off_ref, out_ref, *rest):
+    near_ref, far_ref, held, in_sems, energies, energy_sems, halves, waves, kept, out_sems, perm_ref, tri_ref = rest
     columns = out_ref.shape[-1]
     chunk = kept.shape[-1]
     count = columns // chunk
@@ -190,28 +123,57 @@
             kept.at[j % 2], (near_ref if near else far_ref).at[:, there], out_sems.at[j % 2]
         )
 
+    def copy_energy(j, a):
+        there = pl.ds(pl.multiple_of(sc_ref[0] * columns + j * chunk, chunk), chunk)
+        here = pl.ds(pl.multiple_of(j * chunk, chunk), chunk)
+        return pltpu.make_async_copy(energy_ref.at[:, a, there], energies.at[a, :, here], energy_sems.at[j, a])
+
+    def copy_out(j, near):
+        there = pl.ds(pl.multiple_of((j if near else j - inside) * chunk, chunk), chunk)
+        return pltpu.make_async_copy(
+            kept.at[j % 2], (near_ref if near else far_ref).at[:, there], out_sems.at[j % 2]
+        )
+
     def copy_waves(j):
         lanes = pl.ds(pl.multiple_of(j * chunk, chunk), chunk)
         return pltpu.make_async_copy(waves_ref.at[:, :, :, lanes], waves.at[:, :, :, lanes], wave_sems.at[j])
 
     for j in range(count):
+        for a in range(2):
+            copy_energy(j, a).start()
         copy_in(j).start()
-        copy_waves(j).start()
 
     def spans(j, n):
         first = j * chunk + n * WIDE
         local = [pl.ds(pl.multiple_of(first + LANES * t, LANES), LANES) for t in range(4)]
         return local
 
-    def pair(part, a, s0, local, t):
-        rows = slice(s0, s0 + 8)
-        return jnp.concatenate([waves[part, a, rows, local[t]], waves[part, a, rows, local[t + 2]]], axis=-1)
-
-    def off_row(part, later_side, j, n, t, a):
-        row = 2 * ((sc_ref[0] * (columns // LANES)) + j * tiles + 4 * n + t) + a
-        return jnp.concatenate(
-            [off_ref[part, later_side, pl.ds(row, 1)], off_ref[part, later_side, pl.ds(row + 4, 1)]], axis=-1
-        )
+    def pair(n, part, a, s0, t):
+        both = [waves[n % 2, part, a, s0 : s0 + 8, LANES * m : LANES * (m + 1)] for m in (t, t + 2)]
+        return jnp.concatenate(both, axis=-1)
+
+    def sum_phases(first):
+        for a in range(2):
+            e = energies[a, :, pl.ds(pl.multiple_of(first, WIDE), WIDE)]
+            top = e.astype(BF)
+            rest = e - top.astype(F32)
+            mid = rest.astype(BF)
+            low = (rest - mid.astype(F32)).astype(BF)
+            parts = jnp.concatenate([top, mid, low], axis=0)
+            halves[a] = jnp.dot(tri_ref[...], parts, preferred_element_type=F32)
+
+    def make_waves(first, n, i):
+        after = lax.broadcasted_iota(jnp.int32, (group, WIDE), 0) + i * group > edge
+        tile = sc_ref[0] * (columns // LANES) + lax.div(first, LANES)
+        rows = slice(i * group, (i + 1) * group)
+        for a in range(2):
+            low, up = [
+                jnp.concatenate([off_ref[later, pl.ds(2 * (tile + t) + a, 1)] for t in range(4)], axis=-1)
+                for later in range(2)
+            ]
+            s, c = half_sincos(halves[a, rows] + jnp.where(after, up, low))
+            waves[n % 2, 0, a, rows] = c
+            waves[n % 2, 1, a, rows] = s
 
     def move(j, n, i):
         row = pl.multiple_of(j * tiles * 8 + n * 32, 16)
@@ -226,16 +188,9 @@
             moved.append(jnp.dot(perm_ref[...], jnp.concatenate(h, axis=1), preferred_element_type=F32))
         return moved
 
-    def turned_rows(local, i, t, g, moved, turn):
+    def turned_rows(n, i, t, g, moved):
         s0 = i * group + 8 * g
-        after = lax.broadcasted_iota(jnp.int32, (8, 2 * LANES), 0) + s0 > edge
-        angle = []
-        for a in range(2):
-            c = pair(0, a, s0, local, t)
-            s = pair(1, a, s0, local, t)
-            co = jnp.where(after, turn[t][1][a], turn[t][0][a])
-            so = jnp.where(after, turn[2 + t][1][a], turn[2 + t][0][a])
-            angle.append((c * co - s * so, s * co + c * so))
+        angle = [[pair(n, part, a, s0, t) for part in range(2)] for a in range(2)]
         real, imag = [], []
         for e in range(8):
             c, s = angle[(e >> 1) & 1]
@@ -268,21 +223,18 @@
         moved = move(j, *items[0])
         waiting = None
         for at, (n, i) in enumerate(items):
+            later = move(j, *items[at + 1]) if at + 1 < len(items) else None
             if waiting is not None:
                 contract(*waiting)
-            later = move(j, *items[at + 1]) if at + 1 < len(items) else None
-            local = spans(j, n)
+            following = jnp.minimum(j * chunk + (n + 1) * WIDE, columns - WIDE)
             if i == 0:
-                turn = [
-                    [[off_row(part, later_side, j, n, t, a) for a in range(2)] for later_side in range(2)]
-                    for part in range(2)
-                    for t in range(2)
-                ]
+                sum_phases(following)
+            make_waves(following, n + 1, i)
             ready = []
             rows = slice(i * 16 * group, (i + 1) * 16 * group)
             for t in range(2):
                 x = jnp.concatenate(
-                    [row for g in range(blocks) for row in turned_rows(local, i, t, g, moved, turn)], axis=0
+                    [row for g in range(blocks) for row in turned_rows(n, i, t, g, moved)], axis=0
                 )
                 kept[buf, rows, n * WIDE + t * LANES : n * WIDE + (t + 1) * LANES] = x[:, :LANES]
                 kept[buf, rows, n * WIDE + (t + 2) * LANES : n * WIDE + (t + 3) * LANES] = x[:, LANES:]
@@ -296,7 +248,11 @@
         @pl.loop(first, last)
         def _(j):
             copy_in(j).wait()
-            copy_waves(j).wait()
+
+            @pl.when(j + 1 < count)
+            def _():
+                for a in range(2):
+                    copy_energy(j + 1, a).wait()
 
             @pl.when(j >= 2)
             def _():
@@ -305,15 +261,21 @@
             work(j)
             copy_out(j, near).start()
 
+    perm_ref[...] = permutation()
+    tri_ref[...] = suffix_rows(steps)
+    for a in range(2):
+        copy_energy(0, a).wait()
+    sum_phases(0)
+    for i in range(steps // group):
+        make_waves(0, 0, i)
     span(0, inside, True)
     span(inside, count, False)
     for j in range(max(count - 2, 0), count):
         copy_out(j, j < inside).wait()
 
 
-def predict(side, edge, weights, stored, waves, off):
-    steps = waves.shape[2]
-    columns = waves.shape[3]
+def predict(side, edge, weights, stored, energy, off):
+    steps, columns = energy.shape[0], energy.shape[2] // 2
     group = GROUP
     chunk = min(CHUNK, columns)
     count = columns // chunk
@@ -321,22 +283,32 @@
     size = steps * 16 * columns
     return pl.pallas_call(
         functools.partial(predict_kernel, inside, steps, group),
-        in_specs=[SM, VM, VM, HB, HB, VM],
+        in_specs=[SM, VM, HB, HB, VM],
         out_specs=[VM, HB, HB],
         out_shape=[jax.ShapeDtypeStruct((16, columns), F32)]
         + [jax.ShapeDtypeStruct((steps * 16, c), F32) for c in (inside * chunk, columns - inside * chunk)],
         scratch_shapes=[
             pltpu.VMEM((steps, 2, columns // 16, LANES), BF),
             pltpu.SemaphoreType.DMA((count,)),
-            pltpu.VMEM((2, 2, steps, columns), F32),
-            pltpu.SemaphoreType.DMA((count,)),
+            pltpu.VMEM((2, steps, columns), F32),
+            pltpu.SemaphoreType.DMA((count, 2)),
+            pltpu.VMEM((2, steps, WIDE), F32),
+            pltpu.VMEM((2, 2, 2, steps, WIDE), F32),
             pltpu.VMEM((2, steps * 16, chunk), F32),
             pltpu.SemaphoreType.DMA((2,)),
+            pltpu.VMEM((16 * group, 16 * group), BF),
+            pltpu.VMEM((steps, 3 * steps), BF),
         ],
         compiler_params=pltpu.CompilerParams(vmem_limit_bytes=51 << 20),
         cost_estimate=pl.CostEstimate(flops=200 * size, bytes_accessed=6 * size, transcendentals=0),
         name="predict",
-    )(jnp.stack([side, edge]).astype(jnp.int32), permutation(group), weights, stored, waves, off)
+    )(
+        jnp.stack([side, edge]).astype(jnp.int32),
+        weights,
+        stored,
+        energy,
+        off,
+    )
 
 
 def correct_kernel(inside, steps, group, sc_ref, k_ref, start_ref, pred_ref, *rest):
@@ -540,8 +512,8 @@
 
 def rotate(values, angles):
     columns = angles.shape[-1]
-    spread = jnp.broadcast_to(angles[None, :, None, :], (2, 2, 2, columns)).reshape(8, columns)
-    c, s = jnp.cos(spread), jnp.sin(spread)
+    waves = half_sincos(0.5 * angles)
+    s, c = [jnp.broadcast_to(x[None, :, None, :], (2, 2, 2, columns)).reshape(8, columns) for x in waves]
     real, imag = values[:8], values[8:]
     return jnp.concatenate([c * real + s * imag, c * imag - s * real], axis=0)
 
@@ -568,64 +540,61 @@
     value, late = totals(edge, energy)
 
     total, ahead = value, jnp.zeros_like(value)
-    waves = []
-    for t in range(bits):
-        mask = 6 if t == 2 else 1 << t
-        if t < 2:
-            total, seen = lax.optimization_barrier((total, energy))
-            got, made = lax.optimization_barrier((swap(total, mask), trig((other, side)[t], seen)))
-            waves.append(made)
-        else:
-            got = swap(total, mask)
-        here, there = place_here >> t, owner >> t
-        upper = (here & 1) == 1
-        partner = here ^ 1
-        counted_low = ~((there == here) & (place_here < owner))
-        counted_high = (there == partner) | ((there == here) & (place_here >= owner))
-        ahead = ahead + jnp.where(jnp.where(upper, counted_high, counted_low), got, 0.0)
-        low_group = jnp.where(upper, partner, here)
-        total = jnp.where(there == low_group, jnp.where(upper, got, total), total + got)
-    off = jnp.stack([jnp.where(mine, -late, ahead), jnp.where(mine, ahead + value, ahead)])
-    off_sin, off_cos = sincos(off)
-    off = jnp.stack([off_cos, off_sin])
-
-    while len(waves) < 2:
-        waves.append(trig((other, side)[len(waves)], energy))
-    weights = kernel_rows(kernel)
+
     stored = tiled(history)
-    start = rotate(current, step_energy)
-
     new = None
     piece = 0
 
-    def swap_beside(x, mask):
+    def swaps_beside(sent, masks_):
         nonlocal new, piece
         if piece == pieces_of(steps):
-            return swap(x, mask)
-        x, here = lax.optimization_barrier((x, stored))
-        got = swap(x, mask)
+            return [swap(x, mask) for x, mask in zip(sent, masks_)]
+        sent, here = lax.optimization_barrier((sent, stored))
+        got = [swap(x, mask) for x, mask in zip(sent, masks_)]
         got, new = lax.optimization_barrier((got, carry(piece, here, new)))
         piece += 1
         return got
 
+    def counted(t, partner):
+        here, there = place_here >> t, owner >> t
+        beyond, within = partner > here, partner <= there
+        between = jnp.where(here < there, beyond & within, beyond | within)
+        return jnp.where(here == there, place_here >= owner, between)
+
+    direct = bits == 3
+    for t in range(1 if direct else bits):
+        here, there = place_here >> t, owner >> t
+        upper, partner = (here & 1) == 1, here ^ 1
+        got = swap(total, 6 if t == 2 else 1 << t)
+        ahead = ahead + jnp.where(counted(t, partner), got, 0.0)
+        low_group = jnp.where(upper, partner, here)
+        total = jnp.where(there == low_group, jnp.where(upper, got, total), total + got)
+    if direct:
+        for mask, got in zip((2, 4, 6), swaps_beside([total] * 3, (2, 4, 6))):
+            ahead = ahead + jnp.where(counted(1, (place_here ^ mask) >> 1), got, 0.0)
+    start = rotate(current, step_energy)
+    off = 0.5 * jnp.stack([jnp.where(mine, -late, ahead), jnp.where(mine, ahead + value, ahead)])
+    weights = kernel_rows(kernel)
+
     first = split == 0
 
-    def inner_part(x):
+    def inner_part(x, carried):
         keep = jnp.where(first, x[:8], x[8:])
         send = jnp.where(first, x[8:], x[:8])
-        keep = keep + swap_beside(send, masks[0])
-        for mask in masks[1:]:
-            keep = keep + swap_beside(keep, mask)
+        for n, mask in enumerate(masks):
+            sent = keep if n else send
+            (got,) = swaps_beside([sent], [mask]) if carried[min(n, 1)] else [swap(sent, mask)]
+            keep = keep + got
         return keep
 
     def joined(keep, rest):
         return jnp.concatenate([jnp.where(first, keep, rest), jnp.where(first, rest, keep)], axis=0)
 
-    part_other, *turned_other = predict(other, edge, weights, stored, waves[0], off)
+    part_other, *turned_other = predict(other, edge, weights, stored, energy, off)
     from_partner = swap(part_other, 1)
-    part_own, *turned_own = predict(side, edge, weights, stored, waves[1], off)
-    pred_own = inner_part(part_own + from_partner)
-    pred_own = joined(pred_own, swap_beside(pred_own, masks[0]))
+    part_own, *turned_own = predict(side, edge, weights, stored, energy, off)
+    pred_own = inner_part(part_own + from_partner, (False, True))
+    pred_own = joined(pred_own, swap(pred_own, masks[0]))
     pred_other = swap(pred_own, 1)
     corr_own = correct(side, weights, start, pred_own, *turned_own)
     from_partner = swap(corr_own, 1)
@@ -634,7 +603,7 @@
         x = jnp.where(side == 0, x[:, half:], x[:, :half]) if x.shape[1] > half else x
         return jnp.where(first, x[:8], x[8:])
 
-    corr = inner_part(corr_other + from_partner)
+    corr = inner_part(corr_other + from_partner, (True, True))
     fresh = mine_of(start) + 0.5 * (mine_of(pred_other) + corr)
     gathered = [swap(fresh, mask) for mask in (masks[0], masks[0] ^ 1, 1)]
     new_other = joined(fresh, gathered[0])

time: 107 us -> 101 us (0.944)
  Pallas kernels: 64.2 us -> 54 us
  waiting for transfers between devices: 14 us -> 22.6 us
  starting transfers between devices: 22.2 us -> 19.3 us
    pallas_call x2 -> x0, Pallas kernels: 10.5 us -> none  [trig(): pl.pallas_call(trig_kernel, in_specs=[SM, VM, HB], out_specs=HB, out_shap...]
    ppermute x14 -> x15, waiting for transfers between devices: 14 us -> 22.6 us  [swap(): return lax.ppermute(x, 'ta', [(i, i ^ mask) for i in range(count)])]
    ppermute x14 -> x15, starting transfers between devices: 22.2 us -> 19.3 us  [swap(): return lax.ppermute(x, 'ta', [(i, i ^ mask) for i in range(count)])]
    cos x2 -> x0, local copies, waits for them, and re-layouts: 1.15 us -> none  [rotate(): c, s = (jnp.cos(spread), jnp.sin(spread))]
  transfers between devices with their start and end apart: 14 -> 15, of which waited for: 8 -> 12; matrix products, arithmetic and copies ran while one was open for 3% -> 3% of each run, Pallas kernels for 45% -> 37%
where the time goes in v4:
time: 101 us
  Pallas kernels  54 us (53%)
  waiting for transfers between devices  22.6 us (22%)
  starting transfers between devices  19.3 us (19%)
  local copies, waits for them, and re-layouts  2.09 us (2%)
  between operations  1.83 us (2%)
    pallas_call x2, Pallas kernels, predict(): pl.pallas_call(functools.partial(predict_kernel, inside, steps, group), i...  25.1 us
    ppermute x15, waiting for transfers between devices, swap(): return lax.ppermute(x, 'ta', [(i, i ^ mask) for i in range(count)])  22.6 us
    ppermute x15, starting transfers between devices, swap(): return lax.ppermute(x, 'ta', [(i, i ^ mask) for i in range(count)])  19.3 us
    pallas_call x4, Pallas kernels, carry(): pl.pallas_call(functools.partial(carry_kernel, piece), in_specs=[HB] * le...  13.5 us
    pallas_call x2, Pallas kernels, correct(): pl.pallas_call(functools.partial(correct_kernel, inside, steps, group), i...  11.7 us
    pallas_call x1, Pallas kernels, totals(): pl.pallas_call(totals_kernel, in_specs=[SM, HB], out_specs=[VM, VM], out_...  2.33 us
  transfers between devices with their start and end apart: 15, of which 12 were waited for; matrix products, arithmetic and copies ran while one was open for 3% of the time, Pallas kernels for 37%

profile of v4, /device:TPU:0, one launch (start us, length us, event | category | flops | bytes accessed | tf_op | source)
XLA Modules:
  0.0 100.7 jit_solution(16076508586766487717)
XLA Ops:
  1.3 2.3 %totals.1 = (f32[128,128]{1,0:T(8,128)S(1)}, f32[128,128]{1,0:T(8,128)S(1)}) custom-call(s32[1]{0:T(128)} %bitcast.8.edge_ref, f32[64,128,128]{2,1,0:T(8,128)} %bitcast.45), custom_call_target="tpu_custom_call" | custom-call | flops 4194304 | bytes 4194304 | tf_op jit(solution)/shard_map/totals/pallas_call | solution.py:72
  3.6 3.0 %collective-permute-start = (f32[128,128]{1,0:T(8,128)S(1)}, f32[128,128]{1,0:T(8,128)S(1)}, u32[]{:S(2)}, u32[]{:S(2)}) collective-permute-start(f32[128,128]{1,0:T(8,128)S(1)} %get-tuple-element.33), channel_id=1, source_target_pairs={{0,1},{1,0},{2,3},{3,2},{4,5},{5,4},{6,7},{7,6},{8,9},{9,8},{10,11... | collective-permute-start | bytes 196616 | tf_op jit(solution)/shard_map/ppermute | solution.py:534
  6.7 1.2 %copy.14 = f32[64,16,16]{2,1,0:T(8,128)S(1)} copy(f32[64,16,16]{0,2,1:T(8,128)} %param.8) | data formatting | bytes 131072 | tf_op args[2]
  7.8 0.2 copy.15
  8.1 0.2 copy.16
  8.3 0.6 collective-permute-done
  8.9 2.1 %collective-permute-start.1 = (f32[128,128]{1,0:T(8,128)S(1)}, f32[128,128]{1,0:T(8,128)S(1)}, u32[]{:S(2)}, u32[]{:S(2)}) collective-permute-start(f32[128,128]{1,0:T(8,128)S(1)} %add_select_fusion.1), channel_id=1, source_target_pairs={{0,2},{1,3},{2,0},{3,1},{4,6},{5,7},{6,4},{7,5},{8,10},{9,11},{10,... | collective-permute-start | bytes 196616 | tf_op jit(solution)/shard_map/ppermute | solution.py:534
  11.1 2.6 %collective-permute-start.2 = (f32[128,128]{1,0:T(8,128)S(1)}, f32[128,128]{1,0:T(8,128)S(1)}, u32[]{:S(2)}, u32[]{:S(2)}) collective-permute-start(f32[128,128]{1,0:T(8,128)S(1)} %add_select_fusion.1), channel_id=1, source_target_pairs={{0,4},{1,5},{2,6},{3,7},{4,0},{5,1},{6,2},{7,3},{8,12},{9,13},{10,... | collective-permute-start | bytes 196616 | tf_op jit(solution)/shard_map/ppermute | solution.py:534
  13.6 0.0 collective-permute-start.3
  13.6 0.1 pad_add_fusion.1
  13.7 3.3 %carry.4.rest_0_ = bf16[64,2,512,128]{3,2,1,0:T(8,128)(2,1)} custom-call(bf16[64,2,512,128]{3,2,1,0:T(8,128)(2,1)} %bitcast.38), custom_call_target="tpu_custom_call" | custom-call | bytes 8388608 | tf_op jit(solution)/shard_map/carry/pallas_call | solution.py:437
  17.0 0.0 collective-permute-done.1
  17.0 0.6 collective-permute-done.2
  17.6 2.1 %collective-permute-done.3 = f32[128,128]{1,0:T(8,128)S(1)} collective-permute-done((f32[128,128]{1,0:T(8,128)S(1)}, f32[128,128]{1,0:T(8,128)S(1)}, u32[]{:S(2)}, u32[]{:S(2)}) %collective-permute-start.3) | collective-permute-done | bytes 65568 | tf_op jit(solution)/shard_map/ppermute | solution.py:534
  19.8 0.0 copy-start.1
  19.8 12.5 %predict.3 = (f32[16,4096]{1,0:T(8,128)S(1)}, f32[1024,2048]{1,0:T(8,128)}, f32[1024,2048]{1,0:T(8,128)}) custom-call(s32[2]{0:T(128)S(1)} %get-tuple-element.77.sc_ref, bf16[8,32,128]{2,1,0:T(8,128)(2,1)S(1)} %pad_maximum_fusion.4.k_ref, bf16[64,2,512,128]{3,2,1,0:T(8,128)(2,1)} %bitcast.39, f32[64,2,8192]{2,1,0:T(2,128)} %energy_ref.3, ...), custom_call_target="tpu_custom_call" | custom-call | flops 838860800 | bytes 25165824 | tf_op jit(solution)/shard_map/predict/pallas_call | solution.py:284
  32.3 0.0 copy-start
  32.4 1.6 %collective-permute-start.4 = (f32[16,4096]{1,0:T(8,128)S(1)}, f32[16,4096]{1,0:T(8,128)S(1)}, u32[]{:S(2)}, u32[]{:S(2)}) collective-permute-start(f32[16,4096]{1,0:T(8,128)S(1)} %get-tuple-element.42), channel_id=1, source_target_pairs={{0,1},{1,0},{2,3},{3,2},{4,5},{5,4},{6,7},{7,6},{8,9},{9,8},{10,11... | collective-permute-start | bytes 786440 | tf_op jit(solution)/shard_map/ppermute | solution.py:534
  33.9 12.5 %predict.2 = (f32[16,4096]{1,0:T(8,128)S(1)}, f32[1024,2048]{1,0:T(8,128)}, f32[1024,2048]{1,0:T(8,128)}) custom-call(s32[2]{0:T(128)S(1)} %get-tuple-element.76.sc_ref, bf16[8,32,128]{2,1,0:T(8,128)(2,1)S(1)} %pad_maximum_fusion.4.k_ref, bf16[64,2,512,128]{3,2,1,0:T(8,128)(2,1)} %bitcast.40, f32[64,2,8192]{2,1,0:T(2,128)} %energy_ref.3, ...), custom_call_target="tpu_custom_call" | custom-call | flops 838860800 | bytes 25165824 | tf_op jit(solution)/shard_map/predict/pallas_call | solution.py:284
  46.5 0.0 collective-permute-done.4
  46.6 0.1 collective-permute-start.5
  46.6 0.0 copy-done.1
  46.7 0.2 multiply_subtract_fusion.1
  46.9 0.1 broadcast_in_dim.19
  47.0 0.2 reshape.44
  47.2 0.1 broadcast_in_dim.20
  47.2 0.2 reshape.45
  47.4 4.2 %collective-permute-done.5 = f32[8,4096]{1,0:T(8,128)S(1)} collective-permute-done((f32[8,4096]{1,0:T(8,128)S(1)}, f32[8,4096]{1,0:T(8,128)S(1)}, u32[]{:S(2)}, u32[]{:S(2)}) %collective-permute-start.5) | collective-permute-done | bytes 131104 | tf_op jit(solution)/shard_map/ppermute | solution.py:534
  51.6 1.2 %collective-permute-start.6 = (f32[8,4096]{1,0:T(8,128)S(1)}, f32[8,4096]{1,0:T(8,128)S(1)}, u32[]{:S(2)}, u32[]{:S(2)}) collective-permute-start(f32[8,4096]{1,0:T(8,128)S(1)} %select_add_fusion.1), channel_id=1, source_target_pairs={{0,6},{1,7},{2,4},{3,5},{4,2},{5,3},{6,0},{7,1},{8,14},{9,15},{10,... | collective-permute-start | bytes 393224 | tf_op jit(solution)/shard_map/ppermute | solution.py:534
  52.9 0.0 copy-done
  52.9 0.0 slice-start.2
  52.9 0.1 multiply_add_fusion
  52.9 0.0 slice-start.3
  53.0 3.6 %carry.5.rest_0_ = bf16[64,2,512,128]{3,2,1,0:T(8,128)(2,1)} custom-call(bf16[64,2,512,128]{3,2,1,0:T(8,128)(2,1)} %bitcast.41, bf16[64,2,512,128]{3,2,1,0:T(8,128)(2,1)} %carry.4.rest_0_), custom_call_target="tpu_custom_call", output_to_operand_aliasing={{}: (1, {})} | custom-call | bytes 8388608 | tf_op jit(solution)/shard_map/carry/pallas_call | solution.py:437
  56.5 0.0 slice-start
  56.6 2.2 %collective-permute-done.6 = f32[8,4096]{1,0:T(8,128)S(1)} collective-permute-done((f32[8,4096]{1,0:T(8,128)S(1)}, f32[8,4096]{1,0:T(8,128)S(1)}, u32[]{:S(2)}, u32[]{:S(2)}) %collective-permute-start.6) | collective-permute-done | bytes 131104 | tf_op jit(solution)/shard_map/ppermute | solution.py:534
  58.8 0.1 collective-permute-start.7
  58.9 4.9 %collective-permute-done.7 = f32[8,4096]{1,0:T(8,128)S(1)} collective-permute-done((f32[8,4096]{1,0:T(8,128)S(1)}, f32[8,4096]{1,0:T(8,128)S(1)}, u32[]{:S(2)}, u32[]{:S(2)}) %collective-permute-start.7) | collective-permute-done | bytes 131104 | tf_op jit(solution)/shard_map/ppermute | solution.py:534
  63.9 0.6 collective-permute-start.8
  64.4 0.0 slice-done.2
  64.4 0.0 slice-done.3
  64.4 0.0 slice-start.1
  64.4 5.8 %correct.3 = f32[16,4096]{1,0:T(8,128)S(1)} custom-call(s32[1]{0:T(128)} %bitcast.sc_ref, bf16[8,32,128]{2,1,0:T(8,128)(2,1)S(1)} %pad_maximum_fusion.4.k_ref, f32[16,8192]{1,0:T(8,128)S(1)} %pad_maximum_fusion.start_ref, f32[16,4096]{1,0:T(8,128)S(1)} %pad_maximum_fusion.1.pred_ref, f32[1024,2048]{1,0:T(8,128)S(1)} %bitcast.37, ...), custom_call_target="tpu_custom_call" | custom-call | flops 503316480 | bytes 16777216 | tf_op jit(solution)/shard_map/correct/pallas_call | solution.py:391
  70.2 1.6 %collective-permute-start.9 = (f32[16,4096]{1,0:T(8,128)S(1)}, f32[16,4096]{1,0:T(8,128)S(1)}, u32[]{:S(2)}, u32[]{:S(2)}) collective-permute-start(f32[16,4096]{1,0:T(8,128)S(1)} %correct.3), channel_id=1, source_target_pairs={{0,1},{1,0},{2,3},{3,2},{4,5},{5,4},{6,7},{7,6},{8,9},{9,8},{10,11... | collective-permute-start | bytes 786440 | tf_op jit(solution)/shard_map/ppermute | solution.py:534
  71.8 0.3 collective-permute-done.8.pred_ref
  72.1 0.0 slice-done
  72.1 0.0 slice-done.1
  72.1 5.9 %correct.2 = f32[16,4096]{1,0:T(8,128)S(1)} custom-call(s32[1]{0:T(128)} %bitcast.4.sc_ref, bf16[8,32,128]{2,1,0:T(8,128)(2,1)S(1)} %pad_maximum_fusion.4.k_ref, f32[16,8192]{1,0:T(8,128)S(1)} %pad_maximum_fusion.start_ref, f32[16,4096]{1,0:T(8,128)S(1)} %collective-permute-done.8.pred_ref, f32[1024,2048]{1,0:T(8,128)S(1)} %bitcast.35, ...), custom_call_target="tpu_custom_call" | custom-call | flops 503316480 | bytes 16777216 | tf_op jit(solution)/shard_map/correct/pallas_call | solution.py:391
  78.0 0.0 collective-permute-done.9
  78.1 1.1 %collective-permute-start.10 = (f32[8,4096]{1,0:T(8,128)S(1)}, f32[8,4096]{1,0:T(8,128)S(1)}, u32[]{:S(2)}, u32[]{:S(2)}) collective-permute-start(f32[8,4096]{1,0:T(8,128)S(1)} %slice_select_fusion.2), channel_id=1, source_target_pairs={{0,2},{1,3},{2,0},{3,1},{4,6},{5,7},{6,4},{7,5},{8,10},{9,11},{10,... | collective-permute-start | bytes 393224 | tf_op jit(solution)/shard_map/ppermute | solution.py:534
  79.2 3.3 %carry.6.rest_0_ = bf16[64,2,512,128]{3,2,1,0:T(8,128)(2,1)} custom-call(bf16[64,2,512,128]{3,2,1,0:T(8,128)(2,1)} %bitcast.42, bf16[64,2,512,128]{3,2,1,0:T(8,128)(2,1)} %carry.5.rest_0_), custom_call_target="tpu_custom_call", output_to_operand_aliasing={{}: (1, {})} | custom-call | bytes 8388608 | tf_op jit(solution)/shard_map/carry/pallas_call | solution.py:437
  82.5 1.1 %collective-permute-done.10 = f32[8,4096]{1,0:T(8,128)S(1)} collective-permute-done((f32[8,4096]{1,0:T(8,128)S(1)}, f32[8,4096]{1,0:T(8,128)S(1)}, u32[]{:S(2)}, u32[]{:S(2)}) %collective-permute-start.10) | collective-permute-done | bytes 131104 | tf_op jit(solution)/shard_map/ppermute | solution.py:534
  83.6 1.8 %collective-permute-start.11 = (f32[8,4096]{1,0:T(8,128)S(1)}, f32[8,4096]{1,0:T(8,128)S(1)}, u32[]{:S(2)}, u32[]{:S(2)}) collective-permute-start(f32[8,4096]{1,0:T(8,128)S(1)} %select_add_fusion), channel_id=1, source_target_pairs={{0,6},{1,7},{2,4},{3,5},{4,2},{5,3},{6,0},{7,1},{8,14},{9,15},{10,... | collective-permute-start | bytes 393224 | tf_op jit(solution)/shard_map/ppermute | solution.py:534
  85.4 3.3 %carry.7.old_ref = bf16[64,2,512,128]{3,2,1,0:T(8,128)(2,1)} custom-call(bf16[64,2,512,128]{3,2,1,0:T(8,128)(2,1)} %bitcast.43, bf16[64,2,512,128]{3,2,1,0:T(8,128)(2,1)} %carry.6.rest_0_), custom_call_target="tpu_custom_call", output_to_operand_aliasing={{}: (1, {})} | custom-call | bytes 8388608 | tf_op jit(solution)/shard_map/carry/pallas_call | solution.py:437
  88.8 2.6 %collective-permute-done.11 = f32[8,4096]{1,0:T(8,128)S(1)} collective-permute-done((f32[8,4096]{1,0:T(8,128)S(1)}, f32[8,4096]{1,0:T(8,128)S(1)}, u32[]{:S(2)}, u32[]{:S(2)}) %collective-permute-start.11) | collective-permute-done | bytes 131104 | tf_op jit(solution)/shard_map/ppermute | solution.py:534
  91.4 0.1 fusion.5
  91.4 0.1 collective-permute-start.14
  91.5 0.1 pad_add_fusion.sc_ref
  91.6 1.7 %collective-permute-start.12 = (f32[8,4096]{1,0:T(8,128)S(1)}, f32[8,4096]{1,0:T(8,128)S(1)}, u32[]{:S(2)}, u32[]{:S(2)}) collective-permute-start(f32[8,4096]{1,0:T(8,128)S(1)} %fusion.5), channel_id=1, source_target_pairs={{0,1},{1,0},{2,3},{3,2},{4,5},{5,4},{6,7},{7,6},{8,9},{9,8},{10,11... | collective-permute-start | bytes 393224 | tf_op jit(solution)/shard_map/ppermute | solution.py:534
  93.3 1.8 %collective-permute-start.13 = (f32[8,4096]{1,0:T(8,128)S(1)}, f32[8,4096]{1,0:T(8,128)S(1)}, u32[]{:S(2)}, u32[]{:S(2)}) collective-permute-start(f32[8,4096]{1,0:T(8,128)S(1)} %fusion.5), channel_id=1, source_target_pairs={{0,3},{1,2},{2,1},{3,0},{4,7},{5,6},{6,5},{7,4},{8,11},{9,10},{10,... | collective-permute-start | bytes 393224 | tf_op jit(solution)/shard_map/ppermute | solution.py:534
  95.1 1.4 %collective-permute-done.14 = f32[8,4096]{1,0:T(8,128)S(1)} collective-permute-done((f32[8,4096]{1,0:T(8,128)S(1)}, f32[8,4096]{1,0:T(8,128)S(1)}, u32[]{:S(2)}, u32[]{:S(2)}) %collective-permute-start.14) | collective-permute-done | bytes 131104 | tf_op jit(solution)/shard_map/ppermute | solution.py:534
  96.5 0.1 collective-permute-done.12
  96.6 2.6 %collective-permute-done.13 = f32[8,4096]{1,0:T(8,128)S(1)} collective-permute-done((f32[8,4096]{1,0:T(8,128)S(1)}, f32[8,4096]{1,0:T(8,128)S(1)}, u32[]{:S(2)}, u32[]{:S(2)}) %collective-permute-start.13) | collective-permute-done | bytes 131104 | tf_op jit(solution)/shard_map/ppermute | solution.py:534
  99.2 1.4 %finish.1 = (f32[16,8192]{1,0:T(8,128)}, bf16[64,2,512,128]{3,2,1,0:T(8,128)(2,1)}) custom-call(s32[3]{0:T(128)S(1)} %pad_add_fusion.sc_ref, bf16[64,2,512,128]{3,2,1,0:T(8,128)(2,1)} %carry.7.old_ref, f32[16,4096]{1,0:T(8,128)S(1)} %pad_maximum_fusion.2.own_ref, f32[16,4096]{1,0:T(8,128)S(1)} %pad_maximum_fusion.3.other_ref), custom_call_target="tpu_custom_call", output_to_operand_aliasing={{1}: (1, {})} | custom-call | tf_op jit(solution)/shard_map/finish/pallas_call | solution.py:485
  (23 shorter events, 0.4 us)
Async XLA Ops:
  3.6 5.3 %collective-permute-start = (f32[128,128]{1,0:T(8,128)S(1)}, f32[128,128]{1,0:T(8,128)S(1)}, u32[]{:S(2)}, u32[]{:S(2)}) collective-permute-start(f32[128,128]{1,0:T(8,128)S(1)} %get-tuple-element.33), channel_id=1, source_target_pairs={{0,1},{1,0},{2,3},{3,2},{4,5},{5,4},{6,7},{7,6},{8,9},{9,8},{10,11... | collective-permute-start | bytes 196616 | tf_op jit(solution)/shard_map/ppermute | solution.py:534
  8.9 8.1 %collective-permute-start.1 = (f32[128,128]{1,0:T(8,128)S(1)}, f32[128,128]{1,0:T(8,128)S(1)}, u32[]{:S(2)}, u32[]{:S(2)}) collective-permute-start(f32[128,128]{1,0:T(8,128)S(1)} %add_select_fusion.1), channel_id=1, source_target_pairs={{0,2},{1,3},{2,0},{3,1},{4,6},{5,7},{6,4},{7,5},{8,10},{9,11},{10,... | collective-permute-start | bytes 196616 | tf_op jit(solution)/shard_map/ppermute | solution.py:534
  11.1 6.6 %collective-permute-start.2 = (f32[128,128]{1,0:T(8,128)S(1)}, f32[128,128]{1,0:T(8,128)S(1)}, u32[]{:S(2)}, u32[]{:S(2)}) collective-permute-start(f32[128,128]{1,0:T(8,128)S(1)} %add_select_fusion.1), channel_id=1, source_target_pairs={{0,4},{1,5},{2,6},{3,7},{4,0},{5,1},{6,2},{7,3},{8,12},{9,13},{10,... | collective-permute-start | bytes 196616 | tf_op jit(solution)/shard_map/ppermute | solution.py:534
  13.6 6.1 %collective-permute-start.3 = (f32[128,128]{1,0:T(8,128)S(1)}, f32[128,128]{1,0:T(8,128)S(1)}, u32[]{:S(2)}, u32[]{:S(2)}) collective-permute-start(f32[128,128]{1,0:T(8,128)S(1)} %add_select_fusion.1), channel_id=1, source_target_pairs={{0,6},{1,7},{2,4},{3,5},{4,2},{5,3},{6,0},{7,1},{8,14},{9,15},{10,... | collective-permute-start | bytes 196616 | tf_op jit(solution)/shard_map/ppermute | solution.py:534
  19.8 26.9 %copy-start.1 = (f32[2,8192]{1,0:T(2,128)S(1)}, f32[2,8192]{1,0:T(2,128)}, u32[]{:S(2)}) copy-start(f32[2,8192]{1,0:T(2,128)} %param.11) | copy-start | bytes 196612
  32.3 20.5 %copy-start = (f32[16,8192]{1,0:T(8,128)S(1)}, f32[16,8192]{1,0:T(8,128)}, u32[]{:S(2)}) copy-start(f32[16,8192]{1,0:T(8,128)} %param.10) | copy-start | bytes 1572868
  32.4 14.1 %collective-permute-start.4 = (f32[16,4096]{1,0:T(8,128)S(1)}, f32[16,4096]{1,0:T(8,128)S(1)}, u32[]{:S(2)}, u32[]{:S(2)}) collective-permute-start(f32[16,4096]{1,0:T(8,128)S(1)} %get-tuple-element.42), channel_id=1, source_target_pairs={{0,1},{1,0},{2,3},{3,2},{4,5},{5,4},{6,7},{7,6},{8,9},{9,8},{10,11... | collective-permute-start | bytes 786440 | tf_op jit(solution)/shard_map/ppermute | solution.py:534
  46.6 5.0 %collective-permute-start.5 = (f32[8,4096]{1,0:T(8,128)S(1)}, f32[8,4096]{1,0:T(8,128)S(1)}, u32[]{:S(2)}, u32[]{:S(2)}) collective-permute-start(f32[8,4096]{1,0:T(8,128)S(1)} %slice_select_fusion.3), channel_id=1, source_target_pairs={{0,2},{1,3},{2,0},{3,1},{4,6},{5,7},{6,4},{7,5},{8,10},{9,11},{10,... | collective-permute-start | bytes 393224 | tf_op jit(solution)/shard_map/ppermute | solution.py:534
  51.6 7.1 %collective-permute-start.6 = (f32[8,4096]{1,0:T(8,128)S(1)}, f32[8,4096]{1,0:T(8,128)S(1)}, u32[]{:S(2)}, u32[]{:S(2)}) collective-permute-start(f32[8,4096]{1,0:T(8,128)S(1)} %select_add_fusion.1), channel_id=1, source_target_pairs={{0,6},{1,7},{2,4},{3,5},{4,2},{5,3},{6,0},{7,1},{8,14},{9,15},{10,... | collective-permute-start | bytes 393224 | tf_op jit(solution)/shard_map/ppermute | solution.py:534
  52.9 11.6 %slice-start.2 = ((s8[8388608]{0:T(1024)(128)(4,1)}), s8[4194304]{0:T(1024)(128)(4,1)S(1)}, s32[]{:S(2)}) async-start(s8[8388608]{0:T(1024)(128)(4,1)} %bitcast.36), calls=%async_computation.2 | async-start | bytes 8388608
  52.9 11.5 %slice-start.3 = ((s8[8388608]{0:T(1024)(128)(4,1)}), s8[4194304]{0:T(1024)(128)(4,1)S(1)}, s32[]{:S(2)}) async-start(s8[8388608]{0:T(1024)(128)(4,1)} %bitcast.36), calls=%async_computation.3 | async-start | bytes 8388608
  56.5 15.5 %slice-start = ((s8[8388608]{0:T(1024)(128)(4,1)}), s8[4194304]{0:T(1024)(128)(4,1)S(1)}, s32[]{:S(2)}) async-start(s8[8388608]{0:T(1024)(128)(4,1)} %bitcast.34), calls=%async_computation | async-start | bytes 8388608
  58.8 5.0 %collective-permute-start.7 = (f32[8,4096]{1,0:T(8,128)S(1)}, f32[8,4096]{1,0:T(8,128)S(1)}, u32[]{:S(2)}, u32[]{:S(2)}) collective-permute-start(f32[8,4096]{1,0:T(8,128)S(1)} %add.110), channel_id=1, source_target_pairs={{0,2},{1,3},{2,0},{3,1},{4,6},{5,7},{6,4},{7,5},{8,10},{9,11},{10,... | collective-permute-start | bytes 393224 | tf_op jit(solution)/shard_map/ppermute | solution.py:534
  63.9 8.2 %collective-permute-start.8 = (f32[16,4096]{1,0:T(8,128)S(1)}, f32[16,4096]{1,0:T(8,128)S(1)}, u32[]{:S(2)}, u32[]{:S(2)}) collective-permute-start(f32[16,4096]{1,0:T(8,128)S(1)} %pad_maximum_fusion.1.pred_ref), channel_id=1, source_target_pairs={{0,1},{1,0},{2,3},{3,2},{4,5},{5,4},{6,7},{7,6},{8,9},{9,8},{10,11... | collective-permute-start | bytes 786440 | tf_op jit(solution)/shard_map/ppermute | solution.py:534
  64.4 7.6 %slice-start.1 = ((s8[8388608]{0:T(1024)(128)(4,1)}), s8[4194304]{0:T(1024)(128)(4,1)S(1)}, s32[]{:S(2)}) async-start(s8[8388608]{0:T(1024)(128)(4,1)} %bitcast.34), calls=%async_computation.1 | async-start | bytes 8388608
  70.2 7.8 %collective-permute-start.9 = (f32[16,4096]{1,0:T(8,128)S(1)}, f32[16,4096]{1,0:T(8,128)S(1)}, u32[]{:S(2)}, u32[]{:S(2)}) collective-permute-start(f32[16,4096]{1,0:T(8,128)S(1)} %correct.3), channel_id=1, source_target_pairs={{0,1},{1,0},{2,3},{3,2},{4,5},{5,4},{6,7},{7,6},{8,9},{9,8},{10,11... | collective-permute-start | bytes 786440 | tf_op jit(solution)/shard_map/ppermute | solution.py:534
  78.1 5.5 %collective-permute-start.10 = (f32[8,4096]{1,0:T(8,128)S(1)}, f32[8,4096]{1,0:T(8,128)S(1)}, u32[]{:S(2)}, u32[]{:S(2)}) collective-permute-start(f32[8,4096]{1,0:T(8,128)S(1)} %slice_select_fusion.2), channel_id=1, source_target_pairs={{0,2},{1,3},{2,0},{3,1},{4,6},{5,7},{6,4},{7,5},{8,10},{9,11},{10,... | collective-permute-start | bytes 393224 | tf_op jit(solution)/shard_map/ppermute | solution.py:534
  83.6 7.8 %collective-permute-start.11 = (f32[8,4096]{1,0:T(8,128)S(1)}, f32[8,4096]{1,0:T(8,128)S(1)}, u32[]{:S(2)}, u32[]{:S(2)}) collective-permute-start(f32[8,4096]{1,0:T(8,128)S(1)} %select_add_fusion), channel_id=1, source_target_pairs={{0,6},{1,7},{2,4},{3,5},{4,2},{5,3},{6,0},{7,1},{8,14},{9,15},{10,... | collective-permute-start | bytes 393224 | tf_op jit(solution)/shard_map/ppermute | solution.py:534
  91.4 5.0 %collective-permute-start.14 = (f32[8,4096]{1,0:T(8,128)S(1)}, f32[8,4096]{1,0:T(8,128)S(1)}, u32[]{:S(2)}, u32[]{:S(2)}) collective-permute-start(f32[8,4096]{1,0:T(8,128)S(1)} %fusion.5), channel_id=1, source_target_pairs={{0,2},{1,3},{2,0},{3,1},{4,6},{5,7},{6,4},{7,5},{8,10},{9,11},{10,... | collective-permute-start | bytes 393224 | tf_op jit(solution)/shard_map/ppermute | solution.py:534
  91.6 5.0 %collective-permute-start.12 = (f32[8,4096]{1,0:T(8,128)S(1)}, f32[8,4096]{1,0:T(8,128)S(1)}, u32[]{:S(2)}, u32[]{:S(2)}) collective-permute-start(f32[8,4096]{1,0:T(8,128)S(1)} %fusion.5), channel_id=1, source_target_pairs={{0,1},{1,0},{2,3},{3,2},{4,5},{5,4},{6,7},{7,6},{8,9},{9,8},{10,11... | collective-permute-start | bytes 393224 | tf_op jit(solution)/shard_map/ppermute | solution.py:534
  93.3 5.9 %collective-permute-start.13 = (f32[8,4096]{1,0:T(8,128)S(1)}, f32[8,4096]{1,0:T(8,128)S(1)}, u32[]{:S(2)}, u32[]{:S(2)}) collective-permute-start(f32[8,4096]{1,0:T(8,128)S(1)} %fusion.5), channel_id=1, source_target_pairs={{0,3},{1,2},{2,1},{3,0},{4,7},{5,6},{6,5},{7,4},{8,11},{9,10},{10,... | collective-permute-start | bytes 393224 | tf_op jit(solution)/shard_map/ppermute | solution.py:534

commit v5 on v4

--- a/solution.py
+++ b/solution.py
@@ -117,26 +117,15 @@
         here = pl.ds(pl.multiple_of(j * tiles * 8, 16), tiles * 8)
         return pltpu.make_async_copy(h_ref.at[:, :, there], held.at[:, :, here], in_sems.at[j])
 
-    def copy_out(j, near):
-        there = pl.ds(pl.multiple_of((j if near else j - inside) * chunk, chunk), chunk)
-        return pltpu.make_async_copy(
-            kept.at[j % 2], (near_ref if near else far_ref).at[:, there], out_sems.at[j % 2]
-        )
+    def copy_out(j, n, near):
+        there = pl.ds(pl.multiple_of((j if near else j - inside) * chunk + n * WIDE, WIDE), WIDE)
+        here = kept.at[j % 2, :, pl.ds(n * WIDE, WIDE)]
+        return pltpu.make_async_copy(here, (near_ref if near else far_ref).at[:, there], out_sems.at[j % 2, n])
 
     def copy_energy(j, a):
         there = pl.ds(pl.multiple_of(sc_ref[0] * columns + j * chunk, chunk), chunk)
         here = pl.ds(pl.multiple_of(j * chunk, chunk), chunk)
         return pltpu.make_async_copy(energy_ref.at[:, a, there], energies.at[a, :, here], energy_sems.at[j, a])
-
-    def copy_out(j, near):
-        there = pl.ds(pl.multiple_of((j if near else j - inside) * chunk, chunk), chunk)
-        return pltpu.make_async_copy(
-            kept.at[j % 2], (near_ref if near else far_ref).at[:, there], out_sems.at[j % 2]
-        )
-
-    def copy_waves(j):
-        lanes = pl.ds(pl.multiple_of(j * chunk, chunk), chunk)
-        return pltpu.make_async_copy(waves_ref.at[:, :, :, lanes], waves.at[:, :, :, lanes], wave_sems.at[j])
 
     for j in range(count):
         for a in range(2):
@@ -201,7 +190,7 @@
             imag.append(c * y - s * x)
         return real + imag
 
-    def work(j):
+    def work(j, near):
         items = [(n, i) for n in range(chunk // WIDE) for i in range(steps // group)]
         sums = {}
         buf = j % 2
@@ -242,6 +231,8 @@
                 ready.append((top, (x - top.astype(F32)).astype(BF)))
             waiting = (n, i, ready)
             moved = later
+            if i == steps // group - 1:
+                copy_out(j, n, near).start()
         contract(*waiting)
 
     def span(first, last, near):
@@ -256,10 +247,10 @@
 
             @pl.when(j >= 2)
             def _():
-                copy_out(j, near).wait()
-
-            work(j)
-            copy_out(j, near).start()
+                for n in range(chunk // WIDE):
+                    copy_out(j, n, near).wait()
+
+            work(j, near)
 
     perm_ref[...] = permutation()
     tri_ref[...] = suffix_rows(steps)
@@ -271,7 +262,8 @@
     span(0, inside, True)
     span(inside, count, False)
     for j in range(max(count - 2, 0), count):
-        copy_out(j, j < inside).wait()
+        for n in range(chunk // WIDE):
+            copy_out(j, n, j < inside).wait()
 
 
 def predict(side, edge, weights, stored, energy, off):
@@ -295,7 +287,7 @@
             pltpu.VMEM((2, steps, WIDE), F32),
             pltpu.VMEM((2, 2, 2, steps, WIDE), F32),
             pltpu.VMEM((2, steps * 16, chunk), F32),
-            pltpu.SemaphoreType.DMA((2,)),
+            pltpu.SemaphoreType.DMA((2, chunk // WIDE)),
             pltpu.VMEM((16 * group, 16 * group), BF),
             pltpu.VMEM((steps, 3 * steps), BF),
         ],

time: 101 us -> 99.6 us (0.986)
  Pallas kernels: 54 us -> 52.7 us
    pallas_call x2, Pallas kernels: 25.1 us -> 23.8 us  [predict(): pl.pallas_call(functools.partial(predict_kernel, inside, steps, group), i...]
where the time goes in v5:
time: 99.6 us; the launch traced here: 99.4 us
  Pallas kernels  52.7 us (53%)
  waiting for transfers between devices  22.6 us (23%)
  starting transfers between devices  19.3 us (19%)
  local copies, waits for them, and re-layouts  2.09 us (2%)
  between operations  1.83 us (2%)
    pallas_call x2, Pallas kernels, predict(): pl.pallas_call(functools.partial(predict_kernel, inside, steps, group), i...  23.8 us
    ppermute x15, waiting for transfers between devices, swap(): return lax.ppermute(x, 'ta', [(i, i ^ mask) for i in range(count)])  22.6 us
    ppermute x15, starting transfers between devices, swap(): return lax.ppermute(x, 'ta', [(i, i ^ mask) for i in range(count)])  19.3 us
    pallas_call x4, Pallas kernels, carry(): pl.pallas_call(functools.partial(carry_kernel, piece), in_specs=[HB] * le...  13.5 us
    pallas_call x2, Pallas kernels, correct(): pl.pallas_call(functools.partial(correct_kernel, inside, steps, group), i...  11.7 us
    pallas_call x1, Pallas kernels, totals(): pl.pallas_call(totals_kernel, in_specs=[SM, HB], out_specs=[VM, VM], out_...  2.33 us
  transfers between devices with their start and end apart: 15, of which 12 were waited for; matrix products, arithmetic and copies ran while one was open for 3% of the time, Pallas kernels for 37%

profile of v5, /device:TPU:0, one launch (start us, length us, event | category | flops | bytes accessed | tf_op | source)
XLA Modules:
  0.0 99.4 jit_solution(13201459745425108486)
XLA Ops:
  1.3 2.3 %totals.1 = (f32[128,128]{1,0:T(8,128)S(1)}, f32[128,128]{1,0:T(8,128)S(1)}) custom-call(s32[1]{0:T(128)} %bitcast.8.edge_ref, f32[64,128,128]{2,1,0:T(8,128)} %bitcast.45), custom_call_target="tpu_custom_call" | custom-call | flops 4194304 | bytes 4194304 | tf_op jit(solution)/shard_map/totals/pallas_call | solution.py:72
  3.6 3.0 %collective-permute-start = (f32[128,128]{1,0:T(8,128)S(1)}, f32[128,128]{1,0:T(8,128)S(1)}, u32[]{:S(2)}, u32[]{:S(2)}) collective-permute-start(f32[128,128]{1,0:T(8,128)S(1)} %get-tuple-element.33), channel_id=1, source_target_pairs={{0,1},{1,0},{2,3},{3,2},{4,5},{5,4},{6,7},{7,6},{8,9},{9,8},{10,11... | collective-permute-start | bytes 196616 | tf_op jit(solution)/shard_map/ppermute | solution.py:526
  6.7 1.2 %copy.14 = f32[64,16,16]{2,1,0:T(8,128)S(1)} copy(f32[64,16,16]{0,2,1:T(8,128)} %param.8) | data formatting | bytes 131072 | tf_op args[2]
  7.8 0.2 copy.15
  8.1 0.2 copy.16
  8.3 0.6 collective-permute-done
  8.9 2.1 %collective-permute-start.1 = (f32[128,128]{1,0:T(8,128)S(1)}, f32[128,128]{1,0:T(8,128)S(1)}, u32[]{:S(2)}, u32[]{:S(2)}) collective-permute-start(f32[128,128]{1,0:T(8,128)S(1)} %add_select_fusion.1), channel_id=1, source_target_pairs={{0,2},{1,3},{2,0},{3,1},{4,6},{5,7},{6,4},{7,5},{8,10},{9,11},{10,... | collective-permute-start | bytes 196616 | tf_op jit(solution)/shard_map/ppermute | solution.py:526
  11.1 2.6 %collective-permute-start.2 = (f32[128,128]{1,0:T(8,128)S(1)}, f32[128,128]{1,0:T(8,128)S(1)}, u32[]{:S(2)}, u32[]{:S(2)}) collective-permute-start(f32[128,128]{1,0:T(8,128)S(1)} %add_select_fusion.1), channel_id=1, source_target_pairs={{0,4},{1,5},{2,6},{3,7},{4,0},{5,1},{6,2},{7,3},{8,12},{9,13},{10,... | collective-permute-start | bytes 196616 | tf_op jit(solution)/shard_map/ppermute | solution.py:526
  13.6 0.0 collective-permute-start.3
  13.6 0.1 pad_add_fusion.1
  13.7 3.3 %carry.4.rest_0_ = bf16[64,2,512,128]{3,2,1,0:T(8,128)(2,1)} custom-call(bf16[64,2,512,128]{3,2,1,0:T(8,128)(2,1)} %bitcast.38), custom_call_target="tpu_custom_call" | custom-call | bytes 8388608 | tf_op jit(solution)/shard_map/carry/pallas_call | solution.py:429
  17.0 0.0 collective-permute-done.1
  17.0 0.6 collective-permute-done.2
  17.6 2.1 %collective-permute-done.3 = f32[128,128]{1,0:T(8,128)S(1)} collective-permute-done((f32[128,128]{1,0:T(8,128)S(1)}, f32[128,128]{1,0:T(8,128)S(1)}, u32[]{:S(2)}, u32[]{:S(2)}) %collective-permute-start.3) | collective-permute-done | bytes 65568 | tf_op jit(solution)/shard_map/ppermute | solution.py:526
  19.8 0.0 copy-start.1
  19.8 11.9 %predict.3 = (f32[16,4096]{1,0:T(8,128)S(1)}, f32[1024,2048]{1,0:T(8,128)}, f32[1024,2048]{1,0:T(8,128)}) custom-call(s32[2]{0:T(128)S(1)} %get-tuple-element.77.sc_ref, bf16[8,32,128]{2,1,0:T(8,128)(2,1)S(1)} %pad_maximum_fusion.4.k_ref, bf16[64,2,512,128]{3,2,1,0:T(8,128)(2,1)} %bitcast.39, f32[64,2,8192]{2,1,0:T(2,128)} %energy_ref.3, ...), custom_call_target="tpu_custom_call" | custom-call | flops 838860800 | bytes 25165824 | tf_op jit(solution)/shard_map/predict/pallas_call | solution.py:276
  31.7 0.0 copy-start
  31.7 1.6 %collective-permute-start.4 = (f32[16,4096]{1,0:T(8,128)S(1)}, f32[16,4096]{1,0:T(8,128)S(1)}, u32[]{:S(2)}, u32[]{:S(2)}) collective-permute-start(f32[16,4096]{1,0:T(8,128)S(1)} %get-tuple-element.42), channel_id=1, source_target_pairs={{0,1},{1,0},{2,3},{3,2},{4,5},{5,4},{6,7},{7,6},{8,9},{9,8},{10,11... | collective-permute-start | bytes 786440 | tf_op jit(solution)/shard_map/ppermute | solution.py:526
  33.3 11.9 %predict.2 = (f32[16,4096]{1,0:T(8,128)S(1)}, f32[1024,2048]{1,0:T(8,128)}, f32[1024,2048]{1,0:T(8,128)}) custom-call(s32[2]{0:T(128)S(1)} %get-tuple-element.76.sc_ref, bf16[8,32,128]{2,1,0:T(8,128)(2,1)S(1)} %pad_maximum_fusion.4.k_ref, bf16[64,2,512,128]{3,2,1,0:T(8,128)(2,1)} %bitcast.40, f32[64,2,8192]{2,1,0:T(2,128)} %energy_ref.3, ...), custom_call_target="tpu_custom_call" | custom-call | flops 838860800 | bytes 25165824 | tf_op jit(solution)/shard_map/predict/pallas_call | solution.py:276
  45.2 0.0 collective-permute-done.4
  45.3 0.1 collective-permute-start.5
  45.3 0.0 copy-done.1
  45.4 0.2 multiply_subtract_fusion.1
  45.6 0.1 broadcast_in_dim.19
  45.7 0.2 reshape.44
  45.9 0.1 broadcast_in_dim.20
  45.9 0.2 reshape.45
  46.1 4.2 %collective-permute-done.5 = f32[8,4096]{1,0:T(8,128)S(1)} collective-permute-done((f32[8,4096]{1,0:T(8,128)S(1)}, f32[8,4096]{1,0:T(8,128)S(1)}, u32[]{:S(2)}, u32[]{:S(2)}) %collective-permute-start.5) | collective-permute-done | bytes 131104 | tf_op jit(solution)/shard_map/ppermute | solution.py:526
  50.3 1.2 %collective-permute-start.6 = (f32[8,4096]{1,0:T(8,128)S(1)}, f32[8,4096]{1,0:T(8,128)S(1)}, u32[]{:S(2)}, u32[]{:S(2)}) collective-permute-start(f32[8,4096]{1,0:T(8,128)S(1)} %select_add_fusion.1), channel_id=1, source_target_pairs={{0,6},{1,7},{2,4},{3,5},{4,2},{5,3},{6,0},{7,1},{8,14},{9,15},{10,... | collective-permute-start | bytes 393224 | tf_op jit(solution)/shard_map/ppermute | solution.py:526
  51.6 0.0 copy-done
  51.6 0.0 slice-start.2
  51.6 0.1 multiply_add_fusion
  51.6 0.0 slice-start.3
  51.6 3.6 %carry.5.rest_0_ = bf16[64,2,512,128]{3,2,1,0:T(8,128)(2,1)} custom-call(bf16[64,2,512,128]{3,2,1,0:T(8,128)(2,1)} %bitcast.41, bf16[64,2,512,128]{3,2,1,0:T(8,128)(2,1)} %carry.4.rest_0_), custom_call_target="tpu_custom_call", output_to_operand_aliasing={{}: (1, {})} | custom-call | bytes 8388608 | tf_op jit(solution)/shard_map/carry/pallas_call | solution.py:429
  55.2 0.0 slice-start
  55.2 2.2 %collective-permute-done.6 = f32[8,4096]{1,0:T(8,128)S(1)} collective-permute-done((f32[8,4096]{1,0:T(8,128)S(1)}, f32[8,4096]{1,0:T(8,128)S(1)}, u32[]{:S(2)}, u32[]{:S(2)}) %collective-permute-start.6) | collective-permute-done | bytes 131104 | tf_op jit(solution)/shard_map/ppermute | solution.py:526
  57.5 0.1 collective-permute-start.7
  57.6 4.9 %collective-permute-done.7 = f32[8,4096]{1,0:T(8,128)S(1)} collective-permute-done((f32[8,4096]{1,0:T(8,128)S(1)}, f32[8,4096]{1,0:T(8,128)S(1)}, u32[]{:S(2)}, u32[]{:S(2)}) %collective-permute-start.7) | collective-permute-done | bytes 131104 | tf_op jit(solution)/shard_map/ppermute | solution.py:526
  62.5 0.6 collective-permute-start.8
  63.1 0.0 slice-done.2
  63.1 0.0 slice-done.3
  63.1 0.0 slice-start.1
  63.1 5.8 %correct.3 = f32[16,4096]{1,0:T(8,128)S(1)} custom-call(s32[1]{0:T(128)} %bitcast.sc_ref, bf16[8,32,128]{2,1,0:T(8,128)(2,1)S(1)} %pad_maximum_fusion.4.k_ref, f32[16,8192]{1,0:T(8,128)S(1)} %pad_maximum_fusion.start_ref, f32[16,4096]{1,0:T(8,128)S(1)} %pad_maximum_fusion.1.pred_ref, f32[1024,2048]{1,0:T(8,128)S(1)} %bitcast.37, ...), custom_call_target="tpu_custom_call" | custom-call | flops 503316480 | bytes 16777216 | tf_op jit(solution)/shard_map/correct/pallas_call | solution.py:383
  68.9 1.6 %collective-permute-start.9 = (f32[16,4096]{1,0:T(8,128)S(1)}, f32[16,4096]{1,0:T(8,128)S(1)}, u32[]{:S(2)}, u32[]{:S(2)}) collective-permute-start(f32[16,4096]{1,0:T(8,128)S(1)} %correct.3), channel_id=1, source_target_pairs={{0,1},{1,0},{2,3},{3,2},{4,5},{5,4},{6,7},{7,6},{8,9},{9,8},{10,11... | collective-permute-start | bytes 786440 | tf_op jit(solution)/shard_map/ppermute | solution.py:526
  70.5 0.2 collective-permute-done.8.pred_ref
  70.7 0.0 slice-done
  70.7 0.0 slice-done.1
  70.7 5.9 %correct.2 = f32[16,4096]{1,0:T(8,128)S(1)} custom-call(s32[1]{0:T(128)} %bitcast.4.sc_ref, bf16[8,32,128]{2,1,0:T(8,128)(2,1)S(1)} %pad_maximum_fusion.4.k_ref, f32[16,8192]{1,0:T(8,128)S(1)} %pad_maximum_fusion.start_ref, f32[16,4096]{1,0:T(8,128)S(1)} %collective-permute-done.8.pred_ref, f32[1024,2048]{1,0:T(8,128)S(1)} %bitcast.35, ...), custom_call_target="tpu_custom_call" | custom-call | flops 503316480 | bytes 16777216 | tf_op jit(solution)/shard_map/correct/pallas_call | solution.py:383
  76.7 0.0 collective-permute-done.9
  76.8 1.1 %collective-permute-start.10 = (f32[8,4096]{1,0:T(8,128)S(1)}, f32[8,4096]{1,0:T(8,128)S(1)}, u32[]{:S(2)}, u32[]{:S(2)}) collective-permute-start(f32[8,4096]{1,0:T(8,128)S(1)} %slice_select_fusion.2), channel_id=1, source_target_pairs={{0,2},{1,3},{2,0},{3,1},{4,6},{5,7},{6,4},{7,5},{8,10},{9,11},{10,... | collective-permute-start | bytes 393224 | tf_op jit(solution)/shard_map/ppermute | solution.py:526
  77.8 3.3 %carry.6.rest_0_ = bf16[64,2,512,128]{3,2,1,0:T(8,128)(2,1)} custom-call(bf16[64,2,512,128]{3,2,1,0:T(8,128)(2,1)} %bitcast.42, bf16[64,2,512,128]{3,2,1,0:T(8,128)(2,1)} %carry.5.rest_0_), custom_call_target="tpu_custom_call", output_to_operand_aliasing={{}: (1, {})} | custom-call | bytes 8388608 | tf_op jit(solution)/shard_map/carry/pallas_call | solution.py:429
  81.1 1.1 %collective-permute-done.10 = f32[8,4096]{1,0:T(8,128)S(1)} collective-permute-done((f32[8,4096]{1,0:T(8,128)S(1)}, f32[8,4096]{1,0:T(8,128)S(1)}, u32[]{:S(2)}, u32[]{:S(2)}) %collective-permute-start.10) | collective-permute-done | bytes 131104 | tf_op jit(solution)/shard_map/ppermute | solution.py:526
  82.3 1.8 %collective-permute-start.11 = (f32[8,4096]{1,0:T(8,128)S(1)}, f32[8,4096]{1,0:T(8,128)S(1)}, u32[]{:S(2)}, u32[]{:S(2)}) collective-permute-start(f32[8,4096]{1,0:T(8,128)S(1)} %select_add_fusion), channel_id=1, source_target_pairs={{0,6},{1,7},{2,4},{3,5},{4,2},{5,3},{6,0},{7,1},{8,14},{9,15},{10,... | collective-permute-start | bytes 393224 | tf_op jit(solution)/shard_map/ppermute | solution.py:526
  84.1 3.3 %carry.7.old_ref = bf16[64,2,512,128]{3,2,1,0:T(8,128)(2,1)} custom-call(bf16[64,2,512,128]{3,2,1,0:T(8,128)(2,1)} %bitcast.43, bf16[64,2,512,128]{3,2,1,0:T(8,128)(2,1)} %carry.6.rest_0_), custom_call_target="tpu_custom_call", output_to_operand_aliasing={{}: (1, {})} | custom-call | bytes 8388608 | tf_op jit(solution)/shard_map/carry/pallas_call | solution.py:429
  87.4 2.6 %collective-permute-done.11 = f32[8,4096]{1,0:T(8,128)S(1)} collective-permute-done((f32[8,4096]{1,0:T(8,128)S(1)}, f32[8,4096]{1,0:T(8,128)S(1)}, u32[]{:S(2)}, u32[]{:S(2)}) %collective-permute-start.11) | collective-permute-done | bytes 131104 | tf_op jit(solution)/shard_map/ppermute | solution.py:526
  90.1 0.1 fusion.5
  90.2 0.1 collective-permute-start.14
  90.3 0.1 pad_add_fusion.sc_ref
  90.3 1.7 %collective-permute-start.12 = (f32[8,4096]{1,0:T(8,128)S(1)}, f32[8,4096]{1,0:T(8,128)S(1)}, u32[]{:S(2)}, u32[]{:S(2)}) collective-permute-start(f32[8,4096]{1,0:T(8,128)S(1)} %fusion.5), channel_id=1, source_target_pairs={{0,1},{1,0},{2,3},{3,2},{4,5},{5,4},{6,7},{7,6},{8,9},{9,8},{10,11... | collective-permute-start | bytes 393224 | tf_op jit(solution)/shard_map/ppermute | solution.py:526
  92.0 1.8 %collective-permute-start.13 = (f32[8,4096]{1,0:T(8,128)S(1)}, f32[8,4096]{1,0:T(8,128)S(1)}, u32[]{:S(2)}, u32[]{:S(2)}) collective-permute-start(f32[8,4096]{1,0:T(8,128)S(1)} %fusion.5), channel_id=1, source_target_pairs={{0,3},{1,2},{2,1},{3,0},{4,7},{5,6},{6,5},{7,4},{8,11},{9,10},{10,... | collective-permute-start | bytes 393224 | tf_op jit(solution)/shard_map/ppermute | solution.py:526
  93.8 1.4 %collective-permute-done.14 = f32[8,4096]{1,0:T(8,128)S(1)} collective-permute-done((f32[8,4096]{1,0:T(8,128)S(1)}, f32[8,4096]{1,0:T(8,128)S(1)}, u32[]{:S(2)}, u32[]{:S(2)}) %collective-permute-start.14) | collective-permute-done | bytes 131104 | tf_op jit(solution)/shard_map/ppermute | solution.py:526
  95.2 0.1 collective-permute-done.12
  95.3 2.6 %collective-permute-done.13 = f32[8,4096]{1,0:T(8,128)S(1)} collective-permute-done((f32[8,4096]{1,0:T(8,128)S(1)}, f32[8,4096]{1,0:T(8,128)S(1)}, u32[]{:S(2)}, u32[]{:S(2)}) %collective-permute-start.13) | collective-permute-done | bytes 131104 | tf_op jit(solution)/shard_map/ppermute | solution.py:526
  97.9 1.4 %finish.1 = (f32[16,8192]{1,0:T(8,128)}, bf16[64,2,512,128]{3,2,1,0:T(8,128)(2,1)}) custom-call(s32[3]{0:T(128)S(1)} %pad_add_fusion.sc_ref, bf16[64,2,512,128]{3,2,1,0:T(8,128)(2,1)} %carry.7.old_ref, f32[16,4096]{1,0:T(8,128)S(1)} %pad_maximum_fusion.2.own_ref, f32[16,4096]{1,0:T(8,128)S(1)} %pad_maximum_fusion.3.other_ref), custom_call_target="tpu_custom_call", output_to_operand_aliasing={{1}: (1, {})} | custom-call | tf_op jit(solution)/shard_map/finish/pallas_call | solution.py:477
  (23 shorter events, 0.4 us)
Async XLA Ops:
  3.6 5.3 %collective-permute-start = (f32[128,128]{1,0:T(8,128)S(1)}, f32[128,128]{1,0:T(8,128)S(1)}, u32[]{:S(2)}, u32[]{:S(2)}) collective-permute-start(f32[128,128]{1,0:T(8,128)S(1)} %get-tuple-element.33), channel_id=1, source_target_pairs={{0,1},{1,0},{2,3},{3,2},{4,5},{5,4},{6,7},{7,6},{8,9},{9,8},{10,11... | collective-permute-start | bytes 196616 | tf_op jit(solution)/shard_map/ppermute | solution.py:526
  8.9 8.1 %collective-permute-start.1 = (f32[128,128]{1,0:T(8,128)S(1)}, f32[128,128]{1,0:T(8,128)S(1)}, u32[]{:S(2)}, u32[]{:S(2)}) collective-permute-start(f32[128,128]{1,0:T(8,128)S(1)} %add_select_fusion.1), channel_id=1, source_target_pairs={{0,2},{1,3},{2,0},{3,1},{4,6},{5,7},{6,4},{7,5},{8,10},{9,11},{10,... | collective-permute-start | bytes 196616 | tf_op jit(solution)/shard_map/ppermute | solution.py:526
  11.1 6.6 %collective-permute-start.2 = (f32[128,128]{1,0:T(8,128)S(1)}, f32[128,128]{1,0:T(8,128)S(1)}, u32[]{:S(2)}, u32[]{:S(2)}) collective-permute-start(f32[128,128]{1,0:T(8,128)S(1)} %add_select_fusion.1), channel_id=1, source_target_pairs={{0,4},{1,5},{2,6},{3,7},{4,0},{5,1},{6,2},{7,3},{8,12},{9,13},{10,... | collective-permute-start | bytes 196616 | tf_op jit(solution)/shard_map/ppermute | solution.py:526
  13.6 6.1 %collective-permute-start.3 = (f32[128,128]{1,0:T(8,128)S(1)}, f32[128,128]{1,0:T(8,128)S(1)}, u32[]{:S(2)}, u32[]{:S(2)}) collective-permute-start(f32[128,128]{1,0:T(8,128)S(1)} %add_select_fusion.1), channel_id=1, source_target_pairs={{0,6},{1,7},{2,4},{3,5},{4,2},{5,3},{6,0},{7,1},{8,14},{9,15},{10,... | collective-permute-start | bytes 196616 | tf_op jit(solution)/shard_map/ppermute | solution.py:526
  19.8 25.6 %copy-start.1 = (f32[2,8192]{1,0:T(2,128)S(1)}, f32[2,8192]{1,0:T(2,128)}, u32[]{:S(2)}) copy-start(f32[2,8192]{1,0:T(2,128)} %param.11) | copy-start | bytes 196612
  31.7 19.9 %copy-start = (f32[16,8192]{1,0:T(8,128)S(1)}, f32[16,8192]{1,0:T(8,128)}, u32[]{:S(2)}) copy-start(f32[16,8192]{1,0:T(8,128)} %param.10) | copy-start | bytes 1572868
  31.7 13.5 %collective-permute-start.4 = (f32[16,4096]{1,0:T(8,128)S(1)}, f32[16,4096]{1,0:T(8,128)S(1)}, u32[]{:S(2)}, u32[]{:S(2)}) collective-permute-start(f32[16,4096]{1,0:T(8,128)S(1)} %get-tuple-element.42), channel_id=1, source_target_pairs={{0,1},{1,0},{2,3},{3,2},{4,5},{5,4},{6,7},{7,6},{8,9},{9,8},{10,11... | collective-permute-start | bytes 786440 | tf_op jit(solution)/shard_map/ppermute | solution.py:526
  45.3 5.0 %collective-permute-start.5 = (f32[8,4096]{1,0:T(8,128)S(1)}, f32[8,4096]{1,0:T(8,128)S(1)}, u32[]{:S(2)}, u32[]{:S(2)}) collective-permute-start(f32[8,4096]{1,0:T(8,128)S(1)} %slice_select_fusion.3), channel_id=1, source_target_pairs={{0,2},{1,3},{2,0},{3,1},{4,6},{5,7},{6,4},{7,5},{8,10},{9,11},{10,... | collective-permute-start | bytes 393224 | tf_op jit(solution)/shard_map/ppermute | solution.py:526
  50.3 7.1 %collective-permute-start.6 = (f32[8,4096]{1,0:T(8,128)S(1)}, f32[8,4096]{1,0:T(8,128)S(1)}, u32[]{:S(2)}, u32[]{:S(2)}) collective-permute-start(f32[8,4096]{1,0:T(8,128)S(1)} %select_add_fusion.1), channel_id=1, source_target_pairs={{0,6},{1,7},{2,4},{3,5},{4,2},{5,3},{6,0},{7,1},{8,14},{9,15},{10,... | collective-permute-start | bytes 393224 | tf_op jit(solution)/shard_map/ppermute | solution.py:526
  51.6 11.6 %slice-start.2 = ((s8[8388608]{0:T(1024)(128)(4,1)}), s8[4194304]{0:T(1024)(128)(4,1)S(1)}, s32[]{:S(2)}) async-start(s8[8388608]{0:T(1024)(128)(4,1)} %bitcast.36), calls=%async_computation.2 | async-start | bytes 8388608
  51.6 11.5 %slice-start.3 = ((s8[8388608]{0:T(1024)(128)(4,1)}), s8[4194304]{0:T(1024)(128)(4,1)S(1)}, s32[]{:S(2)}) async-start(s8[8388608]{0:T(1024)(128)(4,1)} %bitcast.36), calls=%async_computation.3 | async-start | bytes 8388608
  55.2 15.5 %slice-start = ((s8[8388608]{0:T(1024)(128)(4,1)}), s8[4194304]{0:T(1024)(128)(4,1)S(1)}, s32[]{:S(2)}) async-start(s8[8388608]{0:T(1024)(128)(4,1)} %bitcast.34), calls=%async_computation | async-start | bytes 8388608
  57.5 5.0 %collective-permute-start.7 = (f32[8,4096]{1,0:T(8,128)S(1)}, f32[8,4096]{1,0:T(8,128)S(1)}, u32[]{:S(2)}, u32[]{:S(2)}) collective-permute-start(f32[8,4096]{1,0:T(8,128)S(1)} %add.110), channel_id=1, source_target_pairs={{0,2},{1,3},{2,0},{3,1},{4,6},{5,7},{6,4},{7,5},{8,10},{9,11},{10,... | collective-permute-start | bytes 393224 | tf_op jit(solution)/shard_map/ppermute | solution.py:526
  62.5 8.2 %collective-permute-start.8 = (f32[16,4096]{1,0:T(8,128)S(1)}, f32[16,4096]{1,0:T(8,128)S(1)}, u32[]{:S(2)}, u32[]{:S(2)}) collective-permute-start(f32[16,4096]{1,0:T(8,128)S(1)} %pad_maximum_fusion.1.pred_ref), channel_id=1, source_target_pairs={{0,1},{1,0},{2,3},{3,2},{4,5},{5,4},{6,7},{7,6},{8,9},{9,8},{10,11... | collective-permute-start | bytes 786440 | tf_op jit(solution)/shard_map/ppermute | solution.py:526
  63.1 7.6 %slice-start.1 = ((s8[8388608]{0:T(1024)(128)(4,1)}), s8[4194304]{0:T(1024)(128)(4,1)S(1)}, s32[]{:S(2)}) async-start(s8[8388608]{0:T(1024)(128)(4,1)} %bitcast.34), calls=%async_computation.1 | async-start | bytes 8388608
  68.9 7.8 %collective-permute-start.9 = (f32[16,4096]{1,0:T(8,128)S(1)}, f32[16,4096]{1,0:T(8,128)S(1)}, u32[]{:S(2)}, u32[]{:S(2)}) collective-permute-start(f32[16,4096]{1,0:T(8,128)S(1)} %correct.3), channel_id=1, source_target_pairs={{0,1},{1,0},{2,3},{3,2},{4,5},{5,4},{6,7},{7,6},{8,9},{9,8},{10,11... | collective-permute-start | bytes 786440 | tf_op jit(solution)/shard_map/ppermute | solution.py:526
  76.8 5.5 %collective-permute-start.10 = (f32[8,4096]{1,0:T(8,128)S(1)}, f32[8,4096]{1,0:T(8,128)S(1)}, u32[]{:S(2)}, u32[]{:S(2)}) collective-permute-start(f32[8,4096]{1,0:T(8,128)S(1)} %slice_select_fusion.2), channel_id=1, source_target_pairs={{0,2},{1,3},{2,0},{3,1},{4,6},{5,7},{6,4},{7,5},{8,10},{9,11},{10,... | collective-permute-start | bytes 393224 | tf_op jit(solution)/shard_map/ppermute | solution.py:526
  82.3 7.8 %collective-permute-start.11 = (f32[8,4096]{1,0:T(8,128)S(1)}, f32[8,4096]{1,0:T(8,128)S(1)}, u32[]{:S(2)}, u32[]{:S(2)}) collective-permute-start(f32[8,4096]{1,0:T(8,128)S(1)} %select_add_fusion), channel_id=1, source_target_pairs={{0,6},{1,7},{2,4},{3,5},{4,2},{5,3},{6,0},{7,1},{8,14},{9,15},{10,... | collective-permute-start | bytes 393224 | tf_op jit(solution)/shard_map/ppermute | solution.py:526
  90.2 5.0 %collective-permute-start.14 = (f32[8,4096]{1,0:T(8,128)S(1)}, f32[8,4096]{1,0:T(8,128)S(1)}, u32[]{:S(2)}, u32[]{:S(2)}) collective-permute-start(f32[8,4096]{1,0:T(8,128)S(1)} %fusion.5), channel_id=1, source_target_pairs={{0,2},{1,3},{2,0},{3,1},{4,6},{5,7},{6,4},{7,5},{8,10},{9,11},{10,... | collective-permute-start | bytes 393224 | tf_op jit(solution)/shard_map/ppermute | solution.py:526
  90.3 5.0 %collective-permute-start.12 = (f32[8,4096]{1,0:T(8,128)S(1)}, f32[8,4096]{1,0:T(8,128)S(1)}, u32[]{:S(2)}, u32[]{:S(2)}) collective-permute-start(f32[8,4096]{1,0:T(8,128)S(1)} %fusion.5), channel_id=1, source_target_pairs={{0,1},{1,0},{2,3},{3,2},{4,5},{5,4},{6,7},{7,6},{8,9},{9,8},{10,11... | collective-permute-start | bytes 393224 | tf_op jit(solution)/shard_map/ppermute | solution.py:526
  92.0 5.9 %collective-permute-start.13 = (f32[8,4096]{1,0:T(8,128)S(1)}, f32[8,4096]{1,0:T(8,128)S(1)}, u32[]{:S(2)}, u32[]{:S(2)}) collective-permute-start(f32[8,4096]{1,0:T(8,128)S(1)} %fusion.5), channel_id=1, source_target_pairs={{0,3},{1,2},{2,1},{3,0},{4,7},{5,6},{6,5},{7,4},{8,11},{9,10},{10,... | collective-permute-start | bytes 393224 | tf_op jit(solution)/shard_map/ppermute | solution.py:526

commit v6 on v5

--- a/solution.py
+++ b/solution.py
@@ -112,10 +112,11 @@
     blocks = group // 8
     edge = sc_ref[1]
 
-    def copy_in(j):
-        there = pl.ds(pl.multiple_of((sc_ref[0] * (columns // LANES) + j * tiles) * 8, 16), tiles * 8)
-        here = pl.ds(pl.multiple_of(j * tiles * 8, 16), tiles * 8)
-        return pltpu.make_async_copy(h_ref.at[:, :, there], held.at[:, :, here], in_sems.at[j])
+    def copy_in(j, n):
+        row = (j * tiles + 4 * n) * 8
+        there = pl.ds(pl.multiple_of(sc_ref[0] * (columns // LANES) * 8 + row, 32), 32)
+        here = pl.ds(pl.multiple_of(row, 32), 32)
+        return pltpu.make_async_copy(h_ref.at[:, :, there], held.at[:, :, here], in_sems.at[j, n])
 
     def copy_out(j, n, near):
         there = pl.ds(pl.multiple_of((j if near else j - inside) * chunk + n * WIDE, WIDE), WIDE)
@@ -130,7 +131,8 @@
     for j in range(count):
         for a in range(2):
             copy_energy(j, a).start()
-        copy_in(j).start()
+        for n in range(chunk // WIDE):
+            copy_in(j, n).start()
 
     def spans(j, n):
         first = j * chunk + n * WIDE
@@ -209,9 +211,12 @@
                     out_ref[:, local[t]] = total[:, :LANES]
                     out_ref[:, local[t + 2]] = total[:, LANES:]
 
+        copy_in(j, 0).wait()
         moved = move(j, *items[0])
         waiting = None
         for at, (n, i) in enumerate(items):
+            if at + 1 < len(items) and items[at + 1][1] == 0:
+                copy_in(j, n + 1).wait()
             later = move(j, *items[at + 1]) if at + 1 < len(items) else None
             if waiting is not None:
                 contract(*waiting)
@@ -238,8 +243,6 @@
     def span(first, last, near):
         @pl.loop(first, last)
         def _(j):
-            copy_in(j).wait()
-
             @pl.when(j + 1 < count)
             def _():
                 for a in range(2):
@@ -281,7 +284,7 @@
         + [jax.ShapeDtypeStruct((steps * 16, c), F32) for c in (inside * chunk, columns - inside * chunk)],
         scratch_shapes=[
             pltpu.VMEM((steps, 2, columns // 16, LANES), BF),
-            pltpu.SemaphoreType.DMA((count,)),
+            pltpu.SemaphoreType.DMA((count, chunk // WIDE)),
             pltpu.VMEM((2, steps, columns), F32),
             pltpu.SemaphoreType.DMA((count, 2)),
             pltpu.VMEM((2, steps, WIDE), F32),

time: 99.6 us -> 102 us (1.024)
  starting transfers between devices: 19.3 us -> 17.2 us
  waiting for transfers between devices: 22.6 us -> 24.7 us
  Pallas kernels: 52.7 us -> 54.8 us
    pallas_call x2, Pallas kernels: 23.8 us -> 26 us  [predict(): pl.pallas_call(functools.partial(predict_kernel, inside, steps, group), i...]
    ppermute x15, waiting for transfers between devices: 22.6 us -> 24.7 us  [swap(): return lax.ppermute(x, 'ta', [(i, i ^ mask) for i in range(count)])]
    ppermute x15, starting transfers between devices: 19.3 us -> 17.2 us  [swap(): return lax.ppermute(x, 'ta', [(i, i ^ mask) for i in range(count)])]
where the time goes in v6:
time: 102 us
  Pallas kernels  54.8 us (54%)
  waiting for transfers between devices  24.7 us (24%)
  starting transfers between devices  17.2 us (17%)
  local copies, waits for them, and re-layouts  2.09 us (2%)
  between operations  1.83 us (2%)
    pallas_call x2, Pallas kernels, predict(): pl.pallas_call(functools.partial(predict_kernel, inside, steps, group), i...  26 us
    ppermute x15, waiting for transfers between devices, swap(): return lax.ppermute(x, 'ta', [(i, i ^ mask) for i in range(count)])  24.7 us
    ppermute x15, starting transfers between devices, swap(): return lax.ppermute(x, 'ta', [(i, i ^ mask) for i in range(count)])  17.2 us
    pallas_call x4, Pallas kernels, carry(): pl.pallas_call(functools.partial(carry_kernel, piece), in_specs=[HB] * le...  13.5 us
    pallas_call x2, Pallas kernels, correct(): pl.pallas_call(functools.partial(correct_kernel, inside, steps, group), i...  11.6 us
    pallas_call x1, Pallas kernels, totals(): pl.pallas_call(totals_kernel, in_specs=[SM, HB], out_specs=[VM, VM], out_...  2.33 us
  transfers between devices with their start and end apart: 15, of which 12 were waited for; matrix products, arithmetic and copies ran while one was open for 3% of the time, Pallas kernels for 37%

profile of v6, /device:TPU:0, one launch (start us, length us, event | category | flops | bytes accessed | tf_op | source)
XLA Modules:
  0.0 101.6 jit_solution(14175252221804453425)
XLA Ops:
  1.3 2.3 %totals.1 = (f32[128,128]{1,0:T(8,128)S(1)}, f32[128,128]{1,0:T(8,128)S(1)}) custom-call(s32[1]{0:T(128)} %bitcast.8.edge_ref, f32[64,128,128]{2,1,0:T(8,128)} %bitcast.45), custom_call_target="tpu_custom_call" | custom-call | flops 4194304 | bytes 4194304 | tf_op jit(solution)/shard_map/totals/pallas_call | solution.py:72
  3.6 3.0 %collective-permute-start = (f32[128,128]{1,0:T(8,128)S(1)}, f32[128,128]{1,0:T(8,128)S(1)}, u32[]{:S(2)}, u32[]{:S(2)}) collective-permute-start(f32[128,128]{1,0:T(8,128)S(1)} %get-tuple-element.33), channel_id=1, source_target_pairs={{0,1},{1,0},{2,3},{3,2},{4,5},{5,4},{6,7},{7,6},{8,9},{9,8},{10,11... | collective-permute-start | bytes 196616 | tf_op jit(solution)/shard_map/ppermute | solution.py:529
  6.7 1.2 %copy.14 = f32[64,16,16]{2,1,0:T(8,128)S(1)} copy(f32[64,16,16]{0,2,1:T(8,128)} %param.8) | data formatting | bytes 131072 | tf_op args[2]
  7.8 0.2 copy.15
  8.1 0.2 copy.16
  8.3 0.6 collective-permute-done
  8.9 2.1 %collective-permute-start.1 = (f32[128,128]{1,0:T(8,128)S(1)}, f32[128,128]{1,0:T(8,128)S(1)}, u32[]{:S(2)}, u32[]{:S(2)}) collective-permute-start(f32[128,128]{1,0:T(8,128)S(1)} %add_select_fusion.1), channel_id=1, source_target_pairs={{0,2},{1,3},{2,0},{3,1},{4,6},{5,7},{6,4},{7,5},{8,10},{9,11},{10,... | collective-permute-start | bytes 196616 | tf_op jit(solution)/shard_map/ppermute | solution.py:529
  11.1 2.6 %collective-permute-start.2 = (f32[128,128]{1,0:T(8,128)S(1)}, f32[128,128]{1,0:T(8,128)S(1)}, u32[]{:S(2)}, u32[]{:S(2)}) collective-permute-start(f32[128,128]{1,0:T(8,128)S(1)} %add_select_fusion.1), channel_id=1, source_target_pairs={{0,4},{1,5},{2,6},{3,7},{4,0},{5,1},{6,2},{7,3},{8,12},{9,13},{10,... | collective-permute-start | bytes 196616 | tf_op jit(solution)/shard_map/ppermute | solution.py:529
  13.6 0.0 collective-permute-start.3
  13.6 0.1 pad_add_fusion.1
  13.7 3.3 %carry.4.rest_0_ = bf16[64,2,512,128]{3,2,1,0:T(8,128)(2,1)} custom-call(bf16[64,2,512,128]{3,2,1,0:T(8,128)(2,1)} %bitcast.38), custom_call_target="tpu_custom_call" | custom-call | bytes 8388608 | tf_op jit(solution)/shard_map/carry/pallas_call | solution.py:432
  17.0 0.0 collective-permute-done.1
  17.0 0.6 collective-permute-done.2
  17.6 2.1 %collective-permute-done.3 = f32[128,128]{1,0:T(8,128)S(1)} collective-permute-done((f32[128,128]{1,0:T(8,128)S(1)}, f32[128,128]{1,0:T(8,128)S(1)}, u32[]{:S(2)}, u32[]{:S(2)}) %collective-permute-start.3) | collective-permute-done | bytes 65568 | tf_op jit(solution)/shard_map/ppermute | solution.py:529
  19.8 0.0 copy-start.1
  19.8 13.0 %predict.3 = (f32[16,4096]{1,0:T(8,128)S(1)}, f32[1024,2048]{1,0:T(8,128)}, f32[1024,2048]{1,0:T(8,128)}) custom-call(s32[2]{0:T(128)S(1)} %get-tuple-element.77.sc_ref, bf16[8,32,128]{2,1,0:T(8,128)(2,1)S(1)} %pad_maximum_fusion.4.k_ref, bf16[64,2,512,128]{3,2,1,0:T(8,128)(2,1)} %bitcast.39, f32[64,2,8192]{2,1,0:T(2,128)} %energy_ref.3, ...), custom_call_target="tpu_custom_call" | custom-call | flops 838860800 | bytes 25165824 | tf_op jit(solution)/shard_map/predict/pallas_call | solution.py:279
  32.8 0.0 copy-start
  32.8 1.6 %collective-permute-start.4 = (f32[16,4096]{1,0:T(8,128)S(1)}, f32[16,4096]{1,0:T(8,128)S(1)}, u32[]{:S(2)}, u32[]{:S(2)}) collective-permute-start(f32[16,4096]{1,0:T(8,128)S(1)} %get-tuple-element.42), channel_id=1, source_target_pairs={{0,1},{1,0},{2,3},{3,2},{4,5},{5,4},{6,7},{7,6},{8,9},{9,8},{10,11... | collective-permute-start | bytes 786440 | tf_op jit(solution)/shard_map/ppermute | solution.py:529
  34.4 13.0 %predict.2 = (f32[16,4096]{1,0:T(8,128)S(1)}, f32[1024,2048]{1,0:T(8,128)}, f32[1024,2048]{1,0:T(8,128)}) custom-call(s32[2]{0:T(128)S(1)} %get-tuple-element.76.sc_ref, bf16[8,32,128]{2,1,0:T(8,128)(2,1)S(1)} %pad_maximum_fusion.4.k_ref, bf16[64,2,512,128]{3,2,1,0:T(8,128)(2,1)} %bitcast.40, f32[64,2,8192]{2,1,0:T(2,128)} %energy_ref.3, ...), custom_call_target="tpu_custom_call" | custom-call | flops 838860800 | bytes 25165824 | tf_op jit(solution)/shard_map/predict/pallas_call | solution.py:279
  47.4 0.0 collective-permute-done.4
  47.5 0.1 collective-permute-start.5
  47.6 0.0 copy-done.1
  47.6 0.2 multiply_subtract_fusion.1
  47.8 0.1 broadcast_in_dim.19
  47.9 0.2 reshape.44
  48.1 0.1 broadcast_in_dim.20
  48.2 0.2 reshape.45
  48.4 4.2 %collective-permute-done.5 = f32[8,4096]{1,0:T(8,128)S(1)} collective-permute-done((f32[8,4096]{1,0:T(8,128)S(1)}, f32[8,4096]{1,0:T(8,128)S(1)}, u32[]{:S(2)}, u32[]{:S(2)}) %collective-permute-start.5) | collective-permute-done | bytes 131104 | tf_op jit(solution)/shard_map/ppermute | solution.py:529
  52.6 1.2 %collective-permute-start.6 = (f32[8,4096]{1,0:T(8,128)S(1)}, f32[8,4096]{1,0:T(8,128)S(1)}, u32[]{:S(2)}, u32[]{:S(2)}) collective-permute-start(f32[8,4096]{1,0:T(8,128)S(1)} %select_add_fusion.1), channel_id=1, source_target_pairs={{0,6},{1,7},{2,4},{3,5},{4,2},{5,3},{6,0},{7,1},{8,14},{9,15},{10,... | collective-permute-start | bytes 393224 | tf_op jit(solution)/shard_map/ppermute | solution.py:529
  53.8 0.0 copy-done
  53.8 0.0 slice-start.2
  53.8 0.1 multiply_add_fusion
  53.9 0.0 slice-start.3
  53.9 3.6 %carry.5.rest_0_ = bf16[64,2,512,128]{3,2,1,0:T(8,128)(2,1)} custom-call(bf16[64,2,512,128]{3,2,1,0:T(8,128)(2,1)} %bitcast.41, bf16[64,2,512,128]{3,2,1,0:T(8,128)(2,1)} %carry.4.rest_0_), custom_call_target="tpu_custom_call", output_to_operand_aliasing={{}: (1, {})} | custom-call | bytes 8388608 | tf_op jit(solution)/shard_map/carry/pallas_call | solution.py:432
  57.5 0.0 slice-start
  57.5 2.2 %collective-permute-done.6 = f32[8,4096]{1,0:T(8,128)S(1)} collective-permute-done((f32[8,4096]{1,0:T(8,128)S(1)}, f32[8,4096]{1,0:T(8,128)S(1)}, u32[]{:S(2)}, u32[]{:S(2)}) %collective-permute-start.6) | collective-permute-done | bytes 131104 | tf_op jit(solution)/shard_map/ppermute | solution.py:529
  59.7 0.1 collective-permute-start.7
  59.8 4.9 %collective-permute-done.7 = f32[8,4096]{1,0:T(8,128)S(1)} collective-permute-done((f32[8,4096]{1,0:T(8,128)S(1)}, f32[8,4096]{1,0:T(8,128)S(1)}, u32[]{:S(2)}, u32[]{:S(2)}) %collective-permute-start.7) | collective-permute-done | bytes 131104 | tf_op jit(solution)/shard_map/ppermute | solution.py:529
  64.8 0.6 collective-permute-start.8
  65.4 0.0 slice-done.2
  65.4 0.0 slice-done.3
  65.4 0.0 slice-start.1
  65.4 5.8 %correct.3 = f32[16,4096]{1,0:T(8,128)S(1)} custom-call(s32[1]{0:T(128)} %bitcast.sc_ref, bf16[8,32,128]{2,1,0:T(8,128)(2,1)S(1)} %pad_maximum_fusion.4.k_ref, f32[16,8192]{1,0:T(8,128)S(1)} %pad_maximum_fusion.start_ref, f32[16,4096]{1,0:T(8,128)S(1)} %pad_maximum_fusion.1.pred_ref, f32[1024,2048]{1,0:T(8,128)S(1)} %bitcast.37, ...), custom_call_target="tpu_custom_call" | custom-call | flops 503316480 | bytes 16777216 | tf_op jit(solution)/shard_map/correct/pallas_call | solution.py:386
  71.2 1.6 %collective-permute-start.9 = (f32[16,4096]{1,0:T(8,128)S(1)}, f32[16,4096]{1,0:T(8,128)S(1)}, u32[]{:S(2)}, u32[]{:S(2)}) collective-permute-start(f32[16,4096]{1,0:T(8,128)S(1)} %correct.3), channel_id=1, source_target_pairs={{0,1},{1,0},{2,3},{3,2},{4,5},{5,4},{6,7},{7,6},{8,9},{9,8},{10,11... | collective-permute-start | bytes 786440 | tf_op jit(solution)/shard_map/ppermute | solution.py:529
  72.8 1.1 %collective-permute-done.8.pred_ref = f32[16,4096]{1,0:T(8,128)S(1)} collective-permute-done((f32[16,4096]{1,0:T(8,128)S(1)}, f32[16,4096]{1,0:T(8,128)S(1)}, u32[]{:S(2)}, u32[]{:S(2)}) %collective-permute-start.8) | collective-permute-done | bytes 262176 | tf_op jit(solution)/shard_map/ppermute | solution.py:529
  73.9 0.0 slice-done
  73.9 0.0 slice-done.1
  73.9 5.8 %correct.2 = f32[16,4096]{1,0:T(8,128)S(1)} custom-call(s32[1]{0:T(128)} %bitcast.4.sc_ref, bf16[8,32,128]{2,1,0:T(8,128)(2,1)S(1)} %pad_maximum_fusion.4.k_ref, f32[16,8192]{1,0:T(8,128)S(1)} %pad_maximum_fusion.start_ref, f32[16,4096]{1,0:T(8,128)S(1)} %collective-permute-done.8.pred_ref, f32[1024,2048]{1,0:T(8,128)S(1)} %bitcast.35, ...), custom_call_target="tpu_custom_call" | custom-call | flops 503316480 | bytes 16777216 | tf_op jit(solution)/shard_map/correct/pallas_call | solution.py:386
  79.7 0.0 collective-permute-done.9
  79.8 0.2 collective-permute-start.10
  79.9 3.3 %carry.6.rest_0_ = bf16[64,2,512,128]{3,2,1,0:T(8,128)(2,1)} custom-call(bf16[64,2,512,128]{3,2,1,0:T(8,128)(2,1)} %bitcast.42, bf16[64,2,512,128]{3,2,1,0:T(8,128)(2,1)} %carry.5.rest_0_), custom_call_target="tpu_custom_call", output_to_operand_aliasing={{}: (1, {})} | custom-call | bytes 8388608 | tf_op jit(solution)/shard_map/carry/pallas_call | solution.py:432
  83.2 2.3 %collective-permute-done.10 = f32[8,4096]{1,0:T(8,128)S(1)} collective-permute-done((f32[8,4096]{1,0:T(8,128)S(1)}, f32[8,4096]{1,0:T(8,128)S(1)}, u32[]{:S(2)}, u32[]{:S(2)}) %collective-permute-start.10) | collective-permute-done | bytes 131104 | tf_op jit(solution)/shard_map/ppermute | solution.py:529
  85.6 0.6 collective-permute-start.11
  86.3 3.3 %carry.7.old_ref = bf16[64,2,512,128]{3,2,1,0:T(8,128)(2,1)} custom-call(bf16[64,2,512,128]{3,2,1,0:T(8,128)(2,1)} %bitcast.43, bf16[64,2,512,128]{3,2,1,0:T(8,128)(2,1)} %carry.6.rest_0_), custom_call_target="tpu_custom_call", output_to_operand_aliasing={{}: (1, {})} | custom-call | bytes 8388608 | tf_op jit(solution)/shard_map/carry/pallas_call | solution.py:432
  89.6 2.9 %collective-permute-done.11 = f32[8,4096]{1,0:T(8,128)S(1)} collective-permute-done((f32[8,4096]{1,0:T(8,128)S(1)}, f32[8,4096]{1,0:T(8,128)S(1)}, u32[]{:S(2)}, u32[]{:S(2)}) %collective-permute-start.11) | collective-permute-done | bytes 131104 | tf_op jit(solution)/shard_map/ppermute | solution.py:529
  92.5 0.1 fusion.5
  92.5 0.1 collective-permute-start.14
  92.6 0.1 pad_add_fusion.sc_ref
  92.7 1.5 %collective-permute-start.12 = (f32[8,4096]{1,0:T(8,128)S(1)}, f32[8,4096]{1,0:T(8,128)S(1)}, u32[]{:S(2)}, u32[]{:S(2)}) collective-permute-start(f32[8,4096]{1,0:T(8,128)S(1)} %fusion.5), channel_id=1, source_target_pairs={{0,1},{1,0},{2,3},{3,2},{4,5},{5,4},{6,7},{7,6},{8,9},{9,8},{10,11... | collective-permute-start | bytes 393224 | tf_op jit(solution)/shard_map/ppermute | solution.py:529
  94.2 2.0 %collective-permute-start.13 = (f32[8,4096]{1,0:T(8,128)S(1)}, f32[8,4096]{1,0:T(8,128)S(1)}, u32[]{:S(2)}, u32[]{:S(2)}) collective-permute-start(f32[8,4096]{1,0:T(8,128)S(1)} %fusion.5), channel_id=1, source_target_pairs={{0,3},{1,2},{2,1},{3,0},{4,7},{5,6},{6,5},{7,4},{8,11},{9,10},{10,... | collective-permute-start | bytes 393224 | tf_op jit(solution)/shard_map/ppermute | solution.py:529
  96.2 1.4 %collective-permute-done.14 = f32[8,4096]{1,0:T(8,128)S(1)} collective-permute-done((f32[8,4096]{1,0:T(8,128)S(1)}, f32[8,4096]{1,0:T(8,128)S(1)}, u32[]{:S(2)}, u32[]{:S(2)}) %collective-permute-start.14) | collective-permute-done | bytes 131104 | tf_op jit(solution)/shard_map/ppermute | solution.py:529
  97.6 0.1 collective-permute-done.12
  97.7 2.4 %collective-permute-done.13 = f32[8,4096]{1,0:T(8,128)S(1)} collective-permute-done((f32[8,4096]{1,0:T(8,128)S(1)}, f32[8,4096]{1,0:T(8,128)S(1)}, u32[]{:S(2)}, u32[]{:S(2)}) %collective-permute-start.13) | collective-permute-done | bytes 131104 | tf_op jit(solution)/shard_map/ppermute | solution.py:529
  100.1 1.4 %finish.1 = (f32[16,8192]{1,0:T(8,128)}, bf16[64,2,512,128]{3,2,1,0:T(8,128)(2,1)}) custom-call(s32[3]{0:T(128)S(1)} %pad_add_fusion.sc_ref, bf16[64,2,512,128]{3,2,1,0:T(8,128)(2,1)} %carry.7.old_ref, f32[16,4096]{1,0:T(8,128)S(1)} %pad_maximum_fusion.2.own_ref, f32[16,4096]{1,0:T(8,128)S(1)} %pad_maximum_fusion.3.other_ref), custom_call_target="tpu_custom_call", output_to_operand_aliasing={{1}: (1, {})} | custom-call | tf_op jit(solution)/shard_map/finish/pallas_call | solution.py:480
  (23 shorter events, 0.4 us)
Async XLA Ops:
  3.6 5.3 %collective-permute-start = (f32[128,128]{1,0:T(8,128)S(1)}, f32[128,128]{1,0:T(8,128)S(1)}, u32[]{:S(2)}, u32[]{:S(2)}) collective-permute-start(f32[128,128]{1,0:T(8,128)S(1)} %get-tuple-element.33), channel_id=1, source_target_pairs={{0,1},{1,0},{2,3},{3,2},{4,5},{5,4},{6,7},{7,6},{8,9},{9,8},{10,11... | collective-permute-start | bytes 196616 | tf_op jit(solution)/shard_map/ppermute | solution.py:529
  8.9 8.1 %collective-permute-start.1 = (f32[128,128]{1,0:T(8,128)S(1)}, f32[128,128]{1,0:T(8,128)S(1)}, u32[]{:S(2)}, u32[]{:S(2)}) collective-permute-start(f32[128,128]{1,0:T(8,128)S(1)} %add_select_fusion.1), channel_id=1, source_target_pairs={{0,2},{1,3},{2,0},{3,1},{4,6},{5,7},{6,4},{7,5},{8,10},{9,11},{10,... | collective-permute-start | bytes 196616 | tf_op jit(solution)/shard_map/ppermute | solution.py:529
  11.1 6.6 %collective-permute-start.2 = (f32[128,128]{1,0:T(8,128)S(1)}, f32[128,128]{1,0:T(8,128)S(1)}, u32[]{:S(2)}, u32[]{:S(2)}) collective-permute-start(f32[128,128]{1,0:T(8,128)S(1)} %add_select_fusion.1), channel_id=1, source_target_pairs={{0,4},{1,5},{2,6},{3,7},{4,0},{5,1},{6,2},{7,3},{8,12},{9,13},{10,... | collective-permute-start | bytes 196616 | tf_op jit(solution)/shard_map/ppermute | solution.py:529
  13.6 6.1 %collective-permute-start.3 = (f32[128,128]{1,0:T(8,128)S(1)}, f32[128,128]{1,0:T(8,128)S(1)}, u32[]{:S(2)}, u32[]{:S(2)}) collective-permute-start(f32[128,128]{1,0:T(8,128)S(1)} %add_select_fusion.1), channel_id=1, source_target_pairs={{0,6},{1,7},{2,4},{3,5},{4,2},{5,3},{6,0},{7,1},{8,14},{9,15},{10,... | collective-permute-start | bytes 196616 | tf_op jit(solution)/shard_map/ppermute | solution.py:529
  19.8 27.8 %copy-start.1 = (f32[2,8192]{1,0:T(2,128)S(1)}, f32[2,8192]{1,0:T(2,128)}, u32[]{:S(2)}) copy-start(f32[2,8192]{1,0:T(2,128)} %param.11) | copy-start | bytes 196612
  32.8 21.0 %copy-start = (f32[16,8192]{1,0:T(8,128)S(1)}, f32[16,8192]{1,0:T(8,128)}, u32[]{:S(2)}) copy-start(f32[16,8192]{1,0:T(8,128)} %param.10) | copy-start | bytes 1572868
  32.8 14.6 %collective-permute-start.4 = (f32[16,4096]{1,0:T(8,128)S(1)}, f32[16,4096]{1,0:T(8,128)S(1)}, u32[]{:S(2)}, u32[]{:S(2)}) collective-permute-start(f32[16,4096]{1,0:T(8,128)S(1)} %get-tuple-element.42), channel_id=1, source_target_pairs={{0,1},{1,0},{2,3},{3,2},{4,5},{5,4},{6,7},{7,6},{8,9},{9,8},{10,11... | collective-permute-start | bytes 786440 | tf_op jit(solution)/shard_map/ppermute | solution.py:529
  47.5 5.0 %collective-permute-start.5 = (f32[8,4096]{1,0:T(8,128)S(1)}, f32[8,4096]{1,0:T(8,128)S(1)}, u32[]{:S(2)}, u32[]{:S(2)}) collective-permute-start(f32[8,4096]{1,0:T(8,128)S(1)} %slice_select_fusion.3), channel_id=1, source_target_pairs={{0,2},{1,3},{2,0},{3,1},{4,6},{5,7},{6,4},{7,5},{8,10},{9,11},{10,... | collective-permute-start | bytes 393224 | tf_op jit(solution)/shard_map/ppermute | solution.py:529
  52.6 7.1 %collective-permute-start.6 = (f32[8,4096]{1,0:T(8,128)S(1)}, f32[8,4096]{1,0:T(8,128)S(1)}, u32[]{:S(2)}, u32[]{:S(2)}) collective-permute-start(f32[8,4096]{1,0:T(8,128)S(1)} %select_add_fusion.1), channel_id=1, source_target_pairs={{0,6},{1,7},{2,4},{3,5},{4,2},{5,3},{6,0},{7,1},{8,14},{9,15},{10,... | collective-permute-start | bytes 393224 | tf_op jit(solution)/shard_map/ppermute | solution.py:529
  53.8 11.6 %slice-start.2 = ((s8[8388608]{0:T(1024)(128)(4,1)}), s8[4194304]{0:T(1024)(128)(4,1)S(1)}, s32[]{:S(2)}) async-start(s8[8388608]{0:T(1024)(128)(4,1)} %bitcast.36), calls=%async_computation.2 | async-start | bytes 8388608
  53.9 11.5 %slice-start.3 = ((s8[8388608]{0:T(1024)(128)(4,1)}), s8[4194304]{0:T(1024)(128)(4,1)S(1)}, s32[]{:S(2)}) async-start(s8[8388608]{0:T(1024)(128)(4,1)} %bitcast.36), calls=%async_computation.3 | async-start | bytes 8388608
  57.5 16.4 %slice-start = ((s8[8388608]{0:T(1024)(128)(4,1)}), s8[4194304]{0:T(1024)(128)(4,1)S(1)}, s32[]{:S(2)}) async-start(s8[8388608]{0:T(1024)(128)(4,1)} %bitcast.34), calls=%async_computation | async-start | bytes 8388608
  59.7 5.0 %collective-permute-start.7 = (f32[8,4096]{1,0:T(8,128)S(1)}, f32[8,4096]{1,0:T(8,128)S(1)}, u32[]{:S(2)}, u32[]{:S(2)}) collective-permute-start(f32[8,4096]{1,0:T(8,128)S(1)} %add.110), channel_id=1, source_target_pairs={{0,2},{1,3},{2,0},{3,1},{4,6},{5,7},{6,4},{7,5},{8,10},{9,11},{10,... | collective-permute-start | bytes 393224 | tf_op jit(solution)/shard_map/ppermute | solution.py:529
  64.8 9.1 %collective-permute-start.8 = (f32[16,4096]{1,0:T(8,128)S(1)}, f32[16,4096]{1,0:T(8,128)S(1)}, u32[]{:S(2)}, u32[]{:S(2)}) collective-permute-start(f32[16,4096]{1,0:T(8,128)S(1)} %pad_maximum_fusion.1.pred_ref), channel_id=1, source_target_pairs={{0,1},{1,0},{2,3},{3,2},{4,5},{5,4},{6,7},{7,6},{8,9},{9,8},{10,11... | collective-permute-start | bytes 786440 | tf_op jit(solution)/shard_map/ppermute | solution.py:529
  65.4 8.5 %slice-start.1 = ((s8[8388608]{0:T(1024)(128)(4,1)}), s8[4194304]{0:T(1024)(128)(4,1)S(1)}, s32[]{:S(2)}) async-start(s8[8388608]{0:T(1024)(128)(4,1)} %bitcast.34), calls=%async_computation.1 | async-start | bytes 8388608
  71.2 8.5 %collective-permute-start.9 = (f32[16,4096]{1,0:T(8,128)S(1)}, f32[16,4096]{1,0:T(8,128)S(1)}, u32[]{:S(2)}, u32[]{:S(2)}) collective-permute-start(f32[16,4096]{1,0:T(8,128)S(1)} %correct.3), channel_id=1, source_target_pairs={{0,1},{1,0},{2,3},{3,2},{4,5},{5,4},{6,7},{7,6},{8,9},{9,8},{10,11... | collective-permute-start | bytes 786440 | tf_op jit(solution)/shard_map/ppermute | solution.py:529
  79.8 5.8 %collective-permute-start.10 = (f32[8,4096]{1,0:T(8,128)S(1)}, f32[8,4096]{1,0:T(8,128)S(1)}, u32[]{:S(2)}, u32[]{:S(2)}) collective-permute-start(f32[8,4096]{1,0:T(8,128)S(1)} %slice_select_fusion.2), channel_id=1, source_target_pairs={{0,2},{1,3},{2,0},{3,1},{4,6},{5,7},{6,4},{7,5},{8,10},{9,11},{10,... | collective-permute-start | bytes 393224 | tf_op jit(solution)/shard_map/ppermute | solution.py:529
  85.6 6.9 %collective-permute-start.11 = (f32[8,4096]{1,0:T(8,128)S(1)}, f32[8,4096]{1,0:T(8,128)S(1)}, u32[]{:S(2)}, u32[]{:S(2)}) collective-permute-start(f32[8,4096]{1,0:T(8,128)S(1)} %select_add_fusion), channel_id=1, source_target_pairs={{0,6},{1,7},{2,4},{3,5},{4,2},{5,3},{6,0},{7,1},{8,14},{9,15},{10,... | collective-permute-start | bytes 393224 | tf_op jit(solution)/shard_map/ppermute | solution.py:529
  92.5 5.0 %collective-permute-start.14 = (f32[8,4096]{1,0:T(8,128)S(1)}, f32[8,4096]{1,0:T(8,128)S(1)}, u32[]{:S(2)}, u32[]{:S(2)}) collective-permute-start(f32[8,4096]{1,0:T(8,128)S(1)} %fusion.5), channel_id=1, source_target_pairs={{0,2},{1,3},{2,0},{3,1},{4,6},{5,7},{6,4},{7,5},{8,10},{9,11},{10,... | collective-permute-start | bytes 393224 | tf_op jit(solution)/shard_map/ppermute | solution.py:529
  92.7 5.0 %collective-permute-start.12 = (f32[8,4096]{1,0:T(8,128)S(1)}, f32[8,4096]{1,0:T(8,128)S(1)}, u32[]{:S(2)}, u32[]{:S(2)}) collective-permute-start(f32[8,4096]{1,0:T(8,128)S(1)} %fusion.5), channel_id=1, source_target_pairs={{0,1},{1,0},{2,3},{3,2},{4,5},{5,4},{6,7},{7,6},{8,9},{9,8},{10,11... | collective-permute-start | bytes 393224 | tf_op jit(solution)/shard_map/ppermute | solution.py:529
  94.2 5.9 %collective-permute-start.13 = (f32[8,4096]{1,0:T(8,128)S(1)}, f32[8,4096]{1,0:T(8,128)S(1)}, u32[]{:S(2)}, u32[]{:S(2)}) collective-permute-start(f32[8,4096]{1,0:T(8,128)S(1)} %fusion.5), channel_id=1, source_target_pairs={{0,3},{1,2},{2,1},{3,0},{4,7},{5,6},{6,5},{7,4},{8,11},{9,10},{10,... | collective-permute-start | bytes 393224 | tf_op jit(solution)/shard_map/ppermute | solution.py:529
